TPU v7x, 1024 devices: a whole 8x8x8 slice. The times are simulated.
1024 devices in a mesh: replica: 16 (over y_hi, z), fsdp: 32 (over x, y_lo), tensor: 2 (over core).
Axes of the slice: x: 8, y: 8 (y_hi: 2, y_lo: 4; y = y_hi * 4 + y_lo), z: 8, core: 2. Of those that a mesh axis runs over, the one named last changes fastest.
Arguments:
- pre_act: bfloat16 [4096, 24576], P('replica', ('fsdp', 'tensor')), may hold values from -6 to 6
- act_grad: bfloat16 [4096, 24576], P('replica', ('fsdp', 'tensor')), may hold values from -6 to 6
- up_weight: bfloat16 [6144, 24576], P('replica', ('fsdp', 'tensor')), may hold values from -0.0390625 to 0.0390625
- resid_grad: bfloat16 [4096, 6144], P('replica', ('fsdp', 'tensor')), may hold values from -3 to 3
- gram_parts: bfloat16 [16, 12288, 1024], P('replica', ('fsdp', 'tensor')), may hold values from -1.5 to 1.5
- stripe_order: int32 [64, 16], P(('fsdp', 'tensor')), may hold values from 0 to 15, each once within a row
- gram_prev: float32 [64, 16, 12, 1024], P(('fsdp', 'tensor'), 'replica'), may hold values from -6 to 6
Outputs:
- input_grad: bfloat16 [4096, 6144], P('replica', ('fsdp', 'tensor'))
- gram_stats: float32 [64, 16, 12, 1024], P(('fsdp', 'tensor'), 'replica')
Inputs may be any that keep to these rules, and one draw needn't show every extreme that they name: Each row of stripe_order names every stripe 0 to 15 exactly once.
All inputs are finite; a program needn't handle non-finite values.
Results may differ from a plain program's by a relative error of at most 0.015.
Values may be sent and summed in bfloat16 or wider, within the bound.
No kernel may reach another device: no remote copies, remote signals or barrier semaphores. Data moves between devices by JAX's collectives and lax.ppermute only.
A program may use at most 32 MiB of HBM per device.

v0:
```python
import jax
import jax.numpy as jnp
from jax import lax
from jax.sharding import PartitionSpec as P


def gelu_slope(values):
    normal_cdf = 0.5 * (1.0 + jax.scipy.special.erf(values * 0.7071067811865476))
    return normal_cdf + values * jnp.exp(-0.5 * values * values) * 0.3989422804014327


def on_device(pre_act, act_grad, up_weight, resid_grad, gram_parts, stripe_order, gram_prev):
    owners = lax.axis_size("replica")
    stripes = gram_parts[0].reshape(owners, -1, gram_parts.shape[2])
    ordered = stripes[stripe_order[0]]
    stripe_sum = lax.psum_scatter(
        ordered.astype(jnp.float32).astype(jnp.bfloat16), "replica", scatter_dimension=0, tiled=True
    ).astype(jnp.float32)
    gram_stats = gram_prev + stripe_sum.reshape(gram_prev.shape)
    hidden_grad = (act_grad.astype(jnp.float32) * gelu_slope(pre_act.astype(jnp.float32))).astype(
        jnp.bfloat16
    )
    contract = (((1,), (1,)), ((), ()))
    projected = lax.dot_general(
        hidden_grad,
        lax.all_gather(up_weight, "replica", axis=0, tiled=True),
        contract,
        preferred_element_type=jnp.float32,
    )
    shared = lax.psum_scatter(projected, ("fsdp", "tensor"), scatter_dimension=1, tiled=True)
    input_grad = (shared + resid_grad.astype(jnp.float32)).astype(jnp.bfloat16)
    return (input_grad, gram_stats)


def solution(mesh):
    return jax.shard_map(
        on_device,
        mesh=mesh,
        in_specs=(
            P("replica", ("fsdp", "tensor")),
            P("replica", ("fsdp", "tensor")),
            P("replica", ("fsdp", "tensor")),
            P("replica", ("fsdp", "tensor")),
            P("replica", ("fsdp", "tensor"), None),
            P(("fsdp", "tensor"), None),
            P(("fsdp", "tensor"), "replica", None, None),
        ),
        out_specs=(P("replica", ("fsdp", "tensor")), P(("fsdp", "tensor"), "replica", None, None)),
        check_vma=False,
    )
```

profile of v0, /device:TPU:1, one launch (start us, length us, event | category | flops | bytes accessed | tf_op | source)
XLA Modules:
  0.0 691.6 jit_solution(5388873892838266045)
XLA Ops:
  7.2 0.0 all-gather.2.cloned.1.call-start
  7.2 0.7 all-gather.2.cloned.1.call-update
  7.9 0.0 reduce-scatter.5.cloned.1.call-start
  7.9 1.1 reshape_squeeze.3
  9.0 0.7 fusion.15
  9.7 1.4 gather_fusion
  11.1 0.0 reduce-scatter.5.cloned.1.call-update
  11.1 0.0 reduce-scatter.3.cloned.1.call-start
  11.1 158.0 %all-gather.2.cloned.1.call-done = bf16[6144,384]{1,0:T(8,128)(2,1)} async-done(((bf16[384,384]{1,0:T(8,128)(2,1)}), bf16[6144,384]{1,0:T(8,128)(2,1)}) %all-gather.2.cloned.1.call-update) | async-done | bytes 4718608 | tf_op jit(solution)/shard_map/all_gather | solution.py:26
  169.2 7.2 %fusion.8 = f32[256,6144]{0,1:T(8,128)} fusion(bf16[6144,384]{1,0:T(8,128)(2,1)} %all-gather.2.cloned.1.call-done, bf16[256,384]{1,0:T(8,128)(2,1)} %param.7, bf16[256,384]{1,0:T(8,128)(2,1)} %param.8), kind=kOutput, calls=%fused_computation.13 | convolution fusion | flops 1209139200 | bytes 11403264 | tf_op jit(solution)/shard_map/dot_general | solution.py:24
  176.3 0.0 copy-start
  176.3 0.0 copy-start.1
  176.3 0.0 reduce-scatter.3.cloned.1.call-update
  176.4 211.9 %reduce-scatter.5.cloned.1.call-done = bf16[1,12,1024]{2,1,0:T(8,128)(2,1)} async-done(((bf16[16,12,1024]{2,1,0:T(8,128)(2,1)}), bf16[1,12,1024]{2,1,0:T(8,128)(2,1)}) %reduce-scatter.5.cloned.1.call-update) | async-done | bytes 24592 | tf_op jit(solution)/shard_map/reduce_scatter | solution.py:16
  388.2 0.0 copy-done
  388.2 0.8 convert_add_fusion
  389.0 0.7 copy.10
  389.7 293.8 %reduce-scatter.3.cloned.1.call-done = f32[256,96]{0,1:T(8,128)} async-done(((f32[256,6144]{0,1:T(8,128)}), f32[256,96]{0,1:T(8,128)}) %reduce-scatter.3.cloned.1.call-update) | async-done | bytes 98320 | tf_op jit(solution)/shard_map/reduce_scatter | solution.py:30
  683.5 0.0 copy-done.1
  683.5 1.5 add_convert_fusion
  (1 shorter events, 0.0 us)
Async XLA Ops:
  7.2 162.0 %all-gather.2.cloned.1.call-start = ((), (), s32[]{:S(2)}) async-start(), calls=%async_computation.2 | async-start | bytes 5013504 | tf_op jit(solution)/shard_map/all_gather | solution.py:26
  7.9 380.3 %reduce-scatter.5.cloned.1.call-start = ((), (), s32[]{:S(2)}) async-start(), calls=%async_computation.4 | async-start | bytes 557056 | tf_op jit(solution)/shard_map/reduce_scatter | solution.py:16
  11.1 672.4 %reduce-scatter.3.cloned.1.call-start = ((), (), s32[]{:S(2)}) async-start(), calls=%async_computation.3 | async-start | bytes 6389760 | tf_op jit(solution)/shard_map/reduce_scatter | solution.py:30
  176.3 211.9 %copy-start = (f32[1,1,12,1024]{3,1,2,0:T(1,128)S(1)}, f32[1,1,12,1024]{3,1,2,0:T(1,128)}, u32[]{:S(2)}) copy-start(f32[1,1,12,1024]{3,1,2,0:T(1,128)} %param.13) | copy-start | bytes 147460
  176.3 507.2 %copy-start.1 = (bf16[256,96]{0,1:T(8,128)(2,1)S(1)}, bf16[256,96]{0,1:T(8,128)(2,1)}, u32[]{:S(2)}) copy-start(bf16[256,96]{0,1:T(8,128)(2,1)} %param.10) | copy-start | bytes 147460
Sparse Core Ops, SparseCore 0:
  12.3 156.8 all-gather.1
  174.7 213.4 reduce-scatter.4
  392.0 291.4 reduce-scatter.2
where the time goes:
time: 692 us
  waiting for transfers between devices  664 us (96%)
  between operations  13.8 us (2%)
  matrix products  7.16 us (1%)
    reduce_scatter x1, waiting for transfers between devices, on_device(): lax.psum_scatter(projected, ('fsdp', 'tensor'), scatter_dimension=1, tile...  294 us
    reduce_scatter x1, waiting for transfers between devices, on_device(): lax.psum_scatter(ordered.astype(jnp.float32).astype(jnp.bfloat16), 'repli...  212 us
    all_gather x1, waiting for transfers between devices, on_device(): lax.all_gather(up_weight, 'replica', axis=0, tiled=True)  158 us
  transfers between devices with their start and end apart: 3, of which 3 were waited for; matrix products, arithmetic and copies ran while one was open for 2% of the time, Pallas kernels for 0%

commit v1 on v0

v1 whole, which is shorter than its diff:
```python
import jax
import jax.numpy as jnp
from jax import lax
from jax.sharding import Mesh, PartitionSpec as P


def gelu_slope(values):
    normal_cdf = 0.5 * (1.0 + jax.scipy.special.erf(values * 0.7071067811865476))
    return normal_cdf + values * jnp.exp(-0.5 * values * values) * 0.3989422804014327


SWAP = [(0, 1), (1, 0)]


def on_device(pre_act, act_grad, up_weight, resid_grad, gram_parts, stripe_order, gram_prev):
    core = lax.axis_index("core")
    y_hi = lax.axis_index("y_hi")
    tokens, hidden = pre_act.shape
    feats = resid_grad.shape[1]

    rows = up_weight.reshape(2, 2, feats, hidden)
    own = lax.dynamic_index_in_dim(rows, core, 1, keepdims=False)
    away = lax.dynamic_index_in_dim(rows, 1 - core, 1, keepdims=False)
    other = lax.ppermute(away, "core", SWAP)
    pair = jnp.concatenate([own, other], axis=-1).reshape(2 * feats, 2 * hidden)
    weight = lax.all_gather(pair, "z", axis=0, tiled=True)

    hidden_grad = (act_grad.astype(jnp.float32) * gelu_slope(pre_act.astype(jnp.float32))).astype(jnp.bfloat16)
    far = lax.ppermute(hidden_grad, "y_hi", SWAP)
    both = jnp.stack([jnp.where(y_hi == 0, hidden_grad, far), jnp.where(y_hi == 0, far, hidden_grad)])
    both = jnp.concatenate([both, lax.ppermute(both, "core", SWAP)], axis=-1)

    owners = lax.axis_size(("y_hi", "z"))
    stripes = gram_parts[0].reshape(owners, -1, gram_parts.shape[2])
    ordered = stripes[stripe_order[0]]
    kept = lax.all_to_all(ordered, ("y_hi", "z"), 0, 0, tiled=True)
    gram_stats = gram_prev + jnp.sum(kept.astype(jnp.float32), axis=0).reshape(gram_prev.shape)

    contract = (((1,), (1,)), ((), ()))
    partial = jnp.stack(
        [
            lax.dot_general(weight, both[i], contract, preferred_element_type=jnp.float32).astype(jnp.bfloat16)
            for i in range(2)
        ]
    )
    blocks = partial.reshape(-1, feats, tokens)
    arrived = lax.all_to_all(blocks, ("x_hi", "x_lo", "y_lo"), 0, 0, tiled=True)
    shared = jnp.sum(arrived.astype(jnp.float32), axis=0).astype(jnp.bfloat16)
    home = lax.ppermute(shared, ("y_hi", "x_hi"), [(0, 0), (1, 2), (2, 1), (3, 3)])
    input_grad = (home.astype(jnp.float32) + resid_grad.T.astype(jnp.float32)).astype(jnp.bfloat16).T
    return (input_grad, gram_stats)


def solution(mesh):
    fine = Mesh(mesh.devices.reshape(2, 8, 2, 4, 4, 2), ("y_hi", "z", "x_hi", "x_lo", "y_lo", "core"))
    replica = ("y_hi", "z")
    spread = ("x_hi", "x_lo", "y_lo", "core")
    return jax.shard_map(
        on_device,
        mesh=fine,
        in_specs=(
            P(replica, spread),
            P(replica, spread),
            P(replica, spread),
            P(replica, spread),
            P(replica, spread, None),
            P(spread, None),
            P(spread, replica, None, None),
        ),
        out_specs=(P(replica, spread), P(spread, replica, None, None)),
        check_vma=False,
    )
```

time: 692 us -> 156 us (0.23)
  the two profiles are of different devices: /device:TPU:1 before, /device:TPU:112 now
where the time goes in v1:
time: 156 us
  waiting for transfers between devices  85.1 us (55%)
  starting transfers between devices  46 us (29%)
  between operations  14.2 us (9%)
  other arithmetic  4.05 us (3%)
  matrix products  3.45 us (2%)
  local copies, waits for them, and re-layouts  2.65 us (2%)
    all_to_all x1, waiting for transfers between devices, on_device(): arrived = lax.all_to_all(blocks, ('x_hi', 'x_lo', 'y_lo'), 0, 0, tiled=True)  36.2 us
    all_gather x1, waiting for transfers between devices, on_device(): weight = lax.all_gather(pair, 'z', axis=0, tiled=True)  26.8 us
    all_to_all x1, starting transfers between devices, on_device(): kept = lax.all_to_all(ordered, ('y_hi', 'z'), 0, 0, tiled=True)  22.1 us
    ppermute x1, waiting for transfers between devices, on_device(): far = lax.ppermute(hidden_grad, 'y_hi', SWAP)  12.3 us
    all_to_all x1, starting transfers between devices, on_device(): arrived = lax.all_to_all(blocks, ('x_hi', 'x_lo', 'y_lo'), 0, 0, tiled=True)  10.2 us
    ppermute x1, waiting for transfers between devices, on_device(): lax.ppermute(shared, ('y_hi', 'x_hi'), [(0, 0), (1, 2), (2, 1), (3, 3)])  8.5 us
    ppermute x1, starting transfers between devices, on_device(): lax.ppermute(shared, ('y_hi', 'x_hi'), [(0, 0), (1, 2), (2, 1), (3, 3)])  5.5 us
    ppermute x1, starting transfers between devices, on_device(): far = lax.ppermute(hidden_grad, 'y_hi', SWAP)  4.26 us
  transfers between devices with their start and end apart: 7, of which 5 were waited for; matrix products, arithmetic and copies ran while one was open for 5% of the time, Pallas kernels for 0%

profile of v1, /device:TPU:112, one launch (start us, length us, event | category | flops | bytes accessed | tf_op | source)
XLA Modules:
  0.0 155.5 jit_solution(8575918132071488873)
XLA Ops:
  7.2 0.0 all-gather.2.cloned.1.call-start
  7.2 1.1 constant_dynamic-slice_fusion
  8.4 0.0 copy-start
  8.4 2.1 %collective-permute-start = (bf16[2,96,384]{2,1,0:T(8,128)(2,1)S(1)}, bf16[2,96,384]{2,1,0:T(8,128)(2,1)S(1)}, u32[]{:S(2)}, u32[]{:S(2)}) collective-permute-start(bf16[2,96,384]{2,1,0:T(8,128)(2,1)S(1)} %get-tuple-element.5), channel_id=1, source_target_pairs={{0,1},{1,0},{2,3},{3,2},{4,5},{5,4},{6,7},{7,6},{8,9},{9,8},{10,11... | collective-permute-start | bytes 442376 | tf_op jit(solution)/shard_map/ppermute | solution.py:24
  10.4 1.3 collective-permute-done
  11.8 0.8 pad_maximum_fusion.3
  12.5 0.0 all-gather.2.cloned.1.call-update
  12.6 0.0 copy-start.6
  12.6 0.2 fusion.9
  12.8 4.3 %collective-permute-start.1 = (bf16[256,384]{1,0:T(8,128)(2,1)S(1)}, bf16[256,384]{1,0:T(8,128)(2,1)S(1)}, u32[]{:S(2)}, u32[]{:S(2)}) collective-permute-start(bf16[256,384]{1,0:T(8,128)(2,1)S(1)} %fusion.9), channel_id=1, source_target_pairs={{0,512},{512,0},{1,513},{513,1},{2,514},{514,2},{3,515},{515,3},{4... | collective-permute-start | bytes 589832 | tf_op jit(solution)/shard_map/ppermute | solution.py:29
  17.1 12.3 %collective-permute-done.1 = bf16[256,384]{1,0:T(8,128)(2,1)S(1)} collective-permute-done((bf16[256,384]{1,0:T(8,128)(2,1)S(1)}, bf16[256,384]{1,0:T(8,128)(2,1)S(1)}, u32[]{:S(2)}, u32[]{:S(2)}) %collective-permute-start.1) | collective-permute-done | bytes 196640 | tf_op jit(solution)/shard_map/ppermute | solution.py:29
  29.4 1.9 %collective-permute-start.2 = (bf16[2,256,384]{2,1,0:T(8,128)(2,1)S(1)}, bf16[2,256,384]{2,1,0:T(8,128)(2,1)S(1)}, u32[]{:S(2)}, u32[]{:S(2)}) collective-permute-start(bf16[2,256,384]{2,1,0:T(8,128)(2,1)S(1)} %pad_maximum_fusion.2), channel_id=1, source_target_pairs={{0,1},{1,0},{2,3},{3,2},{4,5},{5,4},{6,7},{7,6},{8,9},{9,8},{10,11... | collective-permute-start | bytes 1179656 | tf_op jit(solution)/shard_map/ppermute | solution.py:31
  31.4 0.1 reshape_squeeze.3
  31.5 1.4 gather_fusion
  32.9 22.1 %all-to-all-start.1 = ((bf16[16,12,1024]{2,1,0:T(8,128)(2,1)}), bf16[16,12,1024]{2,1,0:T(8,128)(2,1)S(1)}, u32[]{:S(2)}, u32[]{:S(2)}) async-start(bf16[16,12,1024]{2,1,0:T(8,128)(2,1)} %gather_fusion), calls=%async_computation.1 | async-start | bytes 1048576 | tf_op jit(solution)/shard_map/all_to_all | solution.py:36
  55.0 0.0 collective-permute-done.2
  55.0 0.1 pad_maximum_fusion.1
  55.1 26.8 %all-gather.2.cloned.1.call-done = bf16[1536,768]{1,0:T(8,128)(2,1)} async-done(((bf16[192,768]{1,0:T(8,128)(2,1)}), bf16[1536,768]{1,0:T(8,128)(2,1)}) %all-gather.2.cloned.1.call-update) | async-done | bytes 2359312 | tf_op jit(solution)/shard_map/all_gather | solution.py:26
  81.8 2.6 %fusion = bf16[1,1536,256]{2,1,0:T(8,128)(2,1)S(1)} fusion(bf16[1536,768]{1,0:T(8,128)(2,1)} %all-gather.2.cloned.1.call-done, bf16[2,256,768]{2,1,0:T(8,128)(2,1)S(1)} %pad_maximum_fusion.1), kind=kOutput, calls=%fused_computation.3 | convolution fusion | flops 604372992 | bytes 3538944 | tf_op jit(solution)/shard_map/dot_general | solution.py:42
  84.5 0.8 fusion.1
  85.3 1.3 pad_maximum_fusion
  86.6 0.0 all-to-all-done.1
  86.6 10.2 %all-to-all-start = ((bf16[32,96,256]{2,1,0:T(8,128)(2,1)}), bf16[32,96,256]{2,1,0:T(8,128)(2,1)S(1)}, u32[]{:S(2)}, u32[]{:S(2)}) async-start(bf16[32,96,256]{2,1,0:T(8,128)(2,1)} %bitcast.10), calls=%async_computation | async-start | bytes 3145728 | tf_op jit(solution)/shard_map/all_to_all | solution.py:47
  96.8 0.0 copy-start.3
  96.8 0.0 copy-start.4
  96.8 0.1 convert_reduce_fusion
  96.9 36.2 %all-to-all-done = bf16[32,96,256]{2,1,0:T(8,128)(2,1)S(1)} async-done(((bf16[32,96,256]{2,1,0:T(8,128)(2,1)}), bf16[32,96,256]{2,1,0:T(8,128)(2,1)S(1)}, u32[]{:S(2)}, u32[]{:S(2)}) %all-to-all-start) | async-done | bytes 1572896 | tf_op jit(solution)/shard_map/all_to_all | solution.py:47
  133.1 0.2 reduce_sum.21
  133.4 5.5 %collective-permute-start.3 = (bf16[96,256]{1,0:T(8,128)(2,1)S(1)}, bf16[96,256]{1,0:T(8,128)(2,1)S(1)}, u32[]{:S(2)}, u32[]{:S(2)}) collective-permute-start(bf16[96,256]{1,0:T(8,128)(2,1)S(1)} %reduce_sum.21), channel_id=1, source_target_pairs={{0,0},{32,512},{512,32},{544,544},{1,1},{33,513},{513,33},{545,545... | collective-permute-start | bytes 147464 | tf_op jit(solution)/shard_map/ppermute | solution.py:49
  138.9 0.7 reshape_add_fusion
  139.5 8.5 %collective-permute-done.3 = bf16[96,256]{1,0:T(8,128)(2,1)S(1)} collective-permute-done((bf16[96,256]{1,0:T(8,128)(2,1)S(1)}, bf16[96,256]{1,0:T(8,128)(2,1)S(1)}, u32[]{:S(2)}, u32[]{:S(2)}) %collective-permute-start.3) | collective-permute-done | bytes 49184 | tf_op jit(solution)/shard_map/ppermute | solution.py:49
  148.1 0.6 fusion.11
  (14 shorter events, 0.1 us)
Async XLA Ops:
  7.2 5.4 %copy-start.1 = (bf16[256,384]{1,0:T(8,128)(2,1)S(1)}, bf16[256,384]{1,0:T(8,128)(2,1)}, u32[]{:S(2)}) copy-start(bf16[256,384]{1,0:T(8,128)(2,1)} %param.7) | copy-start | bytes 589828
  7.2 5.4 %copy-start.2 = (bf16[256,384]{1,0:T(8,128)(2,1)S(1)}, bf16[256,384]{1,0:T(8,128)(2,1)}, u32[]{:S(2)}) copy-start(bf16[256,384]{1,0:T(8,128)(2,1)} %param.8) | copy-start | bytes 589828
  7.2 74.6 %all-gather.2.cloned.1.call-start = ((), (), s32[]{:S(2)}) async-start(), calls=%async_computation.2 | async-start | bytes 2654208 | tf_op jit(solution)/shard_map/all_gather | solution.py:26
  8.4 23.0 %copy-start = (bf16[1,192,1024]{2,1,0:T(8,128)(2,1)S(1)}, bf16[1,192,1024]{2,1,0:T(8,128)(2,1)}, u32[]{:S(2)}) copy-start(bf16[1,192,1024]{2,1,0:T(8,128)(2,1)} %param.11) | copy-start | bytes 1179652
  8.4 3.4 %collective-permute-start = (bf16[2,96,384]{2,1,0:T(8,128)(2,1)S(1)}, bf16[2,96,384]{2,1,0:T(8,128)(2,1)S(1)}, u32[]{:S(2)}, u32[]{:S(2)}) collective-permute-start(bf16[2,96,384]{2,1,0:T(8,128)(2,1)S(1)} %get-tuple-element.5), channel_id=1, source_target_pairs={{0,1},{1,0},{2,3},{3,2},{4,5},{5,4},{6,7},{7,6},{8,9},{9,8},{10,11... | collective-permute-start | bytes 442376 | tf_op jit(solution)/shard_map/ppermute | solution.py:24
  12.6 18.9 %copy-start.6 = (s32[1,16]{1,0:T(1,128)S(1)}, s32[1,16]{1,0:T(1,128)}, u32[]{:S(2)}) copy-start(s32[1,16]{1,0:T(1,128)} %param.12) | copy-start | bytes 196
  12.8 16.5 %collective-permute-start.1 = (bf16[256,384]{1,0:T(8,128)(2,1)S(1)}, bf16[256,384]{1,0:T(8,128)(2,1)S(1)}, u32[]{:S(2)}, u32[]{:S(2)}) collective-permute-start(bf16[256,384]{1,0:T(8,128)(2,1)S(1)} %fusion.9), channel_id=1, source_target_pairs={{0,512},{512,0},{1,513},{513,1},{2,514},{514,2},{3,515},{515,3},{4... | collective-permute-start | bytes 589832 | tf_op jit(solution)/shard_map/ppermute | solution.py:29
  29.4 25.5 %collective-permute-start.2 = (bf16[2,256,384]{2,1,0:T(8,128)(2,1)S(1)}, bf16[2,256,384]{2,1,0:T(8,128)(2,1)S(1)}, u32[]{:S(2)}, u32[]{:S(2)}) collective-permute-start(bf16[2,256,384]{2,1,0:T(8,128)(2,1)S(1)} %pad_maximum_fusion.2), channel_id=1, source_target_pairs={{0,1},{1,0},{2,3},{3,2},{4,5},{5,4},{6,7},{7,6},{8,9},{9,8},{10,11... | collective-permute-start | bytes 1179656 | tf_op jit(solution)/shard_map/ppermute | solution.py:31
  32.9 53.7 %all-to-all-start.1 = ((bf16[16,12,1024]{2,1,0:T(8,128)(2,1)}), bf16[16,12,1024]{2,1,0:T(8,128)(2,1)S(1)}, u32[]{:S(2)}, u32[]{:S(2)}) async-start(bf16[16,12,1024]{2,1,0:T(8,128)(2,1)} %gather_fusion), calls=%async_computation.1 | async-start | bytes 1048576 | tf_op jit(solution)/shard_map/all_to_all | solution.py:36
  81.8 2.6 %copy-start.5 = (bf16[1536,768]{1,0:T(8,128)(2,1)S(1)}, bf16[1536,768]{1,0:T(8,128)(2,1)}, u32[]{:S(2)}) copy-start(bf16[1536,768]{1,0:T(8,128)(2,1)} %all-gather.2.cloned.1.call-done) | copy-start | bytes 7077892
  86.6 46.5 %all-to-all-start = ((bf16[32,96,256]{2,1,0:T(8,128)(2,1)}), bf16[32,96,256]{2,1,0:T(8,128)(2,1)S(1)}, u32[]{:S(2)}, u32[]{:S(2)}) async-start(bf16[32,96,256]{2,1,0:T(8,128)(2,1)} %bitcast.10), calls=%async_computation | async-start | bytes 3145728 | tf_op jit(solution)/shard_map/all_to_all | solution.py:47
  96.8 42.1 %copy-start.3 = (f32[1,1,12,1024]{3,1,2,0:T(1,128)S(1)}, f32[1,1,12,1024]{3,1,2,0:T(1,128)}, u32[]{:S(2)}) copy-start(f32[1,1,12,1024]{3,1,2,0:T(1,128)} %param.13) | copy-start | bytes 147460
  96.8 51.2 %copy-start.4 = (bf16[256,96]{0,1:T(8,128)(2,1)S(1)}, bf16[256,96]{0,1:T(8,128)(2,1)}, u32[]{:S(2)}) copy-start(bf16[256,96]{0,1:T(8,128)(2,1)} %param.10) | copy-start | bytes 147460
  133.4 14.7 %collective-permute-start.3 = (bf16[96,256]{1,0:T(8,128)(2,1)S(1)}, bf16[96,256]{1,0:T(8,128)(2,1)S(1)}, u32[]{:S(2)}, u32[]{:S(2)}) collective-permute-start(bf16[96,256]{1,0:T(8,128)(2,1)S(1)} %reduce_sum.21), channel_id=1, source_target_pairs={{0,0},{32,512},{512,32},{544,544},{1,1},{33,513},{513,33},{545,545... | collective-permute-start | bytes 147464 | tf_op jit(solution)/shard_map/ppermute | solution.py:49
Sparse Core Ops, SparseCore 0:
  12.7 69.0 all-gather.1

commit v2 on v1

--- a/solution.py
+++ b/solution.py
@@ -10,6 +10,7 @@
 
 
 SWAP = [(0, 1), (1, 0)]
+CHUNKS = ((0, 40), (40, 96))
 
 
 def on_device(pre_act, act_grad, up_weight, resid_grad, gram_parts, stripe_order, gram_prev):
@@ -22,8 +23,10 @@
     own = lax.dynamic_index_in_dim(rows, core, 1, keepdims=False)
     away = lax.dynamic_index_in_dim(rows, 1 - core, 1, keepdims=False)
     other = lax.ppermute(away, "core", SWAP)
-    pair = jnp.concatenate([own, other], axis=-1).reshape(2 * feats, 2 * hidden)
-    weight = lax.all_gather(pair, "z", axis=0, tiled=True)
+    pair = jnp.concatenate([own, other], axis=-1)
+    weights = [
+        lax.all_gather(pair[:, lo:hi].reshape(-1, 2 * hidden), "z", axis=0, tiled=True) for lo, hi in CHUNKS
+    ]
 
     hidden_grad = (act_grad.astype(jnp.float32) * gelu_slope(pre_act.astype(jnp.float32))).astype(jnp.bfloat16)
     far = lax.ppermute(hidden_grad, "y_hi", SWAP)
@@ -37,16 +40,19 @@
     gram_stats = gram_prev + jnp.sum(kept.astype(jnp.float32), axis=0).reshape(gram_prev.shape)
 
     contract = (((1,), (1,)), ((), ()))
-    partial = jnp.stack(
-        [
-            lax.dot_general(weight, both[i], contract, preferred_element_type=jnp.float32).astype(jnp.bfloat16)
-            for i in range(2)
-        ]
-    )
-    blocks = partial.reshape(-1, feats, tokens)
-    arrived = lax.all_to_all(blocks, ("x_hi", "x_lo", "y_lo"), 0, 0, tiled=True)
-    shared = jnp.sum(arrived.astype(jnp.float32), axis=0).astype(jnp.bfloat16)
-    home = lax.ppermute(shared, ("y_hi", "x_hi"), [(0, 0), (1, 2), (2, 1), (3, 3)])
+    homes = []
+    for (lo, hi), weight in zip(CHUNKS, weights):
+        partial = jnp.stack(
+            [
+                lax.dot_general(weight, both[i], contract, preferred_element_type=jnp.float32).astype(jnp.bfloat16)
+                for i in range(2)
+            ]
+        )
+        blocks = partial.reshape(-1, hi - lo, tokens)
+        arrived = lax.all_to_all(blocks, ("x_hi", "x_lo", "y_lo"), 0, 0, tiled=True)
+        shared = jnp.sum(arrived.astype(jnp.float32), axis=0).astype(jnp.bfloat16)
+        homes.append(lax.ppermute(shared, ("y_hi", "x_hi"), [(0, 0), (1, 2), (2, 1), (3, 3)]))
+    home = jnp.concatenate(homes, axis=0)
     input_grad = (home.astype(jnp.float32) + resid_grad.T.astype(jnp.float32)).astype(jnp.bfloat16).T
     return (input_grad, gram_stats)
 

time: 156 us -> 162 us (1.038)
  waiting for transfers between devices: 85.1 us -> 43.7 us
  blocking collectives: 0 us -> 38.8 us
  starting transfers between devices: 46 us -> 53 us
    all_gather x0 -> x1, blocking collectives: none -> 38.8 us  [on_device(): lax.all_gather(pair[:, lo:hi].reshape(-1, 2 * hidden), 'z', axis=0, tiled...]
    all_gather x1, waiting for transfers between devices: 26.8 us -> 0.02 us  [on_device(): lax.all_gather(pair[:, lo:hi].reshape(-1, 2 * hidden), 'z', axis=0, tiled...]
    ppermute x1, waiting for transfers between devices: 12.3 us -> 0.01 us  [on_device(): far = lax.ppermute(hidden_grad, 'y_hi', SWAP)]
    all_to_all x1 -> x2, starting transfers between devices: 10.2 us -> 15.6 us  [on_device(): arrived = lax.all_to_all(blocks, ('x_hi', 'x_lo', 'y_lo'), 0, 0, tiled=True)]
    all_to_all x1 -> x2, waiting for transfers between devices: 36.2 us -> 31.8 us  [on_device(): arrived = lax.all_to_all(blocks, ('x_hi', 'x_lo', 'y_lo'), 0, 0, tiled=True)]
    ppermute x1 -> x2, waiting for transfers between devices: 8.5 us -> 11.9 us  [on_device(): lax.ppermute(shared, ('y_hi', 'x_hi'), [(0, 0), (1, 2), (2, 1), (3, 3)])]
    ppermute x1 -> x2, starting transfers between devices: 5.5 us -> 7.2 us  [on_device(): lax.ppermute(shared, ('y_hi', 'x_hi'), [(0, 0), (1, 2), (2, 1), (3, 3)])]
    dot_general x2 -> x4, matrix products: 3.45 us -> 3.46 us  [on_device(): lax.dot_general(weight, both[i], contract, preferred_element_type=jnp.flo...]
  transfers between devices with their start and end apart: 7 -> 9, of which waited for: 5 -> 3; matrix products, arithmetic and copies ran while one was open for 5% -> 6% of each run, Pallas kernels for 0% -> 0%
where the time goes in v2:
time: 162 us; the launch traced here: 161 us
  starting transfers between devices  53 us (33%)
  waiting for transfers between devices  43.7 us (27%)
  blocking collectives  38.8 us (24%)
  between operations  14.3 us (9%)
  other arithmetic  5.63 us (3%)
  matrix products  3.46 us (2%)
  local copies, waits for them, and re-layouts  2.57 us (2%)
    all_gather x1, blocking collectives, on_device(): lax.all_gather(pair[:, lo:hi].reshape(-1, 2 * hidden), 'z', axis=0, tiled...  38.8 us
    all_to_all x2, waiting for transfers between devices, on_device(): arrived = lax.all_to_all(blocks, ('x_hi', 'x_lo', 'y_lo'), 0, 0, tiled=True)  31.8 us
    all_to_all x1, starting transfers between devices, on_device(): kept = lax.all_to_all(ordered, ('y_hi', 'z'), 0, 0, tiled=True)  22.1 us
    all_to_all x2, starting transfers between devices, on_device(): arrived = lax.all_to_all(blocks, ('x_hi', 'x_lo', 'y_lo'), 0, 0, tiled=True)  15.6 us
    ppermute x2, waiting for transfers between devices, on_device(): lax.ppermute(shared, ('y_hi', 'x_hi'), [(0, 0), (1, 2), (2, 1), (3, 3)])  11.9 us
    ppermute x2, starting transfers between devices, on_device(): lax.ppermute(shared, ('y_hi', 'x_hi'), [(0, 0), (1, 2), (2, 1), (3, 3)])  7.2 us
    ppermute x1, starting transfers between devices, on_device(): far = lax.ppermute(hidden_grad, 'y_hi', SWAP)  4.26 us
    dot_general x4, matrix products, on_device(): lax.dot_general(weight, both[i], contract, preferred_element_type=jnp.flo...  3.46 us
  transfers between devices with their start and end apart: 9, of which 3 were waited for; matrix products, arithmetic and copies ran while one was open for 6% of the time, Pallas kernels for 0%

profile of v2, /device:TPU:112, one launch (start us, length us, event | category | flops | bytes accessed | tf_op | source)
XLA Modules:
  0.0 161.4 jit_solution(6722610848340298815)
XLA Ops:
  7.2 0.0 all-gather.2.cloned.1.call-start
  7.2 1.1 dynamic-slice_bitcast_fusion.1
  8.3 1.9 %collective-permute-start = (bf16[2,96,384]{2,1,0:T(8,128)(2,1)S(1)}, bf16[2,96,384]{2,1,0:T(8,128)(2,1)S(1)}, u32[]{:S(2)}, u32[]{:S(2)}) collective-permute-start(bf16[2,96,384]{2,1,0:T(8,128)(2,1)S(1)} %get-tuple-element.5), channel_id=1, source_target_pairs={{0,1},{1,0},{2,3},{3,2},{4,5},{5,4},{6,7},{7,6},{8,9},{9,8},{10,11... | collective-permute-start | bytes 442376 | tf_op jit(solution)/shard_map/ppermute | solution.py:25
  10.2 1.2 fusion.11
  11.4 4.3 %collective-permute-start.1 = (bf16[256,384]{1,0:T(8,128)(2,1)S(1)}, bf16[256,384]{1,0:T(8,128)(2,1)S(1)}, u32[]{:S(2)}, u32[]{:S(2)}) collective-permute-start(bf16[256,384]{1,0:T(8,128)(2,1)S(1)} %fusion.11), channel_id=1, source_target_pairs={{0,512},{512,0},{1,513},{513,1},{2,514},{514,2},{3,515},{515,3},{4... | collective-permute-start | bytes 589832 | tf_op jit(solution)/shard_map/ppermute | solution.py:32
  15.7 0.7 pad_maximum_fusion.4
  16.4 0.0 all-gather.2.cloned.1.call-update
  16.5 0.1 reshape_squeeze.3
  16.6 1.4 gather_fusion
  18.0 22.1 %all-to-all-start.2 = ((bf16[16,12,1024]{2,1,0:T(8,128)(2,1)}), bf16[16,12,1024]{2,1,0:T(8,128)(2,1)S(1)}, u32[]{:S(2)}, u32[]{:S(2)}) async-start(bf16[16,12,1024]{2,1,0:T(8,128)(2,1)} %gather_fusion), calls=%async_computation.2 | async-start | bytes 1048576 | tf_op jit(solution)/shard_map/all_to_all | solution.py:39
  40.2 1.9 %collective-permute-start.2 = (bf16[2,256,384]{2,1,0:T(8,128)(2,1)S(1)}, bf16[2,256,384]{2,1,0:T(8,128)(2,1)S(1)}, u32[]{:S(2)}, u32[]{:S(2)}) collective-permute-start(bf16[2,256,384]{2,1,0:T(8,128)(2,1)S(1)} %pad_maximum_fusion.3), channel_id=1, source_target_pairs={{0,1},{1,0},{2,3},{3,2},{4,5},{5,4},{6,7},{7,6},{8,9},{9,8},{10,11... | collective-permute-start | bytes 1179656 | tf_op jit(solution)/shard_map/ppermute | solution.py:34
  42.1 38.8 %all_gather.6 = bf16[640,768]{1,0:T(8,128)(2,1)S(1)} all-gather(bf16[80,768]{1,0:T(8,128)(2,1)S(1)} %bitcast.46), channel_id=1, replica_groups=mesh['y_hi'=2,'z'=8,'x_hi'=2,'x_lo'=4,'y_lo'=4,'core'=2] {'z'}, dimensions={0}, use_global_device_ids=true | all-gather | bytes 1105920 | tf_op jit(solution)/shard_map/all_gather | solution.py:28
  80.9 0.1 pad_maximum_fusion.1
  80.9 0.5 fusion.2
  81.4 0.5 fusion.3
  81.9 0.9 pad_maximum_fusion.2
  82.8 10.3 %all-to-all-start = ((bf16[32,40,256]{2,1,0:T(8,128)(2,1)}), bf16[32,40,256]{2,1,0:T(8,128)(2,1)S(1)}, u32[]{:S(2)}, u32[]{:S(2)}) async-start(bf16[32,40,256]{2,1,0:T(8,128)(2,1)} %bitcast.10), calls=%async_computation | async-start | bytes 1310720 | tf_op jit(solution)/shard_map/all_to_all | solution.py:52
  93.1 0.0 all-gather.2.cloned.1.call-done
  93.2 2.0 %fusion = bf16[1,896,256]{2,1,0:T(8,128)(2,1)S(1)} fusion(bf16[896,768]{1,0:T(8,128)(2,1)} %all-gather.2.cloned.1.call-done, bf16[2,256,768]{2,1,0:T(8,128)(2,1)S(1)} %pad_maximum_fusion.1), kind=kOutput, calls=%fused_computation.5 | convolution fusion | flops 352550912 | bytes 2228224 | tf_op jit(solution)/shard_map/dot_general | solution.py:47
  95.2 0.6 fusion.1
  95.7 1.0 pad_maximum_fusion
  96.7 12.7 %all-to-all-done = bf16[32,40,256]{2,1,0:T(8,128)(2,1)S(1)} async-done(((bf16[32,40,256]{2,1,0:T(8,128)(2,1)}), bf16[32,40,256]{2,1,0:T(8,128)(2,1)S(1)}, u32[]{:S(2)}, u32[]{:S(2)}) %all-to-all-start) | async-done | bytes 655392 | tf_op jit(solution)/shard_map/all_to_all | solution.py:52
  109.4 5.3 %all-to-all-start.1 = ((bf16[32,56,256]{2,1,0:T(8,128)(2,1)}), bf16[32,56,256]{2,1,0:T(8,128)(2,1)S(1)}, u32[]{:S(2)}, u32[]{:S(2)}) async-start(bf16[32,56,256]{2,1,0:T(8,128)(2,1)} %bitcast.14), calls=%async_computation.1 | async-start | bytes 1835008 | tf_op jit(solution)/shard_map/all_to_all | solution.py:52
  114.7 0.1 convert_reduce_fusion
  114.8 0.1 reduce_sum.33
  114.9 5.3 %collective-permute-start.3 = (bf16[40,256]{1,0:T(8,128)(2,1)S(1)}, bf16[40,256]{1,0:T(8,128)(2,1)S(1)}, u32[]{:S(2)}, u32[]{:S(2)}) collective-permute-start(bf16[40,256]{1,0:T(8,128)(2,1)S(1)} %reduce_sum.33), channel_id=1, source_target_pairs={{0,0},{32,512},{512,32},{544,544},{1,1},{33,513},{513,33},{545,545... | collective-permute-start | bytes 61448 | tf_op jit(solution)/shard_map/ppermute | solution.py:54
  120.2 19.1 %all-to-all-done.1 = bf16[32,56,256]{2,1,0:T(8,128)(2,1)S(1)} async-done(((bf16[32,56,256]{2,1,0:T(8,128)(2,1)}), bf16[32,56,256]{2,1,0:T(8,128)(2,1)S(1)}, u32[]{:S(2)}, u32[]{:S(2)}) %all-to-all-start.1) | async-done | bytes 917536 | tf_op jit(solution)/shard_map/all_to_all | solution.py:52
  139.3 0.1 reduce_sum.34
  139.5 1.9 %collective-permute-start.4 = (bf16[56,256]{1,0:T(8,128)(2,1)S(1)}, bf16[56,256]{1,0:T(8,128)(2,1)S(1)}, u32[]{:S(2)}, u32[]{:S(2)}) collective-permute-start(bf16[56,256]{1,0:T(8,128)(2,1)S(1)} %reduce_sum.34), channel_id=1, source_target_pairs={{0,0},{32,512},{512,32},{544,544},{1,1},{33,513},{513,33},{545,545... | collective-permute-start | bytes 86024 | tf_op jit(solution)/shard_map/ppermute | solution.py:54
  141.4 0.7 reshape_add_fusion
  142.1 11.9 %collective-permute-done.4 = bf16[56,256]{1,0:T(8,128)(2,1)S(1)} collective-permute-done((bf16[56,256]{1,0:T(8,128)(2,1)S(1)}, bf16[56,256]{1,0:T(8,128)(2,1)S(1)}, u32[]{:S(2)}, u32[]{:S(2)}) %collective-permute-start.4) | collective-permute-done | bytes 28704 | tf_op jit(solution)/shard_map/ppermute | solution.py:54
  153.9 0.6 fusion.13
  (20 shorter events, 0.2 us)
Async XLA Ops:
  7.2 9.3 %copy-start.4 = (s32[1,16]{1,0:T(1,128)S(1)}, s32[1,16]{1,0:T(1,128)}, u32[]{:S(2)}) copy-start(s32[1,16]{1,0:T(1,128)} %param.12) | copy-start | bytes 196
  7.2 9.3 %copy-start = (bf16[1,192,1024]{2,1,0:T(8,128)(2,1)S(1)}, bf16[1,192,1024]{2,1,0:T(8,128)(2,1)}, u32[]{:S(2)}) copy-start(bf16[1,192,1024]{2,1,0:T(8,128)(2,1)} %param.11) | copy-start | bytes 1179652
  7.2 85.9 %all-gather.2.cloned.1.call-start = ((), (), s32[]{:S(2)}) async-start(), calls=%async_computation.3 | async-start | bytes 1548288 | tf_op jit(solution)/shard_map/all_gather | solution.py:28
  8.3 7.4 %collective-permute-start = (bf16[2,96,384]{2,1,0:T(8,128)(2,1)S(1)}, bf16[2,96,384]{2,1,0:T(8,128)(2,1)S(1)}, u32[]{:S(2)}, u32[]{:S(2)}) collective-permute-start(bf16[2,96,384]{2,1,0:T(8,128)(2,1)S(1)} %get-tuple-element.5), channel_id=1, source_target_pairs={{0,1},{1,0},{2,3},{3,2},{4,5},{5,4},{6,7},{7,6},{8,9},{9,8},{10,11... | collective-permute-start | bytes 442376 | tf_op jit(solution)/shard_map/ppermute | solution.py:25
  11.4 28.6 %collective-permute-start.1 = (bf16[256,384]{1,0:T(8,128)(2,1)S(1)}, bf16[256,384]{1,0:T(8,128)(2,1)S(1)}, u32[]{:S(2)}, u32[]{:S(2)}) collective-permute-start(bf16[256,384]{1,0:T(8,128)(2,1)S(1)} %fusion.11), channel_id=1, source_target_pairs={{0,512},{512,0},{1,513},{513,1},{2,514},{514,2},{3,515},{515,3},{4... | collective-permute-start | bytes 589832 | tf_op jit(solution)/shard_map/ppermute | solution.py:32
  18.0 64.8 %all-to-all-start.2 = ((bf16[16,12,1024]{2,1,0:T(8,128)(2,1)}), bf16[16,12,1024]{2,1,0:T(8,128)(2,1)S(1)}, u32[]{:S(2)}, u32[]{:S(2)}) async-start(bf16[16,12,1024]{2,1,0:T(8,128)(2,1)} %gather_fusion), calls=%async_computation.2 | async-start | bytes 1048576 | tf_op jit(solution)/shard_map/all_to_all | solution.py:39
  40.2 40.7 %collective-permute-start.2 = (bf16[2,256,384]{2,1,0:T(8,128)(2,1)S(1)}, bf16[2,256,384]{2,1,0:T(8,128)(2,1)S(1)}, u32[]{:S(2)}, u32[]{:S(2)}) collective-permute-start(bf16[2,256,384]{2,1,0:T(8,128)(2,1)S(1)} %pad_maximum_fusion.3), channel_id=1, source_target_pairs={{0,1},{1,0},{2,3},{3,2},{4,5},{5,4},{6,7},{7,6},{8,9},{9,8},{10,11... | collective-permute-start | bytes 1179656 | tf_op jit(solution)/shard_map/ppermute | solution.py:34
  82.8 26.6 %all-to-all-start = ((bf16[32,40,256]{2,1,0:T(8,128)(2,1)}), bf16[32,40,256]{2,1,0:T(8,128)(2,1)S(1)}, u32[]{:S(2)}, u32[]{:S(2)}) async-start(bf16[32,40,256]{2,1,0:T(8,128)(2,1)} %bitcast.10), calls=%async_computation | async-start | bytes 1310720 | tf_op jit(solution)/shard_map/all_to_all | solution.py:52
  93.1 2.0 %copy-start.3 = (bf16[896,768]{1,0:T(8,128)(2,1)S(1)}, bf16[896,768]{1,0:T(8,128)(2,1)}, u32[]{:S(2)}) copy-start(bf16[896,768]{1,0:T(8,128)(2,1)} %all-gather.2.cloned.1.call-done) | copy-start | bytes 4128772
  109.4 29.9 %all-to-all-start.1 = ((bf16[32,56,256]{2,1,0:T(8,128)(2,1)}), bf16[32,56,256]{2,1,0:T(8,128)(2,1)S(1)}, u32[]{:S(2)}, u32[]{:S(2)}) async-start(bf16[32,56,256]{2,1,0:T(8,128)(2,1)} %bitcast.14), calls=%async_computation.1 | async-start | bytes 1835008 | tf_op jit(solution)/shard_map/all_to_all | solution.py:52
  114.7 26.7 %copy-start.1 = (f32[1,1,12,1024]{3,1,2,0:T(1,128)S(1)}, f32[1,1,12,1024]{3,1,2,0:T(1,128)}, u32[]{:S(2)}) copy-start(f32[1,1,12,1024]{3,1,2,0:T(1,128)} %param.13) | copy-start | bytes 147460
  114.7 39.2 %copy-start.2 = (bf16[256,96]{0,1:T(8,128)(2,1)S(1)}, bf16[256,96]{0,1:T(8,128)(2,1)}, u32[]{:S(2)}) copy-start(bf16[256,96]{0,1:T(8,128)(2,1)} %param.10) | copy-start | bytes 147460
  114.9 27.1 %collective-permute-start.3 = (bf16[40,256]{1,0:T(8,128)(2,1)S(1)}, bf16[40,256]{1,0:T(8,128)(2,1)S(1)}, u32[]{:S(2)}, u32[]{:S(2)}) collective-permute-start(bf16[40,256]{1,0:T(8,128)(2,1)S(1)} %reduce_sum.33), channel_id=1, source_target_pairs={{0,0},{32,512},{512,32},{544,544},{1,1},{33,513},{513,33},{545,545... | collective-permute-start | bytes 61448 | tf_op jit(solution)/shard_map/ppermute | solution.py:54
  139.5 14.5 %collective-permute-start.4 = (bf16[56,256]{1,0:T(8,128)(2,1)S(1)}, bf16[56,256]{1,0:T(8,128)(2,1)S(1)}, u32[]{:S(2)}, u32[]{:S(2)}) collective-permute-start(bf16[56,256]{1,0:T(8,128)(2,1)S(1)} %reduce_sum.34), channel_id=1, source_target_pairs={{0,0},{32,512},{512,32},{544,544},{1,1},{33,513},{513,33},{545,545... | collective-permute-start | bytes 86024 | tf_op jit(solution)/shard_map/ppermute | solution.py:54
Sparse Core Ops, SparseCore 0:
  16.6 63.4 all-gather.1

commit v3 on v1

v3 whole, which is shorter than its diff:
```python
import jax
import jax.numpy as jnp
from jax import lax
from jax.sharding import Mesh, PartitionSpec as P


def gelu_slope(values):
    normal_cdf = 0.5 * (1.0 + jax.scipy.special.erf(values * 0.7071067811865476))
    return normal_cdf + values * jnp.exp(-0.5 * values * values) * 0.3989422804014327


SWAP = [(0, 1), (1, 0)]
QUAD = ("x_lo", "core")


def last_hop(flip):
    pairs = []
    for y in range(2):
        for q in range(4):
            for b in range(2):
                pairs.append((y * 8 + q * 2 + b, (b ^ flip) * 8 + y * 4 + q))
    return pairs


def on_device(pre_act, act_grad, up_weight, resid_grad, gram_parts, stripe_order, gram_prev):
    core = lax.axis_index("core")
    x_lo = lax.axis_index("x_lo")
    y_hi = lax.axis_index("y_hi")
    tokens, hidden = pre_act.shape
    half = resid_grad.shape[1] // 2

    rows = up_weight.reshape(2, 2, 2, half, hidden)

    def quarter(x_flip, core_flip):
        piece = lax.dynamic_slice(rows, (0, core ^ core_flip, x_lo ^ x_flip, 0, 0), (2, 1, 1, half, hidden))
        piece = piece.reshape(2 * half, hidden)
        if x_flip or core_flip:
            step = 2 * x_flip + core_flip
            piece = lax.ppermute(piece, QUAD, [(i, i ^ step) for i in range(4)])
        return piece

    pair = jnp.concatenate([quarter(0, 0), quarter(1, 0), quarter(0, 1), quarter(1, 1)], axis=-1)
    weight = lax.all_gather(pair, "z", axis=0, tiled=True)

    hidden_grad = (act_grad.astype(jnp.float32) * gelu_slope(pre_act.astype(jnp.float32))).astype(jnp.bfloat16)
    far = lax.ppermute(hidden_grad, "y_hi", SWAP)
    both = jnp.concatenate([hidden_grad, far], axis=0)
    both = jnp.stack([both, lax.ppermute(both, "x_lo", SWAP)])
    mate = lax.ppermute(both, "core", SWAP)
    both = jnp.concatenate([both[0], both[1], mate[0], mate[1]], axis=-1)

    owners = lax.axis_size(("y_hi", "z"))
    stripes = gram_parts[0].reshape(owners, -1, gram_parts.shape[2])
    ordered = stripes[stripe_order[0]]
    kept = lax.all_to_all(ordered, ("y_hi", "z"), 0, 0, tiled=True)
    gram_stats = gram_prev + jnp.sum(kept.astype(jnp.float32), axis=0).reshape(gram_prev.shape)

    partial = lax.dot_general(
        weight, both, (((1,), (1,)), ((), ())), preferred_element_type=jnp.float32
    ).astype(jnp.bfloat16)
    blocks = partial.reshape(-1, half, 2 * tokens)
    arrived = lax.all_to_all(blocks, ("x_hi", "x_mid", "y_lo"), 0, 0, tiled=True)
    shared = jnp.sum(arrived.astype(jnp.float32), axis=0).astype(jnp.bfloat16)
    own, away = shared[:, :tokens], shared[:, tokens:]
    where = ("y_hi", "x_hi", "x_mid", "x_lo")
    one = lax.ppermute(jnp.where(x_lo == y_hi, own, away), where, last_hop(0))
    two = lax.ppermute(jnp.where(x_lo == y_hi, away, own), where, last_hop(1))
    home = jnp.concatenate([jnp.where(y_hi == 0, one, two), jnp.where(y_hi == 0, two, one)], axis=0)
    input_grad = (home.astype(jnp.float32) + resid_grad.T.astype(jnp.float32)).astype(jnp.bfloat16).T
    return (input_grad, gram_stats)


def solution(mesh):
    axes = ("y_hi", "z", "x_hi", "x_mid", "x_lo", "y_lo", "core")
    fine = Mesh(mesh.devices.reshape(2, 8, 2, 2, 2, 4, 2), axes)
    replica, spread = axes[:2], axes[2:]
    return jax.shard_map(
        on_device,
        mesh=fine,
        in_specs=(
            P(replica, spread),
            P(replica, spread),
            P(replica, spread),
            P(replica, spread),
            P(replica, spread, None),
            P(spread, None),
            P(spread, replica, None, None),
        ),
        out_specs=(P(replica, spread), P(spread, replica, None, None)),
        check_vma=False,
    )
```

time: 156 us -> 153 us (0.981)
  the two profiles are of different devices: /device:TPU:112 before, /device:TPU:116 now
where the time goes in v3:
time: 153 us
  waiting for transfers between devices  65.5 us (43%)
  starting transfers between devices  62.5 us (41%)
  between operations  14.2 us (9%)
  matrix products  3.96 us (3%)
  other arithmetic  3.65 us (2%)
  local copies, waits for them, and re-layouts  2.65 us (2%)
    all_to_all x1, starting transfers between devices, on_device(): kept = lax.all_to_all(ordered, ('y_hi', 'z'), 0, 0, tiled=True)  22.1 us
    all_to_all x1, waiting for transfers between devices, on_device(): lax.all_to_all(blocks, ('x_hi', 'x_mid', 'y_lo'), 0, 0, tiled=True)  17.7 us
    ppermute x1, waiting for transfers between devices, on_device(): far = lax.ppermute(hidden_grad, 'y_hi', SWAP)  12.6 us
    ppermute x1, starting transfers between devices, on_device(): one = lax.ppermute(jnp.where(x_lo == y_hi, own, away), where, last_hop(0))  12.5 us
    ppermute x1, waiting for transfers between devices, on_device(): both = jnp.stack([both, lax.ppermute(both, 'x_lo', SWAP)])  10.5 us
    ppermute x1, waiting for transfers between devices, on_device(): two = lax.ppermute(jnp.where(x_lo == y_hi, away, own), where, last_hop(1))  10 us
    all_to_all x1, waiting for transfers between devices, on_device(): kept = lax.all_to_all(ordered, ('y_hi', 'z'), 0, 0, tiled=True)  9.92 us
    all_to_all x1, starting transfers between devices, on_device(): lax.all_to_all(blocks, ('x_hi', 'x_mid', 'y_lo'), 0, 0, tiled=True)  9.45 us
  transfers between devices with their start and end apart: 11, of which 7 were waited for; matrix products, arithmetic and copies ran while one was open for 5% of the time, Pallas kernels for 0%

profile of v3, /device:TPU:116, one launch (start us, length us, event | category | flops | bytes accessed | tf_op | source)
XLA Modules:
  0.0 152.5 jit_solution(699432484811481398)
XLA Ops:
  7.2 0.0 all-gather.2.cloned.1.call-start
  7.2 1.1 constant_dynamic-slice_fusion.3
  8.3 3.4 %collective-permute-start = (bf16[96,384]{1,0:T(8,128)(2,1)S(1)}, bf16[96,384]{1,0:T(8,128)(2,1)S(1)}, u32[]{:S(2)}, u32[]{:S(2)}) collective-permute-start(bf16[96,384]{1,0:T(8,128)(2,1)S(1)} %bitcast.31), channel_id=1, source_target_pairs={{0,8},{1,9},{8,0},{9,1},{2,10},{3,11},{10,2},{11,3},{4,12},{5,13},... | collective-permute-start | bytes 221192 | tf_op jit(solution)/shard_map/ppermute | solution.py:39
  11.7 1.9 %collective-permute-start.1 = (bf16[96,384]{1,0:T(8,128)(2,1)S(1)}, bf16[96,384]{1,0:T(8,128)(2,1)S(1)}, u32[]{:S(2)}, u32[]{:S(2)}) collective-permute-start(bf16[96,384]{1,0:T(8,128)(2,1)S(1)} %bitcast.30), channel_id=1, source_target_pairs={{0,1},{1,0},{8,9},{9,8},{2,3},{3,2},{10,11},{11,10},{4,5},{5,4},{1... | collective-permute-start | bytes 221192 | tf_op jit(solution)/shard_map/ppermute | solution.py:39
  13.7 2.5 %collective-permute-start.2 = (bf16[96,384]{1,0:T(8,128)(2,1)S(1)}, bf16[96,384]{1,0:T(8,128)(2,1)S(1)}, u32[]{:S(2)}, u32[]{:S(2)}) collective-permute-start(bf16[96,384]{1,0:T(8,128)(2,1)S(1)} %bitcast.29), channel_id=1, source_target_pairs={{0,9},{1,8},{8,1},{9,0},{2,11},{3,10},{10,3},{11,2},{4,13},{5,12},... | collective-permute-start | bytes 221192 | tf_op jit(solution)/shard_map/ppermute | solution.py:39
  16.2 3.3 %collective-permute-done.2 = bf16[96,384]{1,0:T(8,128)(2,1)S(1)} collective-permute-done((bf16[96,384]{1,0:T(8,128)(2,1)S(1)}, bf16[96,384]{1,0:T(8,128)(2,1)S(1)}, u32[]{:S(2)}, u32[]{:S(2)}) %collective-permute-start.2) | collective-permute-done | bytes 73760 | tf_op jit(solution)/shard_map/ppermute | solution.py:39
  19.5 0.7 pad_maximum_fusion.2
  20.2 0.0 all-gather.2.cloned.1.call-update
  20.3 1.2 fusion.20
  21.5 4.3 %collective-permute-start.3 = (bf16[256,384]{1,0:T(8,128)(2,1)S(1)}, bf16[256,384]{1,0:T(8,128)(2,1)S(1)}, u32[]{:S(2)}, u32[]{:S(2)}) collective-permute-start(bf16[256,384]{1,0:T(8,128)(2,1)S(1)} %fusion.20), channel_id=1, source_target_pairs={{0,512},{512,0},{1,513},{513,1},{2,514},{514,2},{3,515},{515,3},{4... | collective-permute-start | bytes 589832 | tf_op jit(solution)/shard_map/ppermute | solution.py:46
  25.7 12.6 %collective-permute-done.3 = bf16[256,384]{1,0:T(8,128)(2,1)S(1)} collective-permute-done((bf16[256,384]{1,0:T(8,128)(2,1)S(1)}, bf16[256,384]{1,0:T(8,128)(2,1)S(1)}, u32[]{:S(2)}, u32[]{:S(2)}) %collective-permute-start.3) | collective-permute-done | bytes 196640 | tf_op jit(solution)/shard_map/ppermute | solution.py:46
  38.3 0.1 fusion.25
  38.4 2.4 %collective-permute-start.4 = (bf16[512,384]{1,0:T(8,128)(2,1)S(1)}, bf16[512,384]{1,0:T(8,128)(2,1)S(1)}, u32[]{:S(2)}, u32[]{:S(2)}) collective-permute-start(bf16[512,384]{1,0:T(8,128)(2,1)S(1)} %get-tuple-element.5), channel_id=1, source_target_pairs={{0,8},{8,0},{1,9},{9,1},{2,10},{10,2},{3,11},{11,3},{4,12},{12,4},... | collective-permute-start | bytes 1179656 | tf_op jit(solution)/shard_map/ppermute | solution.py:48
  40.8 10.5 %collective-permute-done.4 = bf16[512,384]{1,0:T(8,128)(2,1)S(1)} collective-permute-done((bf16[512,384]{1,0:T(8,128)(2,1)S(1)}, bf16[512,384]{1,0:T(8,128)(2,1)S(1)}, u32[]{:S(2)}, u32[]{:S(2)}) %collective-permute-start.4) | collective-permute-done | bytes 393248 | tf_op jit(solution)/shard_map/ppermute | solution.py:48
  51.3 0.1 pad_maximum_fusion
  51.4 1.9 %collective-permute-start.5 = (bf16[2,512,384]{2,1,0:T(8,128)(2,1)S(1)}, bf16[2,512,384]{2,1,0:T(8,128)(2,1)S(1)}, u32[]{:S(2)}, u32[]{:S(2)}) collective-permute-start(bf16[2,512,384]{2,1,0:T(8,128)(2,1)S(1)} %pad_maximum_fusion), channel_id=1, source_target_pairs={{0,1},{1,0},{2,3},{3,2},{4,5},{5,4},{6,7},{7,6},{8,9},{9,8},{10,11... | collective-permute-start | bytes 2359304 | tf_op jit(solution)/shard_map/ppermute | solution.py:49
  53.4 0.1 reshape_squeeze.3
  53.5 1.4 gather_fusion
  54.9 22.1 %all-to-all-start.1 = ((bf16[16,12,1024]{2,1,0:T(8,128)(2,1)}), bf16[16,12,1024]{2,1,0:T(8,128)(2,1)S(1)}, u32[]{:S(2)}, u32[]{:S(2)}) async-start(bf16[16,12,1024]{2,1,0:T(8,128)(2,1)} %gather_fusion), calls=%async_computation.1 | async-start | bytes 1048576 | tf_op jit(solution)/shard_map/all_to_all | solution.py:55
  76.9 0.1 slice_bitcast_fusion.1
  77.0 1.5 all-gather.2.cloned.1.call-done
  78.6 4.0 %fusion.10 = bf16[768,512]{1,0:T(8,128)(2,1)} fusion(bf16[768,1536]{1,0:T(8,128)(2,1)} %all-gather.2.cloned.1.call-done, bf16[512,384]{1,0:T(8,128)(2,1)S(1)} %get-tuple-element.3, bf16[512,384]{1,0:T(8,128)(2,1)S(1)} %get-tuple-element.2, bf16[512,384]{1,0:T(8,128)(2,1)S(1)} %collective-permute-done.4, bf16[256,384]{1,0:T(8,128)(2,1)S(1)} %collective-permute-done.3, ...), kind=kOutput, calls=%fused_computation.11 | convolution fusion | flops 1216217088 | bytes 4718592 | tf_op jit(solution)/shard_map/dot_general | solution.py:58
  82.5 9.9 %all-to-all-done.1 = bf16[16,12,1024]{2,1,0:T(8,128)(2,1)S(1)} async-done(((bf16[16,12,1024]{2,1,0:T(8,128)(2,1)}), bf16[16,12,1024]{2,1,0:T(8,128)(2,1)S(1)}, u32[]{:S(2)}, u32[]{:S(2)}) %all-to-all-start.1) | async-done | bytes 393248 | tf_op jit(solution)/shard_map/all_to_all | solution.py:55
  92.4 9.5 %all-to-all-start = ((bf16[16,48,512]{2,1,0:T(8,128)(2,1)}), bf16[16,48,512]{2,1,0:T(8,128)(2,1)S(1)}, u32[]{:S(2)}, u32[]{:S(2)}) async-start(bf16[16,48,512]{2,1,0:T(8,128)(2,1)} %bitcast.9), calls=%async_computation | async-start | bytes 1572864 | tf_op jit(solution)/shard_map/all_to_all | solution.py:62
  101.9 0.1 convert_reduce_fusion
  102.0 17.7 %all-to-all-done = bf16[16,48,512]{2,1,0:T(8,128)(2,1)S(1)} async-done(((bf16[16,48,512]{2,1,0:T(8,128)(2,1)}), bf16[16,48,512]{2,1,0:T(8,128)(2,1)S(1)}, u32[]{:S(2)}, u32[]{:S(2)}) %all-to-all-start) | async-done | bytes 786464 | tf_op jit(solution)/shard_map/all_to_all | solution.py:62
  119.7 0.1 reduce_sum.21
  119.8 12.5 %collective-permute-start.6 = (bf16[48,256]{1,0:T(8,128)(2,1)S(1)}, bf16[48,256]{1,0:T(8,128)(2,1)S(1)}, u32[]{:S(2)}, u32[]{:S(2)}) collective-permute-start(bf16[48,256]{1,0:T(8,128)(2,1)S(1)} %get-tuple-element.12), channel_id=1, source_target_pairs={{0,0},{8,512},{16,8},{24,520},{32,16},{40,528},{48,24},{56,536},{5... | collective-permute-start | bytes 73736 | tf_op jit(solution)/shard_map/ppermute | solution.py:66
  132.4 1.9 %collective-permute-start.7 = (bf16[48,256]{1,0:T(8,128)(2,1)S(1)}, bf16[48,256]{1,0:T(8,128)(2,1)S(1)}, u32[]{:S(2)}, u32[]{:S(2)}) collective-permute-start(bf16[48,256]{1,0:T(8,128)(2,1)S(1)} %get-tuple-element.13), channel_id=1, source_target_pairs={{0,512},{8,0},{16,520},{24,8},{32,528},{40,16},{48,536},{56,24},{5... | collective-permute-start | bytes 73736 | tf_op jit(solution)/shard_map/ppermute | solution.py:67
  134.3 0.7 reshape_add_fusion
  135.0 10.0 %collective-permute-done.7 = bf16[48,256]{1,0:T(8,128)(2,1)S(1)} collective-permute-done((bf16[48,256]{1,0:T(8,128)(2,1)S(1)}, bf16[48,256]{1,0:T(8,128)(2,1)S(1)}, u32[]{:S(2)}, u32[]{:S(2)}) %collective-permute-start.7) | collective-permute-done | bytes 24608 | tf_op jit(solution)/shard_map/ppermute | solution.py:67
  145.0 0.6 fusion.22
  (16 shorter events, 0.1 us)
Async XLA Ops:
  7.2 71.4 %all-gather.2.cloned.1.call-start = ((), (), s32[]{:S(2)}) async-start(), calls=%async_computation.2 | async-start | bytes 2654208 | tf_op jit(solution)/shard_map/all_gather | solution.py:43
  7.2 46.1 %copy-start = (bf16[1,192,1024]{2,1,0:T(8,128)(2,1)S(1)}, bf16[1,192,1024]{2,1,0:T(8,128)(2,1)}, u32[]{:S(2)}) copy-start(bf16[1,192,1024]{2,1,0:T(8,128)(2,1)} %param.11) | copy-start | bytes 1179652
  8.3 7.9 %collective-permute-start = (bf16[96,384]{1,0:T(8,128)(2,1)S(1)}, bf16[96,384]{1,0:T(8,128)(2,1)S(1)}, u32[]{:S(2)}, u32[]{:S(2)}) collective-permute-start(bf16[96,384]{1,0:T(8,128)(2,1)S(1)} %bitcast.31), channel_id=1, source_target_pairs={{0,8},{1,9},{8,0},{9,1},{2,10},{3,11},{10,2},{11,3},{4,12},{5,13},... | collective-permute-start | bytes 221192 | tf_op jit(solution)/shard_map/ppermute | solution.py:39
  11.7 4.5 %collective-permute-start.1 = (bf16[96,384]{1,0:T(8,128)(2,1)S(1)}, bf16[96,384]{1,0:T(8,128)(2,1)S(1)}, u32[]{:S(2)}, u32[]{:S(2)}) collective-permute-start(bf16[96,384]{1,0:T(8,128)(2,1)S(1)} %bitcast.30), channel_id=1, source_target_pairs={{0,1},{1,0},{8,9},{9,8},{2,3},{3,2},{10,11},{11,10},{4,5},{5,4},{1... | collective-permute-start | bytes 221192 | tf_op jit(solution)/shard_map/ppermute | solution.py:39
  13.7 5.8 %collective-permute-start.2 = (bf16[96,384]{1,0:T(8,128)(2,1)S(1)}, bf16[96,384]{1,0:T(8,128)(2,1)S(1)}, u32[]{:S(2)}, u32[]{:S(2)}) collective-permute-start(bf16[96,384]{1,0:T(8,128)(2,1)S(1)} %bitcast.29), channel_id=1, source_target_pairs={{0,9},{1,8},{8,1},{9,0},{2,11},{3,10},{10,3},{11,2},{4,13},{5,12},... | collective-permute-start | bytes 221192 | tf_op jit(solution)/shard_map/ppermute | solution.py:39
  20.2 33.2 %copy-start.3 = (s32[1,16]{1,0:T(1,128)S(1)}, s32[1,16]{1,0:T(1,128)}, u32[]{:S(2)}) copy-start(s32[1,16]{1,0:T(1,128)} %param.12) | copy-start | bytes 196
  21.5 16.8 %collective-permute-start.3 = (bf16[256,384]{1,0:T(8,128)(2,1)S(1)}, bf16[256,384]{1,0:T(8,128)(2,1)S(1)}, u32[]{:S(2)}, u32[]{:S(2)}) collective-permute-start(bf16[256,384]{1,0:T(8,128)(2,1)S(1)} %fusion.20), channel_id=1, source_target_pairs={{0,512},{512,0},{1,513},{513,1},{2,514},{514,2},{3,515},{515,3},{4... | collective-permute-start | bytes 589832 | tf_op jit(solution)/shard_map/ppermute | solution.py:46
  38.4 12.9 %collective-permute-start.4 = (bf16[512,384]{1,0:T(8,128)(2,1)S(1)}, bf16[512,384]{1,0:T(8,128)(2,1)S(1)}, u32[]{:S(2)}, u32[]{:S(2)}) collective-permute-start(bf16[512,384]{1,0:T(8,128)(2,1)S(1)} %get-tuple-element.5), channel_id=1, source_target_pairs={{0,8},{8,0},{1,9},{9,1},{2,10},{10,2},{3,11},{11,3},{4,12},{12,4},... | collective-permute-start | bytes 1179656 | tf_op jit(solution)/shard_map/ppermute | solution.py:48
  51.4 25.5 %collective-permute-start.5 = (bf16[2,512,384]{2,1,0:T(8,128)(2,1)S(1)}, bf16[2,512,384]{2,1,0:T(8,128)(2,1)S(1)}, u32[]{:S(2)}, u32[]{:S(2)}) collective-permute-start(bf16[2,512,384]{2,1,0:T(8,128)(2,1)S(1)} %pad_maximum_fusion), channel_id=1, source_target_pairs={{0,1},{1,0},{2,3},{3,2},{4,5},{5,4},{6,7},{7,6},{8,9},{9,8},{10,11... | collective-permute-start | bytes 2359304 | tf_op jit(solution)/shard_map/ppermute | solution.py:49
  54.9 37.6 %all-to-all-start.1 = ((bf16[16,12,1024]{2,1,0:T(8,128)(2,1)}), bf16[16,12,1024]{2,1,0:T(8,128)(2,1)S(1)}, u32[]{:S(2)}, u32[]{:S(2)}) async-start(bf16[16,12,1024]{2,1,0:T(8,128)(2,1)} %gather_fusion), calls=%async_computation.1 | async-start | bytes 1048576 | tf_op jit(solution)/shard_map/all_to_all | solution.py:55
  82.5 51.8 %copy-start.1 = (f32[1,1,12,1024]{3,1,2,0:T(1,128)S(1)}, f32[1,1,12,1024]{3,1,2,0:T(1,128)}, u32[]{:S(2)}) copy-start(f32[1,1,12,1024]{3,1,2,0:T(1,128)} %param.13) | copy-start | bytes 147460
  82.5 62.5 %copy-start.2 = (bf16[256,96]{0,1:T(8,128)(2,1)S(1)}, bf16[256,96]{0,1:T(8,128)(2,1)}, u32[]{:S(2)}) copy-start(bf16[256,96]{0,1:T(8,128)(2,1)} %param.10) | copy-start | bytes 147460
  92.4 27.3 %all-to-all-start = ((bf16[16,48,512]{2,1,0:T(8,128)(2,1)}), bf16[16,48,512]{2,1,0:T(8,128)(2,1)S(1)}, u32[]{:S(2)}, u32[]{:S(2)}) async-start(bf16[16,48,512]{2,1,0:T(8,128)(2,1)} %bitcast.9), calls=%async_computation | async-start | bytes 1572864 | tf_op jit(solution)/shard_map/all_to_all | solution.py:62
  119.8 15.2 %collective-permute-start.6 = (bf16[48,256]{1,0:T(8,128)(2,1)S(1)}, bf16[48,256]{1,0:T(8,128)(2,1)S(1)}, u32[]{:S(2)}, u32[]{:S(2)}) collective-permute-start(bf16[48,256]{1,0:T(8,128)(2,1)S(1)} %get-tuple-element.12), channel_id=1, source_target_pairs={{0,0},{8,512},{16,8},{24,520},{32,16},{40,528},{48,24},{56,536},{5... | collective-permute-start | bytes 73736 | tf_op jit(solution)/shard_map/ppermute | solution.py:66
  132.4 12.6 %collective-permute-start.7 = (bf16[48,256]{1,0:T(8,128)(2,1)S(1)}, bf16[48,256]{1,0:T(8,128)(2,1)S(1)}, u32[]{:S(2)}, u32[]{:S(2)}) collective-permute-start(bf16[48,256]{1,0:T(8,128)(2,1)S(1)} %get-tuple-element.13), channel_id=1, source_target_pairs={{0,512},{8,0},{16,520},{24,8},{32,528},{40,16},{48,536},{56,24},{5... | collective-permute-start | bytes 73736 | tf_op jit(solution)/shard_map/ppermute | solution.py:67
Sparse Core Ops, SparseCore 0:
  20.4 58.1 all-gather.1

commit v4 on v1

v4 whole, which is shorter than its diff:
```python
import jax
import jax.numpy as jnp
from jax import lax
from jax.sharding import Mesh, PartitionSpec as P


def gelu_slope(values):
    normal_cdf = 0.5 * (1.0 + jax.scipy.special.erf(values * 0.7071067811865476))
    return normal_cdf + values * jnp.exp(-0.5 * values * values) * 0.3989422804014327


SWAP = [(0, 1), (1, 0)]
QUAD = ("x_lo", "core")
WHERE = ("y_hi", "x_hi", "x_mid", "x_lo", "y_lo")


def last_hop():
    pairs = []
    for y in range(2):
        for x in range(8):
            for low in range(4):
                s, z2, b, z1, z0 = x >> 2, (x >> 1) & 1, x & 1, low >> 1, low & 1
                pairs.append(((y * 8 + x) * 4 + low, ((y ^ s) * 8 + y * 4 + z2 * 2 + z1) * 4 + z0 * 2 + b))
    return pairs


def beside(parts):
    return jnp.concatenate([parts[i] for i in range(parts.shape[0])], axis=-1)


def on_device(pre_act, act_grad, up_weight, resid_grad, gram_parts, stripe_order, gram_prev):
    tokens, hidden = pre_act.shape
    feats = resid_grad.shape[1]

    quarters = lax.all_to_all(up_weight.reshape(4, feats, hidden), QUAD, 0, 0, tiled=True)
    weight = lax.all_gather(beside(quarters), "z", axis=0, tiled=True)

    hidden_grad = (act_grad.astype(jnp.float32) * gelu_slope(pre_act.astype(jnp.float32))).astype(jnp.bfloat16)
    far_grad = lax.ppermute(hidden_grad, "y_hi", SWAP)
    own = beside(lax.all_gather(hidden_grad, QUAD, axis=0))
    far = beside(lax.all_gather(far_grad, QUAD, axis=0))

    owners = lax.axis_size(("y_hi", "z"))
    stripes = gram_parts[0].reshape(owners, -1, gram_parts.shape[2])
    ordered = stripes[stripe_order[0]]
    kept = lax.all_to_all(ordered, ("y_hi", "z"), 0, 0, tiled=True)
    weight, kept = lax.optimization_barrier((weight, kept))
    gram_stats = gram_prev + jnp.sum(kept.astype(jnp.float32), axis=0).reshape(gram_prev.shape)

    contract = (((1,), (1,)), ((), ()))
    partial = jnp.stack(
        [
            lax.dot_general(weight, grads, contract, preferred_element_type=jnp.float32).astype(jnp.bfloat16)
            for grads in (own, far)
        ]
    )
    blocks = partial.reshape(-1, feats, tokens)
    arrived = lax.all_to_all(blocks, ("x_hi", "x_mid", "y_lo"), 0, 0, tiled=True)
    shared = jnp.sum(arrived.astype(jnp.float32), axis=0).astype(jnp.bfloat16)
    home = lax.ppermute(shared, WHERE, last_hop())
    input_grad = (home.astype(jnp.float32) + resid_grad.T.astype(jnp.float32)).astype(jnp.bfloat16).T
    return (input_grad, gram_stats)


def solution(mesh):
    axes = ("y_hi", "z", "x_hi", "x_mid", "x_lo", "y_lo", "core")
    fine = Mesh(mesh.devices.reshape(2, 8, 2, 2, 2, 4, 2), axes)
    replica, spread = axes[:2], axes[2:]
    return jax.shard_map(
        on_device,
        mesh=fine,
        in_specs=(
            P(replica, spread),
            P(replica, spread),
            P(replica, spread),
            P(replica, spread),
            P(replica, spread, None),
            P(spread, None),
            P(spread, replica, None, None),
        ),
        out_specs=(P(replica, spread), P(spread, replica, None, None)),
        check_vma=False,
    )
```

time: 156 us -> 144 us (0.923); the launches traced: 156 us -> 141 us
  waiting for transfers between devices: 85.1 us -> 54 us
  blocking collectives: 0 us -> 26.2 us
  starting transfers between devices: 46 us -> 38.6 us
    all_gather x0 -> x2, blocking collectives: none -> 16.2 us  [the longest x1 8.77 us: on_device(): far = beside(lax.all_gather(far_grad, QUAD, axis=0))]
    all_to_all x1, waiting for transfers between devices: 36.2 us -> 20.3 us  [on_device(): lax.all_to_all(blocks, ('x_hi', 'x_mid', 'y_lo'), 0, 0, tiled=True)]
    ppermute x4 -> x2, waiting for transfers between devices: 22.1 us -> 9.43 us  [the longest x1 9.43 us: on_device(): home = lax.ppermute(shared, WHERE, last_hop())]
    all_to_all x0 -> x1, blocking collectives: none -> 9.95 us  [on_device(): lax.all_to_all(up_weight.reshape(4, feats, hidden), QUAD, 0, 0, tiled=True)]
    ppermute x4 -> x2, starting transfers between devices: 13.7 us -> 6.18 us  [the longest x1 4.26 us: on_device(): far_grad = lax.ppermute(hidden_grad, 'y_hi', SWAP)]
    all_gather x1, waiting for transfers between devices: 26.8 us -> 24 us  [on_device(): weight = lax.all_gather(beside(quarters), 'z', axis=0, tiled=True)]
  transfers between devices with their start and end apart: 7 -> 5, of which waited for: 5 -> 4; matrix products, arithmetic and copies ran while one was open for 5% -> 2% of each run, Pallas kernels for 0% -> 0%
where the time goes in v4:
time: 144 us; the launch traced here: 141 us
  waiting for transfers between devices  54 us (38%)
  starting transfers between devices  38.6 us (27%)
  blocking collectives  26.2 us (18%)
  between operations  14.2 us (10%)
  other arithmetic  3.45 us (2%)
  matrix products  3.42 us (2%)
  local copies, waits for them, and re-layouts  1.7 us (1%)
    all_gather x1, waiting for transfers between devices, on_device(): weight = lax.all_gather(beside(quarters), 'z', axis=0, tiled=True)  24 us
    all_to_all x1, starting transfers between devices, on_device(): kept = lax.all_to_all(ordered, ('y_hi', 'z'), 0, 0, tiled=True)  22.1 us
    all_to_all x1, waiting for transfers between devices, on_device(): lax.all_to_all(blocks, ('x_hi', 'x_mid', 'y_lo'), 0, 0, tiled=True)  20.3 us
    all_to_all x1, starting transfers between devices, on_device(): lax.all_to_all(blocks, ('x_hi', 'x_mid', 'y_lo'), 0, 0, tiled=True)  10.3 us
    all_to_all x1, blocking collectives, on_device(): lax.all_to_all(up_weight.reshape(4, feats, hidden), QUAD, 0, 0, tiled=True)  9.95 us
    ppermute x1, waiting for transfers between devices, on_device(): home = lax.ppermute(shared, WHERE, last_hop())  9.43 us
    all_gather x1, blocking collectives, on_device(): far = beside(lax.all_gather(far_grad, QUAD, axis=0))  8.77 us
    all_gather x1, blocking collectives, on_device(): own = beside(lax.all_gather(hidden_grad, QUAD, axis=0))  7.45 us
  transfers between devices with their start and end apart: 5, of which 4 were waited for; matrix products, arithmetic and copies ran while one was open for 2% of the time, Pallas kernels for 0%

profile of v4, /device:TPU:112, one launch (start us, length us, event | category | flops | bytes accessed | tf_op | source)
XLA Modules:
  0.0 141.5 jit_solution(9685019763686141786)
XLA Ops:
  7.2 0.0 all-gather.4.cloned.1.call-start
  7.2 9.9 %all_to_all.15 = bf16[4,96,384]{2,1,0:T(8,128)(2,1)S(1)} all-to-all(bf16[4,96,384]{2,1,0:T(8,128)(2,1)} %bitcast.28), channel_id=1, replica_groups=mesh['y_hi'=2,'z'=8,'x_hi'=2,'x_mid'=2,'x_lo'=2,'y_lo'=4,'core'=2] {'x_l..., dimensions={0} | all-to-all | bytes 589824 | tf_op jit(solution)/shard_map/all_to_all | solution.py:35
  17.2 0.8 pad_maximum_fusion.1
  18.0 0.0 all-gather.4.cloned.1.call-update
  18.0 0.0 copy-done.2
  18.0 0.0 copy-done.1
  18.0 0.2 fusion.23
  18.2 4.3 %collective-permute-start = (bf16[256,384]{1,0:T(8,128)(2,1)S(1)}, bf16[256,384]{1,0:T(8,128)(2,1)S(1)}, u32[]{:S(2)}, u32[]{:S(2)}) collective-permute-start(bf16[256,384]{1,0:T(8,128)(2,1)S(1)} %fusion.23), channel_id=1, source_target_pairs={{0,512},{512,0},{1,513},{513,1},{2,514},{514,2},{3,515},{515,3},{4... | collective-permute-start | bytes 589832 | tf_op jit(solution)/shard_map/ppermute | solution.py:39
  22.5 0.1 reshape_squeeze.3
  22.6 0.0 copy-done.6
  22.6 1.4 gather_fusion
  24.0 22.1 %all-to-all-start.1 = ((bf16[16,12,1024]{2,1,0:T(8,128)(2,1)}), bf16[16,12,1024]{2,1,0:T(8,128)(2,1)S(1)}, u32[]{:S(2)}, u32[]{:S(2)}) async-start(bf16[16,12,1024]{2,1,0:T(8,128)(2,1)} %gather_fusion), calls=%async_computation.1 | async-start | bytes 1048576 | tf_op jit(solution)/shard_map/all_to_all | solution.py:46
  46.1 7.5 %all-gather = bf16[1024,384]{1,0:T(8,128)(2,1)S(1)} all-gather(bf16[256,384]{1,0:T(8,128)(2,1)S(1)} %fusion.23), channel_id=2, replica_groups=mesh['y_hi'=2,'z'=8,'x_hi'=2,'x_mid'=2,'x_lo'=2,'y_lo'=4,'core'=2] {'x_l..., dimensions={0}, use_global_device_ids=true | all-gather | bytes 983040 | tf_op jit(solution)/shard_map/all_gather | solution.py:40
  53.6 0.1 fusion.29
  53.6 0.0 collective-permute-done
  53.7 8.8 %all-gather.1 = bf16[1024,384]{1,0:T(8,128)(2,1)S(1)} all-gather(bf16[256,384]{1,0:T(8,128)(2,1)S(1)} %collective-permute-done), channel_id=3, replica_groups=mesh['y_hi'=2,'z'=8,'x_hi'=2,'x_mid'=2,'x_lo'=2,'y_lo'=4,'core'=2] {'x_l..., dimensions={0}, use_global_device_ids=true | all-gather | bytes 983040 | tf_op jit(solution)/shard_map/all_gather | solution.py:41
  62.4 0.1 fusion.30
  62.5 0.3 all-to-all-done.1
  62.8 24.0 %all-gather.4.cloned.1.call-done = bf16[768,1536]{1,0:T(8,128)(2,1)} async-done(((bf16[96,1536]{1,0:T(8,128)(2,1)}), bf16[768,1536]{1,0:T(8,128)(2,1)}) %all-gather.4.cloned.1.call-update) | async-done | bytes 2359312 | tf_op jit(solution)/shard_map/all_gather | solution.py:36
  86.8 2.6 %fusion.1 = bf16[1,768,256]{2,1,0:T(8,128)(2,1)S(1)} fusion(bf16[768,1536]{1,0:T(8,128)(2,1)} %all-gather.4.cloned.1.call-done, bf16[256,384]{1,0:T(8,128)(2,1)S(1)} %get-tuple-element.13, bf16[256,384]{1,0:T(8,128)(2,1)S(1)} %get-tuple-element.11, bf16[256,384]{1,0:T(8,128)(2,1)S(1)} %get-tuple-element.12, bf16[256,384]{1,0:T(8,128)(2,1)S(1)} %get-tuple-element.10), kind=kOutput, calls=%fused_computation.4 | convolution fusion | flops 607322112 | bytes 3538944 | tf_op jit(solution)/shard_map/dot_general | solution.py:53
  89.4 0.8 fusion
  90.2 1.0 pad_maximum_fusion
  91.2 10.3 %all-to-all-start.2 = ((bf16[16,96,256]{2,1,0:T(8,128)(2,1)}), bf16[16,96,256]{2,1,0:T(8,128)(2,1)S(1)}, u32[]{:S(2)}, u32[]{:S(2)}) async-start(bf16[16,96,256]{2,1,0:T(8,128)(2,1)} %bitcast.9), calls=%async_computation.2 | async-start | bytes 1572864 | tf_op jit(solution)/shard_map/all_to_all | solution.py:58
  101.5 0.1 convert_reduce_fusion
  101.6 20.3 %all-to-all-done.2 = bf16[16,96,256]{2,1,0:T(8,128)(2,1)S(1)} async-done(((bf16[16,96,256]{2,1,0:T(8,128)(2,1)}), bf16[16,96,256]{2,1,0:T(8,128)(2,1)S(1)}, u32[]{:S(2)}, u32[]{:S(2)}) %all-to-all-start.2) | async-done | bytes 786464 | tf_op jit(solution)/shard_map/all_to_all | solution.py:58
  121.8 0.1 reduce_sum.21
  121.9 1.9 %collective-permute-start.1 = (bf16[96,256]{1,0:T(8,128)(2,1)S(1)}, bf16[96,256]{1,0:T(8,128)(2,1)S(1)}, u32[]{:S(2)}, u32[]{:S(2)}) collective-permute-start(bf16[96,256]{1,0:T(8,128)(2,1)S(1)} %reduce_sum.21), channel_id=1, source_target_pairs={{0,0},{2,4},{4,8},{6,12},{8,2},{10,6},{12,10},{14,14},{16,16},{18,... | collective-permute-start | bytes 147464 | tf_op jit(solution)/shard_map/ppermute | solution.py:60
  123.9 0.0 copy-done.3
  123.9 0.7 reshape_add_fusion
  124.6 9.4 %collective-permute-done.1 = bf16[96,256]{1,0:T(8,128)(2,1)S(1)} collective-permute-done((bf16[96,256]{1,0:T(8,128)(2,1)S(1)}, bf16[96,256]{1,0:T(8,128)(2,1)S(1)}, u32[]{:S(2)}, u32[]{:S(2)}) %collective-permute-start.1) | collective-permute-done | bytes 49184 | tf_op jit(solution)/shard_map/ppermute | solution.py:60
  134.0 0.0 copy-done.4
  134.0 0.6 fusion.25
  (12 shorter events, 0.1 us)
Async XLA Ops:
  7.2 10.9 %copy-start.2 = (bf16[256,384]{1,0:T(8,128)(2,1)S(1)}, bf16[256,384]{1,0:T(8,128)(2,1)}, u32[]{:S(2)}) copy-start(bf16[256,384]{1,0:T(8,128)(2,1)} %param.8) | copy-start | bytes 589828
  7.2 10.9 %copy-start.1 = (bf16[256,384]{1,0:T(8,128)(2,1)S(1)}, bf16[256,384]{1,0:T(8,128)(2,1)}, u32[]{:S(2)}) copy-start(bf16[256,384]{1,0:T(8,128)(2,1)} %param.7) | copy-start | bytes 589828
  7.2 15.3 %copy-start = (bf16[1,192,1024]{2,1,0:T(8,128)(2,1)S(1)}, bf16[1,192,1024]{2,1,0:T(8,128)(2,1)}, u32[]{:S(2)}) copy-start(bf16[1,192,1024]{2,1,0:T(8,128)(2,1)} %param.11) | copy-start | bytes 1179652
  7.2 79.6 %all-gather.4.cloned.1.call-start = ((), (), s32[]{:S(2)}) async-start(), calls=%async_computation.3 | async-start | bytes 2654208 | tf_op jit(solution)/shard_map/all_gather | solution.py:36
  17.2 5.4 %copy-start.6 = (s32[1,16]{1,0:T(1,128)S(1)}, s32[1,16]{1,0:T(1,128)}, u32[]{:S(2)}) copy-start(s32[1,16]{1,0:T(1,128)} %param.12) | copy-start | bytes 196
  18.2 35.4 %collective-permute-start = (bf16[256,384]{1,0:T(8,128)(2,1)S(1)}, bf16[256,384]{1,0:T(8,128)(2,1)S(1)}, u32[]{:S(2)}, u32[]{:S(2)}) collective-permute-start(bf16[256,384]{1,0:T(8,128)(2,1)S(1)} %fusion.23), channel_id=1, source_target_pairs={{0,512},{512,0},{1,513},{513,1},{2,514},{514,2},{3,515},{515,3},{4... | collective-permute-start | bytes 589832 | tf_op jit(solution)/shard_map/ppermute | solution.py:39
  24.0 38.7 %all-to-all-start.1 = ((bf16[16,12,1024]{2,1,0:T(8,128)(2,1)}), bf16[16,12,1024]{2,1,0:T(8,128)(2,1)S(1)}, u32[]{:S(2)}, u32[]{:S(2)}) async-start(bf16[16,12,1024]{2,1,0:T(8,128)(2,1)} %gather_fusion), calls=%async_computation.1 | async-start | bytes 1048576 | tf_op jit(solution)/shard_map/all_to_all | solution.py:46
  86.8 2.6 %copy-start.5 = (bf16[768,1536]{1,0:T(8,128)(2,1)S(1)}, bf16[768,1536]{1,0:T(8,128)(2,1)}, u32[]{:S(2)}) copy-start(bf16[768,1536]{1,0:T(8,128)(2,1)} %all-gather.4.cloned.1.call-done) | copy-start | bytes 7077892
  91.2 32.7 %copy-start.3 = (f32[1,1,12,1024]{3,1,2,0:T(1,128)S(1)}, f32[1,1,12,1024]{3,1,2,0:T(1,128)}, u32[]{:S(2)}) copy-start(f32[1,1,12,1024]{3,1,2,0:T(1,128)} %param.13) | copy-start | bytes 147460
  91.2 42.8 %copy-start.4 = (bf16[256,96]{0,1:T(8,128)(2,1)S(1)}, bf16[256,96]{0,1:T(8,128)(2,1)}, u32[]{:S(2)}) copy-start(bf16[256,96]{0,1:T(8,128)(2,1)} %param.10) | copy-start | bytes 147460
  91.2 30.6 %all-to-all-start.2 = ((bf16[16,96,256]{2,1,0:T(8,128)(2,1)}), bf16[16,96,256]{2,1,0:T(8,128)(2,1)S(1)}, u32[]{:S(2)}, u32[]{:S(2)}) async-start(bf16[16,96,256]{2,1,0:T(8,128)(2,1)} %bitcast.9), calls=%async_computation.2 | async-start | bytes 1572864 | tf_op jit(solution)/shard_map/all_to_all | solution.py:58
  121.9 12.0 %collective-permute-start.1 = (bf16[96,256]{1,0:T(8,128)(2,1)S(1)}, bf16[96,256]{1,0:T(8,128)(2,1)S(1)}, u32[]{:S(2)}, u32[]{:S(2)}) collective-permute-start(bf16[96,256]{1,0:T(8,128)(2,1)S(1)} %reduce_sum.21), channel_id=1, source_target_pairs={{0,0},{2,4},{4,8},{6,12},{8,2},{10,6},{12,10},{14,14},{16,16},{18,... | collective-permute-start | bytes 147464 | tf_op jit(solution)/shard_map/ppermute | solution.py:60
Sparse Core Ops, SparseCore 0:
  18.1 68.5 all-gather.3

commit v5 on v4

--- a/solution.py
+++ b/solution.py
@@ -11,16 +11,24 @@
 
 SWAP = [(0, 1), (1, 0)]
 QUAD = ("x_lo", "core")
-WHERE = ("y_hi", "x_hi", "x_mid", "x_lo", "y_lo")
+WHERE = ("y_hi", "z", "x_hi", "x_mid", "x_lo", "y_lo")
+ORDER = (0, 1, 7, 2, 6, 3, 5, 4)
+
+
+def from_z(value, step):
+    return lax.ppermute(value, "z", [((i + step) % 8, i) for i in range(8)])
 
 
 def last_hop():
     pairs = []
     for y in range(2):
-        for x in range(8):
-            for low in range(4):
-                s, z2, b, z1, z0 = x >> 2, (x >> 1) & 1, x & 1, low >> 1, low & 1
-                pairs.append(((y * 8 + x) * 4 + low, ((y ^ s) * 8 + y * 4 + z2 * 2 + z1) * 4 + z0 * 2 + b))
+        for z in range(8):
+            for x in range(8):
+                for low in range(4):
+                    s, b, p = x >> 2, x & 1, ((x >> 1) & 1) * 4 + low
+                    w = (z + ORDER[p]) % 8
+                    target = (((y ^ s) * 8 + z) * 8 + y * 4 + (w >> 1)) * 4 + (w & 1) * 2 + b
+                    pairs.append((((y * 8 + z) * 8 + x) * 4 + low, target))
     return pairs
 
 
@@ -32,29 +40,39 @@
     tokens, hidden = pre_act.shape
     feats = resid_grad.shape[1]
 
-    quarters = lax.all_to_all(up_weight.reshape(4, feats, hidden), QUAD, 0, 0, tiled=True)
-    weight = lax.all_gather(beside(quarters), "z", axis=0, tiled=True)
-
     hidden_grad = (act_grad.astype(jnp.float32) * gelu_slope(pre_act.astype(jnp.float32))).astype(jnp.bfloat16)
     far_grad = lax.ppermute(hidden_grad, "y_hi", SWAP)
-    own = beside(lax.all_gather(hidden_grad, QUAD, axis=0))
-    far = beside(lax.all_gather(far_grad, QUAD, axis=0))
 
     owners = lax.axis_size(("y_hi", "z"))
     stripes = gram_parts[0].reshape(owners, -1, gram_parts.shape[2])
     ordered = stripes[stripe_order[0]]
+
+    quarters = lax.all_to_all(up_weight.reshape(4, feats, hidden), QUAD, 0, 0, tiled=True)
+    mine = beside(quarters)
+    mine, hidden_grad, ordered = lax.optimization_barrier((mine, hidden_grad, ordered))
+    ring = {0: mine}
+    for step in (2, 6, 1, 7):
+        ring[step] = from_z(mine, step)
+    ring[3] = from_z(ring[2], 1)
+    ring[5] = from_z(ring[6], 7)
+    mid = feats // 2
+    ring[4] = jnp.concatenate([from_z(ring[2][:mid], 2), from_z(ring[6][mid:], 6)], axis=0)
+
+    own = beside(lax.all_gather(hidden_grad, QUAD, axis=0))
+    far_grad, own = lax.optimization_barrier((far_grad, own))
+    far = beside(lax.all_gather(far_grad, QUAD, axis=0))
     kept = lax.all_to_all(ordered, ("y_hi", "z"), 0, 0, tiled=True)
-    weight, kept = lax.optimization_barrier((weight, kept))
+    ring[4], kept = lax.optimization_barrier((ring[4], kept))
     gram_stats = gram_prev + jnp.sum(kept.astype(jnp.float32), axis=0).reshape(gram_prev.shape)
 
     contract = (((1,), (1,)), ((), ()))
-    partial = jnp.stack(
-        [
-            lax.dot_general(weight, grads, contract, preferred_element_type=jnp.float32).astype(jnp.bfloat16)
-            for grads in (own, far)
-        ]
-    )
-    blocks = partial.reshape(-1, feats, tokens)
+    pieces = []
+    for grads in (own, far):
+        for group in (ORDER[:5], ORDER[5:]):
+            weight = jnp.concatenate([ring[step] for step in group], axis=0)
+            product = lax.dot_general(weight, grads, contract, preferred_element_type=jnp.float32)
+            pieces.append(product.astype(jnp.bfloat16))
+    blocks = jnp.concatenate(pieces, axis=0).reshape(-1, feats, tokens)
     arrived = lax.all_to_all(blocks, ("x_hi", "x_mid", "y_lo"), 0, 0, tiled=True)
     shared = jnp.sum(arrived.astype(jnp.float32), axis=0).astype(jnp.bfloat16)
     home = lax.ppermute(shared, WHERE, last_hop())

time: 144 us -> 150 us (1.042)
  starting transfers between devices: 38.6 us -> 71.3 us
  waiting for transfers between devices: 54 us -> 40.3 us
  between operations: 14.2 us -> 0.95 us
  blocking collectives: 26.2 us -> 17.8 us
  local copies, waits for them, and re-layouts: 1.7 us -> 7.68 us
  matrix products: 3.42 us -> 5.17 us
    ppermute x0 -> x8, starting transfers between devices: none -> 40.4 us  [from_z(): return lax.ppermute(value, 'z', [((i + step) % 8, i) for i in range(8)])]
    all_gather x1 -> x0, waiting for transfers between devices: 24 us -> none  [on_device(): weight = lax.all_gather(beside(quarters), 'z', axis=0, tiled=True)]
    all_to_all x1, starting transfers between devices: 22.1 us -> 11.1 us  [on_device(): kept = lax.all_to_all(ordered, ('y_hi', 'z'), 0, 0, tiled=True)]
    all_to_all x1 -> x0, blocking collectives: 9.95 us -> none  [on_device(): lax.all_to_all(up_weight.reshape(4, feats, hidden), QUAD, 0, 0, tiled=True)]
    ppermute x0 -> x8, waiting for transfers between devices: none -> 8.99 us  [from_z(): return lax.ppermute(value, 'z', [((i + step) % 8, i) for i in range(8)])]
    all_to_all x0 -> x1, starting transfers between devices: none -> 3.46 us  [on_device(): lax.all_to_all(up_weight.reshape(4, feats, hidden), QUAD, 0, 0, tiled=True)]
    unnamed x14 -> x26, local copies, waits for them, and re-layouts: 0.03 us -> 3.49 us
    dot_general x2 -> x4, matrix products: 3.42 us -> 5.17 us  [on_device(): lax.dot_general(weight, grads, contract, preferred_element_type=jnp.float32)]
  transfers between devices with their start and end apart: 5 -> 13, of which waited for: 4 -> 6; matrix products, arithmetic and copies ran while one was open for 2% -> 9% of each run, Pallas kernels for 0% -> 0%
where the time goes in v5:
time: 150 us; the launch traced here: 147 us
  starting transfers between devices  71.3 us (48%)
  waiting for transfers between devices  40.3 us (27%)
  blocking collectives  17.8 us (12%)
  local copies, waits for them, and re-layouts  7.68 us (5%)
  matrix products  5.17 us (3%)
  other arithmetic  3.79 us (3%)
    ppermute x8, starting transfers between devices, from_z(): return lax.ppermute(value, 'z', [((i + step) % 8, i) for i in range(8)])  40.4 us
    all_to_all x1, waiting for transfers between devices, on_device(): lax.all_to_all(blocks, ('x_hi', 'x_mid', 'y_lo'), 0, 0, tiled=True)  21.6 us
    all_to_all x1, starting transfers between devices, on_device(): kept = lax.all_to_all(ordered, ('y_hi', 'z'), 0, 0, tiled=True)  11.1 us
    all_to_all x1, starting transfers between devices, on_device(): lax.all_to_all(blocks, ('x_hi', 'x_mid', 'y_lo'), 0, 0, tiled=True)  10.2 us
    ppermute x1, waiting for transfers between devices, on_device(): home = lax.ppermute(shared, WHERE, last_hop())  9.78 us
    all_gather x1, blocking collectives, on_device(): own = beside(lax.all_gather(hidden_grad, QUAD, axis=0))  9.09 us
    ppermute x8, waiting for transfers between devices, from_z(): return lax.ppermute(value, 'z', [((i + step) % 8, i) for i in range(8)])  8.99 us
    all_gather x1, blocking collectives, on_device(): far = beside(lax.all_gather(far_grad, QUAD, axis=0))  8.72 us
  transfers between devices with their start and end apart: 13, of which 6 were waited for; matrix products, arithmetic and copies ran while one was open for 9% of the time, Pallas kernels for 0%

profile of v5, /device:TPU:112, one launch (start us, length us, event | category | flops | bytes accessed | tf_op | source)
XLA Modules:
  0.0 147.1 jit_solution(18094362775617799540)
XLA Ops:
  0.6 3.5 %all-to-all-start = ((bf16[4,96,384]{2,1,0:T(8,128)(2,1)}), bf16[4,96,384]{2,1,0:T(8,128)(2,1)S(1)}, u32[]{:S(2)}, u32[]{:S(2)}) async-start(bf16[4,96,384]{2,1,0:T(8,128)(2,1)} %bitcast.28), calls=%async_computation | async-start | bytes 589824 | tf_op jit(solution)/shard_map/all_to_all | solution.py:50
  4.1 1.2 fusion.7
  5.3 4.3 %collective-permute-start.4 = (bf16[256,384]{1,0:T(8,128)(2,1)S(1)}, bf16[256,384]{1,0:T(8,128)(2,1)S(1)}, u32[]{:S(2)}, u32[]{:S(2)}) collective-permute-start(bf16[256,384]{1,0:T(8,128)(2,1)S(1)} %fusion.7), channel_id=1, source_target_pairs={{0,512},{512,0},{1,513},{513,1},{2,514},{514,2},{3,515},{515,3},{4... | collective-permute-start | bytes 589832 | tf_op jit(solution)/shard_map/ppermute | solution.py:44
  9.6 1.1 reshape_squeeze.3
  10.7 1.4 gather_fusion
  12.2 17.3 %collective-permute-start = (bf16[96,1536]{1,0:T(8,128)(2,1)S(1)}, bf16[96,1536]{1,0:T(8,128)(2,1)S(1)}, u32[]{:S(2)}, u32[]{:S(2)}) collective-permute-start(bf16[96,1536]{1,0:T(8,128)(2,1)S(1)} %pad_maximum_fusion.3), channel_id=1, source_target_pairs={{64,0},{128,64},{192,128},{256,192},{320,256},{384,320},{448,384},... | collective-permute-start | bytes 884744 | tf_op jit(solution)/shard_map/ppermute | solution.py:19
  29.5 1.9 %collective-permute-start.1 = (bf16[96,1536]{1,0:T(8,128)(2,1)S(1)}, bf16[96,1536]{1,0:T(8,128)(2,1)S(1)}, u32[]{:S(2)}, u32[]{:S(2)}) collective-permute-start(bf16[96,1536]{1,0:T(8,128)(2,1)S(1)} %pad_maximum_fusion.3), channel_id=1, source_target_pairs={{448,0},{0,64},{64,128},{128,192},{192,256},{256,320},{320,384},{3... | collective-permute-start | bytes 884744 | tf_op jit(solution)/shard_map/ppermute | solution.py:19
  31.4 3.4 %collective-permute-start.2 = (bf16[96,1536]{1,0:T(8,128)(2,1)S(1)}, bf16[96,1536]{1,0:T(8,128)(2,1)S(1)}, u32[]{:S(2)}, u32[]{:S(2)}) collective-permute-start(bf16[96,1536]{1,0:T(8,128)(2,1)S(1)} %pad_maximum_fusion.3), channel_id=1, source_target_pairs={{128,0},{192,64},{256,128},{320,192},{384,256},{448,320},{0,384},{... | collective-permute-start | bytes 884744 | tf_op jit(solution)/shard_map/ppermute | solution.py:19
  34.8 3.4 %collective-permute-start.3 = (bf16[96,1536]{1,0:T(8,128)(2,1)S(1)}, bf16[96,1536]{1,0:T(8,128)(2,1)S(1)}, u32[]{:S(2)}, u32[]{:S(2)}) collective-permute-start(bf16[96,1536]{1,0:T(8,128)(2,1)S(1)} %pad_maximum_fusion.3), channel_id=1, source_target_pairs={{384,0},{448,64},{0,128},{64,192},{128,256},{192,320},{256,384},{3... | collective-permute-start | bytes 884744 | tf_op jit(solution)/shard_map/ppermute | solution.py:19
  38.2 9.1 %all-gather = bf16[1024,384]{1,0:T(8,128)(2,1)S(1)} all-gather(bf16[256,384]{1,0:T(8,128)(2,1)S(1)} %fusion.7), channel_id=2, replica_groups=mesh['y_hi'=2,'z'=8,'x_hi'=2,'x_mid'=2,'x_lo'=2,'y_lo'=4,'core'=2] {'x_l..., dimensions={0}, use_global_device_ids=true | all-gather | bytes 983040 | tf_op jit(solution)/shard_map/all_gather | solution.py:61
  47.5 8.7 %all-gather.1 = bf16[1024,384]{1,0:T(8,128)(2,1)S(1)} all-gather(bf16[256,384]{1,0:T(8,128)(2,1)S(1)} %collective-permute-done.4), channel_id=3, replica_groups=mesh['y_hi'=2,'z'=8,'x_hi'=2,'x_mid'=2,'x_lo'=2,'y_lo'=4,'core'=2] {'x_l..., dimensions={0}, use_global_device_ids=true | all-gather | bytes 983040 | tf_op jit(solution)/shard_map/all_gather | solution.py:63
  56.2 0.8 fusion.13
  57.0 0.8 constant_dynamic-update-slice_fusion.4
  57.8 11.1 %all-to-all-start.1 = ((bf16[16,12,1024]{2,1,0:T(8,128)(2,1)}), bf16[16,12,1024]{2,1,0:T(8,128)(2,1)S(1)}, u32[]{:S(2)}, u32[]{:S(2)}) async-start(bf16[16,12,1024]{2,1,0:T(8,128)(2,1)} %gather_fusion), calls=%async_computation.1 | async-start | bytes 1048576 | tf_op jit(solution)/shard_map/all_to_all | solution.py:64
  68.9 5.5 %collective-permute-start.7 = (bf16[48,1536]{1,0:T(8,128)(2,1)S(1)}, bf16[48,1536]{1,0:T(8,128)(2,1)S(1)}, u32[]{:S(2)}, u32[]{:S(2)}) collective-permute-start(bf16[48,1536]{1,0:T(8,128)(2,1)S(1)} %slice.74), channel_id=1, source_target_pairs={{128,0},{192,64},{256,128},{320,192},{384,256},{448,320},{0,384},{... | collective-permute-start | bytes 442376 | tf_op jit(solution)/shard_map/ppermute | solution.py:19
  74.4 1.9 %collective-permute-start.8 = (bf16[48,1536]{1,0:T(8,128)(2,1)S(1)}, bf16[48,1536]{1,0:T(8,128)(2,1)S(1)}, u32[]{:S(2)}, u32[]{:S(2)}) collective-permute-start(bf16[48,1536]{1,0:T(8,128)(2,1)S(1)} %slice.75), channel_id=1, source_target_pairs={{384,0},{448,64},{0,128},{64,192},{128,256},{192,320},{256,384},{3... | collective-permute-start | bytes 442376 | tf_op jit(solution)/shard_map/ppermute | solution.py:19
  76.4 0.7 constant_dynamic-update-slice_fusion.3
  77.1 0.7 constant_dynamic-update-slice_fusion.2
  77.8 0.8 constant_dynamic-update-slice_fusion.1
  79.3 2.1 %convolution_convert_fusion.1 = bf16[480,256]{1,0:T(8,128)(2,1)S(1)} fusion(bf16[480,1536]{1,0:T(8,128)(2,1)} %constant_dynamic-update-slice_fusion, bf16[256,1536]{1,0:T(8,128)(2,1)S(1)} %pad_maximum_fusion), kind=kOutput, calls=%fused_computation.2 | convolution fusion | flops 377610240 | bytes 2506752 | tf_op jit(solution)/shard_map/dot_general | solution.py:73
  81.4 5.1 %collective-permute-start.5 = (bf16[96,1536]{1,0:T(8,128)(2,1)S(1)}, bf16[96,1536]{1,0:T(8,128)(2,1)S(1)}, u32[]{:S(2)}, u32[]{:S(2)}) collective-permute-start(bf16[96,1536]{1,0:T(8,128)(2,1)S(1)} %collective-permute-done.2), channel_id=1, source_target_pairs={{64,0},{128,64},{192,128},{256,192},{320,256},{384,320},{448,384},... | collective-permute-start | bytes 884744 | tf_op jit(solution)/shard_map/ppermute | solution.py:19
  86.6 1.3 convolution_convert_fusion
  87.9 1.9 %collective-permute-start.6 = (bf16[96,1536]{1,0:T(8,128)(2,1)S(1)}, bf16[96,1536]{1,0:T(8,128)(2,1)S(1)}, u32[]{:S(2)}, u32[]{:S(2)}) collective-permute-start(bf16[96,1536]{1,0:T(8,128)(2,1)S(1)} %collective-permute-done.3), channel_id=1, source_target_pairs={{448,0},{0,64},{64,128},{128,192},{192,256},{256,320},{320,384},{3... | collective-permute-start | bytes 884744 | tf_op jit(solution)/shard_map/ppermute | solution.py:19
  90.0 1.1 collective-permute-done.8
  91.1 4.1 %collective-permute-done.5 = bf16[96,1536]{1,0:T(8,128)(2,1)S(1)} collective-permute-done((bf16[96,1536]{1,0:T(8,128)(2,1)S(1)}, bf16[96,1536]{1,0:T(8,128)(2,1)S(1)}, u32[]{:S(2)}, u32[]{:S(2)}) %collective-permute-start.5) | collective-permute-done | bytes 294944 | tf_op jit(solution)/shard_map/ppermute | solution.py:19
  95.3 3.6 %collective-permute-done.6 = bf16[96,1536]{1,0:T(8,128)(2,1)S(1)} collective-permute-done((bf16[96,1536]{1,0:T(8,128)(2,1)S(1)}, bf16[96,1536]{1,0:T(8,128)(2,1)S(1)}, u32[]{:S(2)}, u32[]{:S(2)}) %collective-permute-start.6) | collective-permute-done | bytes 294944 | tf_op jit(solution)/shard_map/ppermute | solution.py:19
  99.8 1.4 convolution_convert_fusion.2
  101.2 0.9 pad_maximum_fusion.2
  102.1 10.2 %all-to-all-start.2 = ((bf16[16,96,256]{2,1,0:T(8,128)(2,1)}), bf16[16,96,256]{2,1,0:T(8,128)(2,1)S(1)}, u32[]{:S(2)}, u32[]{:S(2)}) async-start(bf16[16,96,256]{2,1,0:T(8,128)(2,1)} %bitcast.7), calls=%async_computation.2 | async-start | bytes 1572864 | tf_op jit(solution)/shard_map/all_to_all | solution.py:76
  112.4 21.6 %all-to-all-done.2 = bf16[16,96,256]{2,1,0:T(8,128)(2,1)S(1)} async-done(((bf16[16,96,256]{2,1,0:T(8,128)(2,1)}), bf16[16,96,256]{2,1,0:T(8,128)(2,1)S(1)}, u32[]{:S(2)}, u32[]{:S(2)}) %all-to-all-start.2) | async-done | bytes 786464 | tf_op jit(solution)/shard_map/all_to_all | solution.py:76
  134.0 1.9 %collective-permute-start.9 = (bf16[96,256]{1,0:T(8,128)(2,1)S(1)}, bf16[96,256]{1,0:T(8,128)(2,1)S(1)}, u32[]{:S(2)}, u32[]{:S(2)}) collective-permute-start(bf16[96,256]{1,0:T(8,128)(2,1)S(1)} %reduce_sum.21), channel_id=1, source_target_pairs={{0,0},{2,4},{4,28},{6,8},{8,2},{10,6},{12,30},{14,10},{16,24},{18,... | collective-permute-start | bytes 147464 | tf_op jit(solution)/shard_map/ppermute | solution.py:78
  136.7 9.8 %collective-permute-done.9 = bf16[96,256]{1,0:T(8,128)(2,1)S(1)} collective-permute-done((bf16[96,256]{1,0:T(8,128)(2,1)S(1)}, bf16[96,256]{1,0:T(8,128)(2,1)S(1)}, u32[]{:S(2)}, u32[]{:S(2)}) %collective-permute-start.9) | collective-permute-done | bytes 49184 | tf_op jit(solution)/shard_map/ppermute | solution.py:78
  (46 shorter events, 3.7 us)
Async XLA Ops:
  0.6 10.1 %copy-start.9 = (s32[1,16]{1,0:T(1,128)S(1)}, s32[1,16]{1,0:T(1,128)}, u32[]{:S(2)}) copy-start(s32[1,16]{1,0:T(1,128)} %param.12) | copy-start | bytes 196
  0.6 11.5 %all-to-all-start = ((bf16[4,96,384]{2,1,0:T(8,128)(2,1)}), bf16[4,96,384]{2,1,0:T(8,128)(2,1)S(1)}, u32[]{:S(2)}, u32[]{:S(2)}) async-start(bf16[4,96,384]{2,1,0:T(8,128)(2,1)} %bitcast.28), calls=%async_computation | async-start | bytes 589824 | tf_op jit(solution)/shard_map/all_to_all | solution.py:50
  5.3 42.1 %collective-permute-start.4 = (bf16[256,384]{1,0:T(8,128)(2,1)S(1)}, bf16[256,384]{1,0:T(8,128)(2,1)S(1)}, u32[]{:S(2)}, u32[]{:S(2)}) collective-permute-start(bf16[256,384]{1,0:T(8,128)(2,1)S(1)} %fusion.7), channel_id=1, source_target_pairs={{0,512},{512,0},{1,513},{513,1},{2,514},{514,2},{3,515},{515,3},{4... | collective-permute-start | bytes 589832 | tf_op jit(solution)/shard_map/ppermute | solution.py:44
  12.2 64.2 %collective-permute-start = (bf16[96,1536]{1,0:T(8,128)(2,1)S(1)}, bf16[96,1536]{1,0:T(8,128)(2,1)S(1)}, u32[]{:S(2)}, u32[]{:S(2)}) collective-permute-start(bf16[96,1536]{1,0:T(8,128)(2,1)S(1)} %pad_maximum_fusion.3), channel_id=1, source_target_pairs={{64,0},{128,64},{192,128},{256,192},{320,256},{384,320},{448,384},... | collective-permute-start | bytes 884744 | tf_op jit(solution)/shard_map/ppermute | solution.py:19
  29.5 47.6 %collective-permute-start.1 = (bf16[96,1536]{1,0:T(8,128)(2,1)S(1)}, bf16[96,1536]{1,0:T(8,128)(2,1)S(1)}, u32[]{:S(2)}, u32[]{:S(2)}) collective-permute-start(bf16[96,1536]{1,0:T(8,128)(2,1)S(1)} %pad_maximum_fusion.3), channel_id=1, source_target_pairs={{448,0},{0,64},{64,128},{128,192},{192,256},{256,320},{320,384},{3... | collective-permute-start | bytes 884744 | tf_op jit(solution)/shard_map/ppermute | solution.py:19
  31.4 37.4 %collective-permute-start.2 = (bf16[96,1536]{1,0:T(8,128)(2,1)S(1)}, bf16[96,1536]{1,0:T(8,128)(2,1)S(1)}, u32[]{:S(2)}, u32[]{:S(2)}) collective-permute-start(bf16[96,1536]{1,0:T(8,128)(2,1)S(1)} %pad_maximum_fusion.3), channel_id=1, source_target_pairs={{128,0},{192,64},{256,128},{320,192},{384,256},{448,320},{0,384},{... | collective-permute-start | bytes 884744 | tf_op jit(solution)/shard_map/ppermute | solution.py:19
  34.8 39.6 %collective-permute-start.3 = (bf16[96,1536]{1,0:T(8,128)(2,1)S(1)}, bf16[96,1536]{1,0:T(8,128)(2,1)S(1)}, u32[]{:S(2)}, u32[]{:S(2)}) collective-permute-start(bf16[96,1536]{1,0:T(8,128)(2,1)S(1)} %pad_maximum_fusion.3), channel_id=1, source_target_pairs={{384,0},{448,64},{0,128},{64,192},{128,256},{192,320},{256,384},{3... | collective-permute-start | bytes 884744 | tf_op jit(solution)/shard_map/ppermute | solution.py:19
  57.0 29.5 %copy-start.1 = (bf16[256,384]{1,0:T(8,128)(2,1)}, bf16[256,384]{1,0:T(8,128)(2,1)S(1)}, u32[]{:S(2)}) copy-start(bf16[256,384]{1,0:T(8,128)(2,1)S(1)} %get-tuple-element.17) | copy-start | bytes 589828
  57.8 41.1 %all-to-all-start.1 = ((bf16[16,12,1024]{2,1,0:T(8,128)(2,1)}), bf16[16,12,1024]{2,1,0:T(8,128)(2,1)S(1)}, u32[]{:S(2)}, u32[]{:S(2)}) async-start(bf16[16,12,1024]{2,1,0:T(8,128)(2,1)} %gather_fusion), calls=%async_computation.1 | async-start | bytes 1048576 | tf_op jit(solution)/shard_map/all_to_all | solution.py:64
  68.9 21.1 %collective-permute-start.7 = (bf16[48,1536]{1,0:T(8,128)(2,1)S(1)}, bf16[48,1536]{1,0:T(8,128)(2,1)S(1)}, u32[]{:S(2)}, u32[]{:S(2)}) collective-permute-start(bf16[48,1536]{1,0:T(8,128)(2,1)S(1)} %slice.74), channel_id=1, source_target_pairs={{128,0},{192,64},{256,128},{320,192},{384,256},{448,320},{0,384},{... | collective-permute-start | bytes 442376 | tf_op jit(solution)/shard_map/ppermute | solution.py:19
  74.4 16.6 %collective-permute-start.8 = (bf16[48,1536]{1,0:T(8,128)(2,1)S(1)}, bf16[48,1536]{1,0:T(8,128)(2,1)S(1)}, u32[]{:S(2)}, u32[]{:S(2)}) collective-permute-start(bf16[48,1536]{1,0:T(8,128)(2,1)S(1)} %slice.75), channel_id=1, source_target_pairs={{384,0},{448,64},{0,128},{64,192},{128,256},{192,320},{256,384},{3... | collective-permute-start | bytes 442376 | tf_op jit(solution)/shard_map/ppermute | solution.py:19
  79.3 7.2 %copy-start.3 = (bf16[256,384]{1,0:T(8,128)(2,1)S(1)}, bf16[256,384]{1,0:T(8,128)(2,1)}, u32[]{:S(2)}) copy-start(bf16[256,384]{1,0:T(8,128)(2,1)} %get-tuple-element.18) | copy-start | bytes 589828
  79.3 7.2 %copy-start.5 = (bf16[256,384]{1,0:T(8,128)(2,1)S(1)}, bf16[256,384]{1,0:T(8,128)(2,1)}, u32[]{:S(2)}) copy-start(bf16[256,384]{1,0:T(8,128)(2,1)} %get-tuple-element.19) | copy-start | bytes 589828
  79.3 7.3 %copy-start.6 = (bf16[480,1536]{1,0:T(8,128)(2,1)S(1)}, bf16[480,1536]{1,0:T(8,128)(2,1)}, u32[]{:S(2)}) copy-start(bf16[480,1536]{1,0:T(8,128)(2,1)} %constant_dynamic-update-slice_fusion) | copy-start | bytes 4423684
  81.4 13.8 %collective-permute-start.5 = (bf16[96,1536]{1,0:T(8,128)(2,1)S(1)}, bf16[96,1536]{1,0:T(8,128)(2,1)S(1)}, u32[]{:S(2)}, u32[]{:S(2)}) collective-permute-start(bf16[96,1536]{1,0:T(8,128)(2,1)S(1)} %collective-permute-done.2), channel_id=1, source_target_pairs={{64,0},{128,64},{192,128},{256,192},{320,256},{384,320},{448,384},... | collective-permute-start | bytes 884744 | tf_op jit(solution)/shard_map/ppermute | solution.py:19
  87.9 11.0 %collective-permute-start.6 = (bf16[96,1536]{1,0:T(8,128)(2,1)S(1)}, bf16[96,1536]{1,0:T(8,128)(2,1)S(1)}, u32[]{:S(2)}, u32[]{:S(2)}) collective-permute-start(bf16[96,1536]{1,0:T(8,128)(2,1)S(1)} %collective-permute-done.3), channel_id=1, source_target_pairs={{448,0},{0,64},{64,128},{128,192},{192,256},{256,320},{320,384},{3... | collective-permute-start | bytes 884744 | tf_op jit(solution)/shard_map/ppermute | solution.py:19
  95.3 4.1 %copy-start.2 = (bf16[256,384]{1,0:T(8,128)(2,1)S(1)}, bf16[256,384]{1,0:T(8,128)(2,1)}, u32[]{:S(2)}) copy-start(bf16[256,384]{1,0:T(8,128)(2,1)} %copy-done.1) | copy-start | bytes 589828
  98.8 0.9 copy-start.4
  99.8 1.4 copy-start
  102.1 33.9 %copy-start.7 = (f32[1,1,12,1024]{3,1,2,0:T(1,128)S(1)}, f32[1,1,12,1024]{3,1,2,0:T(1,128)}, u32[]{:S(2)}) copy-start(f32[1,1,12,1024]{3,1,2,0:T(1,128)} %param.13) | copy-start | bytes 147460
  102.1 44.3 %copy-start.8 = (bf16[256,96]{0,1:T(8,128)(2,1)S(1)}, bf16[256,96]{0,1:T(8,128)(2,1)}, u32[]{:S(2)}) copy-start(bf16[256,96]{0,1:T(8,128)(2,1)} %param.10) | copy-start | bytes 147460
  102.1 31.8 %all-to-all-start.2 = ((bf16[16,96,256]{2,1,0:T(8,128)(2,1)}), bf16[16,96,256]{2,1,0:T(8,128)(2,1)S(1)}, u32[]{:S(2)}, u32[]{:S(2)}) async-start(bf16[16,96,256]{2,1,0:T(8,128)(2,1)} %bitcast.7), calls=%async_computation.2 | async-start | bytes 1572864 | tf_op jit(solution)/shard_map/all_to_all | solution.py:76
  134.0 12.4 %collective-permute-start.9 = (bf16[96,256]{1,0:T(8,128)(2,1)S(1)}, bf16[96,256]{1,0:T(8,128)(2,1)S(1)}, u32[]{:S(2)}, u32[]{:S(2)}) collective-permute-start(bf16[96,256]{1,0:T(8,128)(2,1)S(1)} %reduce_sum.21), channel_id=1, source_target_pairs={{0,0},{2,4},{4,28},{6,8},{8,2},{10,6},{12,30},{14,10},{16,24},{18,... | collective-permute-start | bytes 147464 | tf_op jit(solution)/shard_map/ppermute | solution.py:78

commit v6 on v5

--- a/solution.py
+++ b/solution.py
@@ -1,6 +1,8 @@
 import jax
 import jax.numpy as jnp
 from jax import lax
+from jax.experimental import pallas as pl
+from jax.experimental.pallas import tpu as pltpu
 from jax.sharding import Mesh, PartitionSpec as P
 
 
@@ -36,6 +38,40 @@
     return jnp.concatenate([parts[i] for i in range(parts.shape[0])], axis=-1)
 
 
+def products(own, far, pieces, feats, before=None):
+    sources, tokens, hidden = own.shape
+    rows = sum(piece.shape[0] for piece in pieces)
+    done = 0 if before is None else before.shape[1]
+
+    def kernel(*refs):
+        own_ref, far_ref, out_ref = refs[0], refs[1], refs[-1]
+        piece_refs = refs[2 : 2 + len(pieces)]
+        for slot, grads_ref in enumerate((own_ref, far_ref)):
+            total = None
+            for source in range(sources):
+                columns = slice(source * hidden, (source + 1) * hidden)
+                weight = jnp.concatenate([ref[:, columns] for ref in piece_refs], axis=0)
+                term = lax.dot_general(
+                    weight, grads_ref[source], (((1,), (1,)), ((), ())), preferred_element_type=jnp.float32
+                )
+                total = term if total is None else total + term
+            if before is not None:
+                out_ref[slot, :done] = refs[2 + len(pieces)][slot]
+            out_ref[slot, done:] = total.astype(jnp.bfloat16)
+
+    operands = [own, far, *pieces] + ([] if before is None else [before])
+    return pl.pallas_call(
+        kernel,
+        out_shape=jax.ShapeDtypeStruct((2, done + rows, tokens), jnp.bfloat16),
+        in_specs=[pl.BlockSpec(memory_space=pltpu.VMEM)] * len(operands),
+        out_specs=pl.BlockSpec(memory_space=pltpu.VMEM),
+        compiler_params=pltpu.CompilerParams(vmem_limit_bytes=32 * 1024 * 1024),
+        cost_estimate=pl.CostEstimate(
+            flops=4 * rows * tokens * sources * hidden, bytes_accessed=6000000, transcendentals=0
+        ),
+    )(*operands)
+
+
 def on_device(pre_act, act_grad, up_weight, resid_grad, gram_parts, stripe_order, gram_prev):
     tokens, hidden = pre_act.shape
     feats = resid_grad.shape[1]
@@ -43,36 +79,33 @@
     hidden_grad = (act_grad.astype(jnp.float32) * gelu_slope(pre_act.astype(jnp.float32))).astype(jnp.bfloat16)
     far_grad = lax.ppermute(hidden_grad, "y_hi", SWAP)
 
-    owners = lax.axis_size(("y_hi", "z"))
-    stripes = gram_parts[0].reshape(owners, -1, gram_parts.shape[2])
-    ordered = stripes[stripe_order[0]]
-
     quarters = lax.all_to_all(up_weight.reshape(4, feats, hidden), QUAD, 0, 0, tiled=True)
     mine = beside(quarters)
-    mine, hidden_grad, ordered = lax.optimization_barrier((mine, hidden_grad, ordered))
+    mine, hidden_grad = lax.optimization_barrier((mine, hidden_grad))
     ring = {0: mine}
     for step in (2, 6, 1, 7):
         ring[step] = from_z(mine, step)
+    own = lax.all_gather(hidden_grad, QUAD, axis=0)
+    own, parts = lax.optimization_barrier((own, gram_parts[0]))
+    stripes = parts.reshape(lax.axis_size(("y_hi", "z")), -1, parts.shape[1])
+    ordered = stripes[stripe_order[0]]
+
+    *first, far_grad, own, ordered = lax.optimization_barrier(
+        (ring[1], ring[7], ring[2], ring[6], far_grad, own, ordered)
+    )
+    ring[1], ring[7], ring[2], ring[6] = first
     ring[3] = from_z(ring[2], 1)
     ring[5] = from_z(ring[6], 7)
     mid = feats // 2
-    ring[4] = jnp.concatenate([from_z(ring[2][:mid], 2), from_z(ring[6][mid:], 6)], axis=0)
+    upper, lower = from_z(ring[2][:mid], 2), from_z(ring[6][mid:], 6)
+    far = lax.all_gather(far_grad, QUAD, axis=0)
+    kept = lax.all_to_all(ordered, ("y_hi", "z"), 0, 0, tiled=True)
 
-    own = beside(lax.all_gather(hidden_grad, QUAD, axis=0))
-    far_grad, own = lax.optimization_barrier((far_grad, own))
-    far = beside(lax.all_gather(far_grad, QUAD, axis=0))
-    kept = lax.all_to_all(ordered, ("y_hi", "z"), 0, 0, tiled=True)
-    ring[4], kept = lax.optimization_barrier((ring[4], kept))
+    near = products(own, far, [ring[step] for step in ORDER[:5]], feats)
+    upper, kept = lax.optimization_barrier((upper, kept))
     gram_stats = gram_prev + jnp.sum(kept.astype(jnp.float32), axis=0).reshape(gram_prev.shape)
-
-    contract = (((1,), (1,)), ((), ()))
-    pieces = []
-    for grads in (own, far):
-        for group in (ORDER[:5], ORDER[5:]):
-            weight = jnp.concatenate([ring[step] for step in group], axis=0)
-            product = lax.dot_general(weight, grads, contract, preferred_element_type=jnp.float32)
-            pieces.append(product.astype(jnp.bfloat16))
-    blocks = jnp.concatenate(pieces, axis=0).reshape(-1, feats, tokens)
+    blocks = products(own, far, [ring[3], ring[5], upper, lower], feats, near)
+    blocks = blocks.reshape(-1, feats, tokens)
     arrived = lax.all_to_all(blocks, ("x_hi", "x_mid", "y_lo"), 0, 0, tiled=True)
     shared = jnp.sum(arrived.astype(jnp.float32), axis=0).astype(jnp.bfloat16)
     home = lax.ppermute(shared, WHERE, last_hop())

time: 150 us -> 140 us (0.933)
  matrix products: 5.17 us -> 0 us
  Pallas kernels: 0 us -> 4 us
  local copies, waits for them, and re-layouts: 7.68 us -> 3.78 us
  blocking collectives: 17.8 us -> 15.4 us
  starting transfers between devices: 71.3 us -> 69.4 us
  waiting for transfers between devices: 40.3 us -> 42 us
    dot_general x4 -> x0, matrix products: 5.17 us -> none  [on_device(): lax.dot_general(weight, grads, contract, preferred_element_type=jnp.float32)]
    pallas_call x0 -> x2, Pallas kernels: none -> 4 us  [products(): pl.pallas_call(kernel, out_shape=jax.ShapeDtypeStruct((2, done + rows, to...]
    all_gather x2, blocking collectives: 17.8 us -> 15.4 us  [the longest x1 7.95 us: on_device(): far = lax.all_gather(far_grad, QUAD, axis=0)]
    all_to_all x1, starting transfers between devices: 11.1 us -> 8.91 us  [on_device(): kept = lax.all_to_all(ordered, ('y_hi', 'z'), 0, 0, tiled=True)]
    unnamed x26 -> x16, local copies, waits for them, and re-layouts: 3.49 us -> 1.6 us
    all_to_all x1, waiting for transfers between devices: 0.01 us -> 1.82 us  [on_device(): lax.all_to_all(up_weight.reshape(4, feats, hidden), QUAD, 0, 0, tiled=True)]
  transfers between devices with their start and end apart: 13 -> 13, of which waited for: 6 -> 5; matrix products, arithmetic and copies ran while one was open for 9% -> 3% of each run, Pallas kernels for 0% -> 1%
where the time goes in v6:
time: 140 us; the launch traced here: 138 us
  starting transfers between devices  69.4 us (50%)
  waiting for transfers between devices  42 us (30%)
  blocking collectives  15.4 us (11%)
  Pallas kernels  4 us (3%)
  local copies, waits for them, and re-layouts  3.78 us (3%)
  other arithmetic  2.79 us (2%)
    ppermute x8, starting transfers between devices, from_z(): return lax.ppermute(value, 'z', [((i + step) % 8, i) for i in range(8)])  39.3 us
    all_to_all x1, waiting for transfers between devices, on_device(): lax.all_to_all(blocks, ('x_hi', 'x_mid', 'y_lo'), 0, 0, tiled=True)  21 us
    all_to_all x1, starting transfers between devices, on_device(): lax.all_to_all(blocks, ('x_hi', 'x_mid', 'y_lo'), 0, 0, tiled=True)  10.7 us
    ppermute x8, waiting for transfers between devices, from_z(): return lax.ppermute(value, 'z', [((i + step) % 8, i) for i in range(8)])  9.84 us
    ppermute x1, waiting for transfers between devices, on_device(): home = lax.ppermute(shared, WHERE, last_hop())  9.34 us
    all_to_all x1, starting transfers between devices, on_device(): kept = lax.all_to_all(ordered, ('y_hi', 'z'), 0, 0, tiled=True)  8.91 us
    all_gather x1, blocking collectives, on_device(): far = lax.all_gather(far_grad, QUAD, axis=0)  7.95 us
    all_gather x1, blocking collectives, on_device(): own = lax.all_gather(hidden_grad, QUAD, axis=0)  7.47 us
  transfers between devices with their start and end apart: 13, of which 5 were waited for; matrix products, arithmetic and copies ran while one was open for 3% of the time, Pallas kernels for 1%

profile of v6, /device:TPU:112, one launch (start us, length us, event | category | flops | bytes accessed | tf_op | source)
XLA Modules:
  0.0 138.3 jit_solution(3282535835026928858)
XLA Ops:
  0.7 3.6 %all-to-all-start = ((bf16[4,96,384]{2,1,0:T(8,128)(2,1)}), bf16[4,96,384]{2,1,0:T(8,128)(2,1)S(1)}, u32[]{:S(2)}, u32[]{:S(2)}) async-start(bf16[4,96,384]{2,1,0:T(8,128)(2,1)} %bitcast.30), calls=%async_computation | async-start | bytes 589824 | tf_op jit(solution)/shard_map/all_to_all | solution.py:82
  4.3 0.2 fusion.7
  4.5 4.3 %collective-permute-start.4 = (bf16[256,384]{1,0:T(8,128)(2,1)S(1)}, bf16[256,384]{1,0:T(8,128)(2,1)}, u32[]{:S(2)}, u32[]{:S(2)}) collective-permute-start(bf16[256,384]{1,0:T(8,128)(2,1)S(1)} %fusion.7), channel_id=1, source_target_pairs={{0,512},{512,0},{1,513},{513,1},{2,514},{514,2},{3,515},{515,3},{4... | collective-permute-start | bytes 589832 | tf_op jit(solution)/shard_map/ppermute | solution.py:80
  8.8 1.8 %all-to-all-done = bf16[4,96,384]{2,1,0:T(8,128)(2,1)S(1)} async-done(((bf16[4,96,384]{2,1,0:T(8,128)(2,1)}), bf16[4,96,384]{2,1,0:T(8,128)(2,1)S(1)}, u32[]{:S(2)}, u32[]{:S(2)}) %all-to-all-start) | async-done | bytes 294944 | tf_op jit(solution)/shard_map/all_to_all | solution.py:82
  10.7 17.4 %collective-permute-start = (bf16[96,1536]{1,0:T(8,128)(2,1)S(1)}, bf16[96,1536]{1,0:T(8,128)(2,1)S(1)}, u32[]{:S(2)}, u32[]{:S(2)}) collective-permute-start(bf16[96,1536]{1,0:T(8,128)(2,1)S(1)} %pad_maximum_fusion.refs_2_), channel_id=1, source_target_pairs={{64,0},{128,64},{192,128},{256,192},{320,256},{384,320},{448,384},... | collective-permute-start | bytes 884744 | tf_op jit(solution)/shard_map/ppermute | solution.py:21
  28.1 1.9 %collective-permute-start.1 = (bf16[96,1536]{1,0:T(8,128)(2,1)S(1)}, bf16[96,1536]{1,0:T(8,128)(2,1)S(1)}, u32[]{:S(2)}, u32[]{:S(2)}) collective-permute-start(bf16[96,1536]{1,0:T(8,128)(2,1)S(1)} %pad_maximum_fusion.refs_2_), channel_id=1, source_target_pairs={{448,0},{0,64},{64,128},{128,192},{192,256},{256,320},{320,384},{3... | collective-permute-start | bytes 884744 | tf_op jit(solution)/shard_map/ppermute | solution.py:21
  30.1 3.4 %collective-permute-start.2 = (bf16[96,1536]{1,0:T(8,128)(2,1)S(1)}, bf16[96,1536]{1,0:T(8,128)(2,1)S(1)}, u32[]{:S(2)}, u32[]{:S(2)}) collective-permute-start(bf16[96,1536]{1,0:T(8,128)(2,1)S(1)} %pad_maximum_fusion.refs_2_), channel_id=1, source_target_pairs={{128,0},{192,64},{256,128},{320,192},{384,256},{448,320},{0,384},{... | collective-permute-start | bytes 884744 | tf_op jit(solution)/shard_map/ppermute | solution.py:21
  33.4 3.4 %collective-permute-start.3 = (bf16[96,1536]{1,0:T(8,128)(2,1)S(1)}, bf16[96,1536]{1,0:T(8,128)(2,1)S(1)}, u32[]{:S(2)}, u32[]{:S(2)}) collective-permute-start(bf16[96,1536]{1,0:T(8,128)(2,1)S(1)} %pad_maximum_fusion.refs_2_), channel_id=1, source_target_pairs={{384,0},{448,64},{0,128},{64,192},{128,256},{192,320},{256,384},{3... | collective-permute-start | bytes 884744 | tf_op jit(solution)/shard_map/ppermute | solution.py:21
  36.8 7.5 %all-gather = bf16[1024,384]{1,0:T(8,128)(2,1)S(1)} all-gather(bf16[256,384]{1,0:T(8,128)(2,1)S(1)} %fusion.7), channel_id=2, replica_groups=mesh['y_hi'=2,'z'=8,'x_hi'=2,'x_mid'=2,'x_lo'=2,'y_lo'=4,'core'=2] {'x_l..., dimensions={0}, use_global_device_ids=true | all-gather | bytes 983040 | tf_op jit(solution)/shard_map/all_gather | solution.py:88
  44.3 0.1 reshape.45
  44.4 1.4 %gather_fusion = bf16[16,12,1024]{2,1,0:T(8,128)(2,1)} fusion(bf16[16,12,1024]{2,1,0:T(8,128)(2,1)S(1)} %reshape.45, s32[1024]{0:T(1024)S(1)} %pad_clamp_fusion), kind=kCustom, calls=%fused_computation | custom fusion | bytes 786496 | tf_op jit(solution)/shard_map/gather | solution.py:91
  45.8 6.1 %collective-permute-done.3.refs_6_ = bf16[96,1536]{1,0:T(8,128)(2,1)S(1)} collective-permute-done((bf16[96,1536]{1,0:T(8,128)(2,1)S(1)}, bf16[96,1536]{1,0:T(8,128)(2,1)S(1)}, u32[]{:S(2)}, u32[]{:S(2)}) %collective-permute-start.3) | collective-permute-done | bytes 294944 | tf_op jit(solution)/shard_map/ppermute | solution.py:21
  51.9 8.9 %all-to-all-start.1 = ((bf16[16,12,1024]{2,1,0:T(8,128)(2,1)}), bf16[16,12,1024]{2,1,0:T(8,128)(2,1)}, u32[]{:S(2)}, u32[]{:S(2)}) async-start(bf16[16,12,1024]{2,1,0:T(8,128)(2,1)} %gather_fusion), calls=%async_computation.1 | async-start | bytes 1048576 | tf_op jit(solution)/shard_map/all_to_all | solution.py:102
  60.8 4.6 %collective-permute-start.5 = (bf16[96,1536]{1,0:T(8,128)(2,1)S(1)}, bf16[96,1536]{1,0:T(8,128)(2,1)}, u32[]{:S(2)}, u32[]{:S(2)}) collective-permute-start(bf16[96,1536]{1,0:T(8,128)(2,1)S(1)} %collective-permute-done.2.refs_5_), channel_id=1, source_target_pairs={{64,0},{128,64},{192,128},{256,192},{320,256},{384,320},{448,384},... | collective-permute-start | bytes 884744 | tf_op jit(solution)/shard_map/ppermute | solution.py:21
  65.4 1.9 %collective-permute-start.6 = (bf16[96,1536]{1,0:T(8,128)(2,1)S(1)}, bf16[96,1536]{1,0:T(8,128)(2,1)}, u32[]{:S(2)}, u32[]{:S(2)}) collective-permute-start(bf16[96,1536]{1,0:T(8,128)(2,1)S(1)} %collective-permute-done.3.refs_6_), channel_id=1, source_target_pairs={{448,0},{0,64},{64,128},{128,192},{192,256},{256,320},{320,384},{3... | collective-permute-start | bytes 884744 | tf_op jit(solution)/shard_map/ppermute | solution.py:21
  67.4 0.7 slice.23
  68.0 4.8 %collective-permute-start.7 = (bf16[48,1536]{1,0:T(8,128)(2,1)S(1)}, bf16[48,1536]{1,0:T(8,128)(2,1)S(1)}, u32[]{:S(2)}, u32[]{:S(2)}) collective-permute-start(bf16[48,1536]{1,0:T(8,128)(2,1)S(1)} %slice.22), channel_id=1, source_target_pairs={{128,0},{192,64},{256,128},{320,192},{384,256},{448,320},{0,384},{... | collective-permute-start | bytes 442376 | tf_op jit(solution)/shard_map/ppermute | solution.py:21
  72.8 1.9 %collective-permute-start.8 = (bf16[48,1536]{1,0:T(8,128)(2,1)}, bf16[48,1536]{1,0:T(8,128)(2,1)}, u32[]{:S(2)}, u32[]{:S(2)}) collective-permute-start(bf16[48,1536]{1,0:T(8,128)(2,1)} %slice.23), channel_id=1, source_target_pairs={{384,0},{448,64},{0,128},{64,192},{128,256},{192,320},{256,384},{3... | collective-permute-start | bytes 442376 | tf_op jit(solution)/shard_map/ppermute | solution.py:21
  74.8 7.9 %all-gather.1 = bf16[1024,384]{1,0:T(8,128)(2,1)S(1)} all-gather(bf16[256,384]{1,0:T(8,128)(2,1)} %collective-permute-done.4), channel_id=3, replica_groups=mesh['y_hi'=2,'z'=8,'x_hi'=2,'x_mid'=2,'x_lo'=2,'y_lo'=4,'core'=2] {'x_l..., dimensions={0}, use_global_device_ids=true | all-gather | bytes 983040 | tf_op jit(solution)/shard_map/all_gather | solution.py:101
  82.7 1.2 shard_map.86.refs_6_
  83.9 3.7 %collective-permute-done.7.refs_4_ = bf16[48,1536]{1,0:T(8,128)(2,1)S(1)} collective-permute-done((bf16[48,1536]{1,0:T(8,128)(2,1)S(1)}, bf16[48,1536]{1,0:T(8,128)(2,1)S(1)}, u32[]{:S(2)}, u32[]{:S(2)}) %collective-permute-start.7) | collective-permute-done | bytes 147488 | tf_op jit(solution)/shard_map/ppermute | solution.py:21
  87.6 0.7 copy-done
  88.3 0.9 copy-done.1
  89.2 2.8 %shard_map.87 = bf16[2,768,256]{2,1,0:T(8,128)(2,1)} custom-call(bf16[4,256,384]{2,1,0:T(8,128)(2,1)S(1)} %bitcast.26, bf16[4,256,384]{2,1,0:T(8,128)(2,1)S(1)} %bitcast.28, bf16[96,1536]{1,0:T(8,128)(2,1)} %collective-permute-done.5.refs_2_, bf16[96,1536]{1,0:T(8,128)(2,1)} %collective-permute-done.6.refs_3_, bf16[48,1536]{1,0:T(8,128)(2,1)S(1)} %copy-done.1, ...), custom_call_target="tpu_custom_call" | custom-call | flops 452984832 | bytes 6000000 | tf_op jit(solution)/shard_map/pallas_call | solution.py:63
  92.0 10.7 %all-to-all-start.2 = ((bf16[16,96,256]{2,1,0:T(8,128)(2,1)}), bf16[16,96,256]{2,1,0:T(8,128)(2,1)S(1)}, u32[]{:S(2)}, u32[]{:S(2)}) async-start(bf16[16,96,256]{2,1,0:T(8,128)(2,1)} %bitcast.10), calls=%async_computation.2 | async-start | bytes 1572864 | tf_op jit(solution)/shard_map/all_to_all | solution.py:109
  102.7 1.1 convert_reduce_fusion
  103.9 21.0 %all-to-all-done.2 = bf16[16,96,256]{2,1,0:T(8,128)(2,1)S(1)} async-done(((bf16[16,96,256]{2,1,0:T(8,128)(2,1)}), bf16[16,96,256]{2,1,0:T(8,128)(2,1)S(1)}, u32[]{:S(2)}, u32[]{:S(2)}) %all-to-all-start.2) | async-done | bytes 786464 | tf_op jit(solution)/shard_map/all_to_all | solution.py:109
  124.9 0.1 reduce_sum.21
  125.0 2.6 %collective-permute-start.9 = (bf16[96,256]{1,0:T(8,128)(2,1)S(1)}, bf16[96,256]{1,0:T(8,128)(2,1)S(1)}, u32[]{:S(2)}, u32[]{:S(2)}) collective-permute-start(bf16[96,256]{1,0:T(8,128)(2,1)S(1)} %reduce_sum.21), channel_id=1, source_target_pairs={{0,0},{2,4},{4,28},{6,8},{8,2},{10,6},{12,30},{14,10},{16,24},{18,... | collective-permute-start | bytes 147464 | tf_op jit(solution)/shard_map/ppermute | solution.py:111
  127.7 0.7 reshape_add_fusion
  128.3 9.3 %collective-permute-done.9 = bf16[96,256]{1,0:T(8,128)(2,1)S(1)} collective-permute-done((bf16[96,256]{1,0:T(8,128)(2,1)S(1)}, bf16[96,256]{1,0:T(8,128)(2,1)S(1)}, u32[]{:S(2)}, u32[]{:S(2)}) %collective-permute-start.9) | collective-permute-done | bytes 49184 | tf_op jit(solution)/shard_map/ppermute | solution.py:111
  137.7 0.6 fusion.9
  (27 shorter events, 0.1 us)
Async XLA Ops:
  0.6 3.6 %copy-start.3 = (bf16[256,384]{1,0:T(8,128)(2,1)S(1)}, bf16[256,384]{1,0:T(8,128)(2,1)}, u32[]{:S(2)}) copy-start(bf16[256,384]{1,0:T(8,128)(2,1)} %param.7) | copy-start | bytes 589828
  0.6 3.6 %copy-start.4 = (bf16[256,384]{1,0:T(8,128)(2,1)S(1)}, bf16[256,384]{1,0:T(8,128)(2,1)}, u32[]{:S(2)}) copy-start(bf16[256,384]{1,0:T(8,128)(2,1)} %param.8) | copy-start | bytes 589828
  0.7 10.0 %all-to-all-start = ((bf16[4,96,384]{2,1,0:T(8,128)(2,1)}), bf16[4,96,384]{2,1,0:T(8,128)(2,1)S(1)}, u32[]{:S(2)}, u32[]{:S(2)}) async-start(bf16[4,96,384]{2,1,0:T(8,128)(2,1)} %bitcast.30), calls=%async_computation | async-start | bytes 589824 | tf_op jit(solution)/shard_map/all_to_all | solution.py:82
  4.3 4.5 %copy-start.7 = (s32[1,16]{1,0:T(1,128)S(1)}, s32[1,16]{1,0:T(1,128)}, u32[]{:S(2)}) copy-start(s32[1,16]{1,0:T(1,128)} %param.12) | copy-start | bytes 196
  4.5 41.3 %collective-permute-start.4 = (bf16[256,384]{1,0:T(8,128)(2,1)S(1)}, bf16[256,384]{1,0:T(8,128)(2,1)}, u32[]{:S(2)}, u32[]{:S(2)}) collective-permute-start(bf16[256,384]{1,0:T(8,128)(2,1)S(1)} %fusion.7), channel_id=1, source_target_pairs={{0,512},{512,0},{1,513},{513,1},{2,514},{514,2},{3,515},{515,3},{4... | collective-permute-start | bytes 589832 | tf_op jit(solution)/shard_map/ppermute | solution.py:80
  10.7 33.6 %copy-start.2 = (bf16[1,192,1024]{2,1,0:T(8,128)(2,1)S(1)}, bf16[1,192,1024]{2,1,0:T(8,128)(2,1)}, u32[]{:S(2)}) copy-start(bf16[1,192,1024]{2,1,0:T(8,128)(2,1)} %param.11) | copy-start | bytes 1179652
  10.7 35.1 %collective-permute-start = (bf16[96,1536]{1,0:T(8,128)(2,1)S(1)}, bf16[96,1536]{1,0:T(8,128)(2,1)S(1)}, u32[]{:S(2)}, u32[]{:S(2)}) collective-permute-start(bf16[96,1536]{1,0:T(8,128)(2,1)S(1)} %pad_maximum_fusion.refs_2_), channel_id=1, source_target_pairs={{64,0},{128,64},{192,128},{256,192},{320,256},{384,320},{448,384},... | collective-permute-start | bytes 884744 | tf_op jit(solution)/shard_map/ppermute | solution.py:21
  28.1 17.6 %collective-permute-start.1 = (bf16[96,1536]{1,0:T(8,128)(2,1)S(1)}, bf16[96,1536]{1,0:T(8,128)(2,1)S(1)}, u32[]{:S(2)}, u32[]{:S(2)}) collective-permute-start(bf16[96,1536]{1,0:T(8,128)(2,1)S(1)} %pad_maximum_fusion.refs_2_), channel_id=1, source_target_pairs={{448,0},{0,64},{64,128},{128,192},{192,256},{256,320},{320,384},{3... | collective-permute-start | bytes 884744 | tf_op jit(solution)/shard_map/ppermute | solution.py:21
  30.1 15.7 %collective-permute-start.2 = (bf16[96,1536]{1,0:T(8,128)(2,1)S(1)}, bf16[96,1536]{1,0:T(8,128)(2,1)S(1)}, u32[]{:S(2)}, u32[]{:S(2)}) collective-permute-start(bf16[96,1536]{1,0:T(8,128)(2,1)S(1)} %pad_maximum_fusion.refs_2_), channel_id=1, source_target_pairs={{128,0},{192,64},{256,128},{320,192},{384,256},{448,320},{0,384},{... | collective-permute-start | bytes 884744 | tf_op jit(solution)/shard_map/ppermute | solution.py:21
  33.4 18.5 %collective-permute-start.3 = (bf16[96,1536]{1,0:T(8,128)(2,1)S(1)}, bf16[96,1536]{1,0:T(8,128)(2,1)S(1)}, u32[]{:S(2)}, u32[]{:S(2)}) collective-permute-start(bf16[96,1536]{1,0:T(8,128)(2,1)S(1)} %pad_maximum_fusion.refs_2_), channel_id=1, source_target_pairs={{384,0},{448,64},{0,128},{64,192},{128,256},{192,320},{256,384},{3... | collective-permute-start | bytes 884744 | tf_op jit(solution)/shard_map/ppermute | solution.py:21
  51.9 36.4 %all-to-all-start.1 = ((bf16[16,12,1024]{2,1,0:T(8,128)(2,1)}), bf16[16,12,1024]{2,1,0:T(8,128)(2,1)}, u32[]{:S(2)}, u32[]{:S(2)}) async-start(bf16[16,12,1024]{2,1,0:T(8,128)(2,1)} %gather_fusion), calls=%async_computation.1 | async-start | bytes 1048576 | tf_op jit(solution)/shard_map/all_to_all | solution.py:102
  60.8 27.5 %collective-permute-start.5 = (bf16[96,1536]{1,0:T(8,128)(2,1)S(1)}, bf16[96,1536]{1,0:T(8,128)(2,1)}, u32[]{:S(2)}, u32[]{:S(2)}) collective-permute-start(bf16[96,1536]{1,0:T(8,128)(2,1)S(1)} %collective-permute-done.2.refs_5_), channel_id=1, source_target_pairs={{64,0},{128,64},{192,128},{256,192},{320,256},{384,320},{448,384},... | collective-permute-start | bytes 884744 | tf_op jit(solution)/shard_map/ppermute | solution.py:21
  65.4 22.9 %collective-permute-start.6 = (bf16[96,1536]{1,0:T(8,128)(2,1)S(1)}, bf16[96,1536]{1,0:T(8,128)(2,1)}, u32[]{:S(2)}, u32[]{:S(2)}) collective-permute-start(bf16[96,1536]{1,0:T(8,128)(2,1)S(1)} %collective-permute-done.3.refs_6_), channel_id=1, source_target_pairs={{448,0},{0,64},{64,128},{128,192},{192,256},{256,320},{320,384},{3... | collective-permute-start | bytes 884744 | tf_op jit(solution)/shard_map/ppermute | solution.py:21
  68.0 19.6 %collective-permute-start.7 = (bf16[48,1536]{1,0:T(8,128)(2,1)S(1)}, bf16[48,1536]{1,0:T(8,128)(2,1)S(1)}, u32[]{:S(2)}, u32[]{:S(2)}) collective-permute-start(bf16[48,1536]{1,0:T(8,128)(2,1)S(1)} %slice.22), channel_id=1, source_target_pairs={{128,0},{192,64},{256,128},{320,192},{384,256},{448,320},{0,384},{... | collective-permute-start | bytes 442376 | tf_op jit(solution)/shard_map/ppermute | solution.py:21
  72.8 15.5 %collective-permute-start.8 = (bf16[48,1536]{1,0:T(8,128)(2,1)}, bf16[48,1536]{1,0:T(8,128)(2,1)}, u32[]{:S(2)}, u32[]{:S(2)}) collective-permute-start(bf16[48,1536]{1,0:T(8,128)(2,1)} %slice.23), channel_id=1, source_target_pairs={{384,0},{448,64},{0,128},{64,192},{128,256},{192,320},{256,384},{3... | collective-permute-start | bytes 442376 | tf_op jit(solution)/shard_map/ppermute | solution.py:21
  87.6 0.7 copy-start
  88.3 0.9 copy-start.1
  92.0 32.8 %all-to-all-start.2 = ((bf16[16,96,256]{2,1,0:T(8,128)(2,1)}), bf16[16,96,256]{2,1,0:T(8,128)(2,1)S(1)}, u32[]{:S(2)}, u32[]{:S(2)}) async-start(bf16[16,96,256]{2,1,0:T(8,128)(2,1)} %bitcast.10), calls=%async_computation.2 | async-start | bytes 1572864 | tf_op jit(solution)/shard_map/all_to_all | solution.py:109
  103.8 23.8 %copy-start.5 = (f32[1,1,12,1024]{3,1,2,0:T(1,128)S(1)}, f32[1,1,12,1024]{3,1,2,0:T(1,128)}, u32[]{:S(2)}) copy-start(f32[1,1,12,1024]{3,1,2,0:T(1,128)} %param.13) | copy-start | bytes 147460
  125.0 12.7 %copy-start.6 = (bf16[256,96]{0,1:T(8,128)(2,1)S(1)}, bf16[256,96]{0,1:T(8,128)(2,1)}, u32[]{:S(2)}) copy-start(bf16[256,96]{0,1:T(8,128)(2,1)} %param.10) | copy-start | bytes 147460
  125.0 12.7 %collective-permute-start.9 = (bf16[96,256]{1,0:T(8,128)(2,1)S(1)}, bf16[96,256]{1,0:T(8,128)(2,1)S(1)}, u32[]{:S(2)}, u32[]{:S(2)}) collective-permute-start(bf16[96,256]{1,0:T(8,128)(2,1)S(1)} %reduce_sum.21), channel_id=1, source_target_pairs={{0,0},{2,4},{4,28},{6,8},{8,2},{10,6},{12,30},{14,10},{16,24},{18,... | collective-permute-start | bytes 147464 | tf_op jit(solution)/shard_map/ppermute | solution.py:111

commit v7 on v6

--- a/solution.py
+++ b/solution.py
@@ -38,38 +38,38 @@
     return jnp.concatenate([parts[i] for i in range(parts.shape[0])], axis=-1)
 
 
-def products(own, far, pieces, feats, before=None):
-    sources, tokens, hidden = own.shape
+def products(own, far, pieces, x_lo):
+    cores, places, tokens, hidden = own.shape
     rows = sum(piece.shape[0] for piece in pieces)
-    done = 0 if before is None else before.shape[1]
 
-    def kernel(*refs):
-        own_ref, far_ref, out_ref = refs[0], refs[1], refs[-1]
-        piece_refs = refs[2 : 2 + len(pieces)]
+    def kernel(x_ref, own_ref, far_ref, *refs):
+        piece_refs, out_ref = refs[:-1], refs[-1]
+        here = x_ref[0]
         for slot, grads_ref in enumerate((own_ref, far_ref)):
             total = None
-            for source in range(sources):
-                columns = slice(source * hidden, (source + 1) * hidden)
-                weight = jnp.concatenate([ref[:, columns] for ref in piece_refs], axis=0)
-                term = lax.dot_general(
-                    weight, grads_ref[source], (((1,), (1,)), ((), ())), preferred_element_type=jnp.float32
-                )
-                total = term if total is None else total + term
-            if before is not None:
-                out_ref[slot, :done] = refs[2 + len(pieces)][slot]
-            out_ref[slot, done:] = total.astype(jnp.bfloat16)
+            for place in range(places):
+                at = here if place == 0 else 1 - here
+                for core in range(cores):
+                    source = place * cores + core
+                    columns = slice(source * hidden, (source + 1) * hidden)
+                    weight = jnp.concatenate([ref[:, columns] for ref in piece_refs], axis=0)
+                    term = lax.dot_general(
+                        weight, grads_ref[core, at], (((1,), (1,)), ((), ())), preferred_element_type=jnp.float32
+                    )
+                    total = term if total is None else total + term
+            out_ref[slot] = total.astype(jnp.bfloat16)
 
-    operands = [own, far, *pieces] + ([] if before is None else [before])
+    in_vmem = pl.BlockSpec(memory_space=pltpu.VMEM)
     return pl.pallas_call(
         kernel,
-        out_shape=jax.ShapeDtypeStruct((2, done + rows, tokens), jnp.bfloat16),
-        in_specs=[pl.BlockSpec(memory_space=pltpu.VMEM)] * len(operands),
-        out_specs=pl.BlockSpec(memory_space=pltpu.VMEM),
+        out_shape=jax.ShapeDtypeStruct((2, rows, tokens), jnp.bfloat16),
+        in_specs=[pl.BlockSpec(memory_space=pltpu.SMEM)] + [in_vmem] * (2 + len(pieces)),
+        out_specs=in_vmem,
         compiler_params=pltpu.CompilerParams(vmem_limit_bytes=32 * 1024 * 1024),
         cost_estimate=pl.CostEstimate(
-            flops=4 * rows * tokens * sources * hidden, bytes_accessed=6000000, transcendentals=0
+            flops=4 * rows * tokens * cores * places * hidden, bytes_accessed=6000000, transcendentals=0
         ),
-    )(*operands)
+    )(x_lo.reshape(1).astype(jnp.int32), own, far, *pieces)
 
 
 def on_device(pre_act, act_grad, up_weight, resid_grad, gram_parts, stripe_order, gram_prev):
@@ -78,6 +78,7 @@
 
     hidden_grad = (act_grad.astype(jnp.float32) * gelu_slope(pre_act.astype(jnp.float32))).astype(jnp.bfloat16)
     far_grad = lax.ppermute(hidden_grad, "y_hi", SWAP)
+    beside_grad = lax.ppermute(hidden_grad, "x_lo", SWAP)
 
     quarters = lax.all_to_all(up_weight.reshape(4, feats, hidden), QUAD, 0, 0, tiled=True)
     mine = beside(quarters)
@@ -85,27 +86,28 @@
     ring = {0: mine}
     for step in (2, 6, 1, 7):
         ring[step] = from_z(mine, step)
-    own = lax.all_gather(hidden_grad, QUAD, axis=0)
-    own, parts = lax.optimization_barrier((own, gram_parts[0]))
+    own = lax.all_gather(jnp.stack([hidden_grad, beside_grad]), "core", axis=0)
+    own, parts, far_grad = lax.optimization_barrier((own, gram_parts[0], far_grad))
+    far_pair = jnp.stack([far_grad, lax.ppermute(far_grad, "x_lo", SWAP)])
     stripes = parts.reshape(lax.axis_size(("y_hi", "z")), -1, parts.shape[1])
     ordered = stripes[stripe_order[0]]
 
-    *first, far_grad, own, ordered = lax.optimization_barrier(
-        (ring[1], ring[7], ring[2], ring[6], far_grad, own, ordered)
+    *first, far_pair, own, ordered = lax.optimization_barrier(
+        (ring[1], ring[7], ring[2], ring[6], far_pair, own, ordered)
     )
     ring[1], ring[7], ring[2], ring[6] = first
     ring[3] = from_z(ring[2], 1)
     ring[5] = from_z(ring[6], 7)
     mid = feats // 2
     upper, lower = from_z(ring[2][:mid], 2), from_z(ring[6][mid:], 6)
-    far = lax.all_gather(far_grad, QUAD, axis=0)
+    far = lax.all_gather(far_pair, "core", axis=0)
+
     kept = lax.all_to_all(ordered, ("y_hi", "z"), 0, 0, tiled=True)
-
-    near = products(own, far, [ring[step] for step in ORDER[:5]], feats)
     upper, kept = lax.optimization_barrier((upper, kept))
     gram_stats = gram_prev + jnp.sum(kept.astype(jnp.float32), axis=0).reshape(gram_prev.shape)
-    blocks = products(own, far, [ring[3], ring[5], upper, lower], feats, near)
-    blocks = blocks.reshape(-1, feats, tokens)
+
+    pieces = [ring[step] for step in ORDER[:-1]] + [upper, lower]
+    blocks = products(own, far, pieces, lax.axis_index("x_lo")).reshape(-1, feats, tokens)
     arrived = lax.all_to_all(blocks, ("x_hi", "x_mid", "y_lo"), 0, 0, tiled=True)
     shared = jnp.sum(arrived.astype(jnp.float32), axis=0).astype(jnp.bfloat16)
     home = lax.ppermute(shared, WHERE, last_hop())

time: 140 us -> 142 us (1.014)
  the two profiles are of different devices: /device:TPU:112 before, /device:TPU:64 now
where the time goes in v7:
time: 142 us; the launch traced here: 141 us
  starting transfers between devices  74.8 us (53%)
  waiting for transfers between devices  47.9 us (34%)
  blocking collectives  5.08 us (4%)
  other arithmetic  4.56 us (3%)
  local copies, waits for them, and re-layouts  3.79 us (3%)
  Pallas kernels  3.66 us (3%)
    ppermute x8, starting transfers between devices, from_z(): return lax.ppermute(value, 'z', [((i + step) % 8, i) for i in range(8)])  29.5 us
    all_to_all x1, waiting for transfers between devices, on_device(): lax.all_to_all(blocks, ('x_hi', 'x_mid', 'y_lo'), 0, 0, tiled=True)  21.7 us
    ppermute x1, starting transfers between devices, on_device(): far_grad = lax.ppermute(hidden_grad, 'y_hi', SWAP)  14.2 us
    ppermute x1, waiting for transfers between devices, on_device(): home = lax.ppermute(shared, WHERE, last_hop())  11.5 us
    all_to_all x1, starting transfers between devices, on_device(): lax.all_to_all(blocks, ('x_hi', 'x_mid', 'y_lo'), 0, 0, tiled=True)  10.3 us
    ppermute x8, waiting for transfers between devices, from_z(): return lax.ppermute(value, 'z', [((i + step) % 8, i) for i in range(8)])  9.07 us
    all_to_all x1, starting transfers between devices, on_device(): kept = lax.all_to_all(ordered, ('y_hi', 'z'), 0, 0, tiled=True)  8.63 us
    ppermute x1, waiting for transfers between devices, on_device(): far_pair = jnp.stack([far_grad, lax.ppermute(far_grad, 'x_lo', SWAP)])  5.55 us
  transfers between devices with their start and end apart: 15, of which 5 were waited for; matrix products, arithmetic and copies ran while one was open for 4% of the time, Pallas kernels for 0%

profile of v7, /device:TPU:64, one launch (start us, length us, event | category | flops | bytes accessed | tf_op | source)
XLA Modules:
  0.0 140.7 jit_solution(17870900964737986450)
XLA Ops:
  0.6 3.6 %all-to-all-start = ((bf16[4,96,384]{2,1,0:T(8,128)(2,1)}), bf16[4,96,384]{2,1,0:T(8,128)(2,1)S(1)}, u32[]{:S(2)}, u32[]{:S(2)}) async-start(bf16[4,96,384]{2,1,0:T(8,128)(2,1)} %bitcast.34), calls=%async_computation | async-start | bytes 589824 | tf_op jit(solution)/shard_map/all_to_all | solution.py:83
  4.3 0.2 fusion.7
  4.5 14.2 %collective-permute-start.5 = (bf16[256,384]{1,0:T(8,128)(2,1)S(1)}, bf16[256,384]{1,0:T(8,128)(2,1)}, u32[]{:S(2)}, u32[]{:S(2)}) collective-permute-start(bf16[256,384]{1,0:T(8,128)(2,1)S(1)} %fusion.7), channel_id=1, source_target_pairs={{0,512},{512,0},{1,513},{513,1},{2,514},{514,2},{3,515},{515,3},{4... | collective-permute-start | bytes 589832 | tf_op jit(solution)/shard_map/ppermute | solution.py:80
  18.7 3.9 %collective-permute-start.4 = (bf16[256,384]{1,0:T(8,128)(2,1)S(1)}, bf16[256,384]{1,0:T(8,128)(2,1)S(1)}, u32[]{:S(2)}, u32[]{:S(2)}) collective-permute-start(bf16[256,384]{1,0:T(8,128)(2,1)S(1)} %fusion.7), channel_id=1, source_target_pairs={{0,8},{8,0},{1,9},{9,1},{2,10},{10,2},{3,11},{11,3},{4,12},{12,4},... | collective-permute-start | bytes 589832 | tf_op jit(solution)/shard_map/ppermute | solution.py:81
  22.7 1.9 %collective-permute-start.3 = (bf16[96,1536]{1,0:T(8,128)(2,1)S(1)}, bf16[96,1536]{1,0:T(8,128)(2,1)S(1)}, u32[]{:S(2)}, u32[]{:S(2)}) collective-permute-start(bf16[96,1536]{1,0:T(8,128)(2,1)S(1)} %pad_maximum_fusion.2.refs_0_), channel_id=1, source_target_pairs={{384,0},{448,64},{0,128},{64,192},{128,256},{192,320},{256,384},{3... | collective-permute-start | bytes 884744 | tf_op jit(solution)/shard_map/ppermute | solution.py:21
  24.6 6.0 %collective-permute-start.2 = (bf16[96,1536]{1,0:T(8,128)(2,1)S(1)}, bf16[96,1536]{1,0:T(8,128)(2,1)S(1)}, u32[]{:S(2)}, u32[]{:S(2)}) collective-permute-start(bf16[96,1536]{1,0:T(8,128)(2,1)S(1)} %pad_maximum_fusion.2.refs_0_), channel_id=1, source_target_pairs={{128,0},{192,64},{256,128},{320,192},{384,256},{448,320},{0,384},{... | collective-permute-start | bytes 884744 | tf_op jit(solution)/shard_map/ppermute | solution.py:21
  30.6 2.7 %collective-permute-start.1 = (bf16[96,1536]{1,0:T(8,128)(2,1)S(1)}, bf16[96,1536]{1,0:T(8,128)(2,1)S(1)}, u32[]{:S(2)}, u32[]{:S(2)}) collective-permute-start(bf16[96,1536]{1,0:T(8,128)(2,1)S(1)} %pad_maximum_fusion.2.refs_0_), channel_id=1, source_target_pairs={{448,0},{0,64},{64,128},{128,192},{192,256},{256,320},{320,384},{3... | collective-permute-start | bytes 884744 | tf_op jit(solution)/shard_map/ppermute | solution.py:21
  33.3 4.4 %collective-permute-start = (bf16[96,1536]{1,0:T(8,128)(2,1)S(1)}, bf16[96,1536]{1,0:T(8,128)(2,1)S(1)}, u32[]{:S(2)}, u32[]{:S(2)}) collective-permute-start(bf16[96,1536]{1,0:T(8,128)(2,1)S(1)} %pad_maximum_fusion.2.refs_0_), channel_id=1, source_target_pairs={{64,0},{128,64},{192,128},{256,192},{320,256},{384,320},{448,384},... | collective-permute-start | bytes 884744 | tf_op jit(solution)/shard_map/ppermute | solution.py:21
  37.8 2.5 %all-gather = bf16[4,256,384]{2,1,0:T(8,128)(2,1)S(1)} all-gather(bf16[2,256,384]{2,1,0:T(8,128)(2,1)S(1)} %pad_maximum_fusion), channel_id=2, replica_groups=mesh['y_hi'=2,'z'=8,'x_hi'=2,'x_mid'=2,'x_lo'=2,'y_lo'=4,'core'=2] {'core'}, dimensions={0}, use_global_device_ids=true | all-gather | bytes 1179648 | tf_op jit(solution)/shard_map/all_gather | solution.py:89
  40.3 2.1 %collective-permute-start.6 = (bf16[256,384]{1,0:T(8,128)(2,1)}, bf16[256,384]{1,0:T(8,128)(2,1)S(1)}, u32[]{:S(2)}, u32[]{:S(2)}) collective-permute-start(bf16[256,384]{1,0:T(8,128)(2,1)} %collective-permute-done.5), channel_id=1, source_target_pairs={{0,8},{8,0},{1,9},{9,1},{2,10},{10,2},{3,11},{11,3},{4,12},{12,4},... | collective-permute-start | bytes 589832 | tf_op jit(solution)/shard_map/ppermute | solution.py:91
  42.5 1.4 gather_fusion
  43.9 5.5 %collective-permute-done.6 = bf16[256,384]{1,0:T(8,128)(2,1)S(1)} collective-permute-done((bf16[256,384]{1,0:T(8,128)(2,1)}, bf16[256,384]{1,0:T(8,128)(2,1)S(1)}, u32[]{:S(2)}, u32[]{:S(2)}) %collective-permute-start.6) | collective-permute-done | bytes 196640 | tf_op jit(solution)/shard_map/ppermute | solution.py:91
  49.5 1.7 %pad_maximum_fusion.1 = bf16[2,256,384]{2,1,0:T(8,128)(2,1)} fusion(bf16[1,256,384]{2,1,0:T(8,128)(2,1)S(1)} %bitcast.36, bf16[1,256,384]{2,1,0:T(8,128)(2,1)} %bitcast.10), kind=kLoop, calls=%fused_computation.14 | loop fusion | flops 196608 | bytes 786432 | tf_op jit(solution)/shard_map/stack | solution.py:91
  51.2 8.6 %all-to-all-start.1 = ((bf16[16,12,1024]{2,1,0:T(8,128)(2,1)}), bf16[16,12,1024]{2,1,0:T(8,128)(2,1)}, u32[]{:S(2)}, u32[]{:S(2)}) async-start(bf16[16,12,1024]{2,1,0:T(8,128)(2,1)} %gather_fusion), calls=%async_computation.1 | async-start | bytes 1048576 | tf_op jit(solution)/shard_map/all_to_all | solution.py:105
  59.8 4.6 %collective-permute-start.7 = (bf16[96,1536]{1,0:T(8,128)(2,1)S(1)}, bf16[96,1536]{1,0:T(8,128)(2,1)S(1)}, u32[]{:S(2)}, u32[]{:S(2)}) collective-permute-start(bf16[96,1536]{1,0:T(8,128)(2,1)S(1)} %collective-permute-done.2.refs_3_), channel_id=1, source_target_pairs={{64,0},{128,64},{192,128},{256,192},{320,256},{384,320},{448,384},... | collective-permute-start | bytes 884744 | tf_op jit(solution)/shard_map/ppermute | solution.py:21
  64.5 1.9 %collective-permute-start.8 = (bf16[96,1536]{1,0:T(8,128)(2,1)S(1)}, bf16[96,1536]{1,0:T(8,128)(2,1)}, u32[]{:S(2)}, u32[]{:S(2)}) collective-permute-start(bf16[96,1536]{1,0:T(8,128)(2,1)S(1)} %collective-permute-done.3.refs_4_), channel_id=1, source_target_pairs={{448,0},{0,64},{64,128},{128,192},{192,256},{256,320},{320,384},{3... | collective-permute-start | bytes 884744 | tf_op jit(solution)/shard_map/ppermute | solution.py:21
  66.4 0.7 slice.23
  67.1 3.6 %collective-permute-start.10 = (bf16[48,1536]{1,0:T(8,128)(2,1)}, bf16[48,1536]{1,0:T(8,128)(2,1)S(1)}, u32[]{:S(2)}, u32[]{:S(2)}) collective-permute-start(bf16[48,1536]{1,0:T(8,128)(2,1)} %slice.23), channel_id=1, source_target_pairs={{384,0},{448,64},{0,128},{64,192},{128,256},{192,320},{256,384},{3... | collective-permute-start | bytes 442376 | tf_op jit(solution)/shard_map/ppermute | solution.py:21
  70.6 4.4 %collective-permute-start.9 = (bf16[48,1536]{1,0:T(8,128)(2,1)S(1)}, bf16[48,1536]{1,0:T(8,128)(2,1)S(1)}, u32[]{:S(2)}, u32[]{:S(2)}) collective-permute-start(bf16[48,1536]{1,0:T(8,128)(2,1)S(1)} %slice.22), channel_id=1, source_target_pairs={{128,0},{192,64},{256,128},{320,192},{384,256},{448,320},{0,384},{... | collective-permute-start | bytes 442376 | tf_op jit(solution)/shard_map/ppermute | solution.py:21
  75.0 2.6 %all-gather.1 = bf16[4,256,384]{2,1,0:T(8,128)(2,1)S(1)} all-gather(bf16[2,256,384]{2,1,0:T(8,128)(2,1)} %pad_maximum_fusion.1), channel_id=3, replica_groups=mesh['y_hi'=2,'z'=8,'x_hi'=2,'x_mid'=2,'x_lo'=2,'y_lo'=4,'core'=2] {'core'}, dimensions={0}, use_global_device_ids=true | all-gather | bytes 1179648 | tf_op jit(solution)/shard_map/all_gather | solution.py:103
  77.6 8.6 %collective-permute-done.9.refs_7_ = bf16[48,1536]{1,0:T(8,128)(2,1)S(1)} collective-permute-done((bf16[48,1536]{1,0:T(8,128)(2,1)S(1)}, bf16[48,1536]{1,0:T(8,128)(2,1)S(1)}, u32[]{:S(2)}, u32[]{:S(2)}) %collective-permute-start.9) | collective-permute-done | bytes 147488 | tf_op jit(solution)/shard_map/ppermute | solution.py:21
  86.2 0.7 copy-done
  86.9 0.4 collective-permute-done.10.refs_8_
  87.3 0.9 copy-done.1
  88.2 3.7 %shard_map.86 = bf16[2,768,256]{2,1,0:T(8,128)(2,1)} custom-call(s32[1]{0:T(128)} %bitcast.x_ref, bf16[2,2,256,384]{3,2,1,0:T(8,128)(2,1)S(1)} %bitcast.30, bf16[2,2,256,384]{3,2,1,0:T(8,128)(2,1)S(1)} %bitcast.31, bf16[96,1536]{1,0:T(8,128)(2,1)S(1)} %pad_maximum_fusion.2.refs_0_, bf16[96,1536]{1,0:T(8,128)(2,1)S(1)} %collective-permute-done.refs_1_, ...), custom_call_target="tpu_custom_call" | custom-call | flops 1207959552 | bytes 6000000 | tf_op jit(solution)/shard_map/pallas_call | solution.py:63
  91.9 10.3 %all-to-all-start.2 = ((bf16[16,96,256]{2,1,0:T(8,128)(2,1)}), bf16[16,96,256]{2,1,0:T(8,128)(2,1)S(1)}, u32[]{:S(2)}, u32[]{:S(2)}) async-start(bf16[16,96,256]{2,1,0:T(8,128)(2,1)} %bitcast.15), calls=%async_computation.2 | async-start | bytes 1572864 | tf_op jit(solution)/shard_map/all_to_all | solution.py:111
  102.2 1.1 convert_reduce_fusion
  103.4 21.7 %all-to-all-done.2 = bf16[16,96,256]{2,1,0:T(8,128)(2,1)S(1)} async-done(((bf16[16,96,256]{2,1,0:T(8,128)(2,1)}), bf16[16,96,256]{2,1,0:T(8,128)(2,1)S(1)}, u32[]{:S(2)}, u32[]{:S(2)}) %all-to-all-start.2) | async-done | bytes 786464 | tf_op jit(solution)/shard_map/all_to_all | solution.py:111
  125.2 2.6 %collective-permute-start.11 = (bf16[96,256]{1,0:T(8,128)(2,1)S(1)}, bf16[96,256]{1,0:T(8,128)(2,1)S(1)}, u32[]{:S(2)}, u32[]{:S(2)}) collective-permute-start(bf16[96,256]{1,0:T(8,128)(2,1)S(1)} %reduce_sum.21), channel_id=1, source_target_pairs={{0,0},{2,4},{4,28},{6,8},{8,2},{10,6},{12,30},{14,10},{16,24},{18,... | collective-permute-start | bytes 147464 | tf_op jit(solution)/shard_map/ppermute | solution.py:113
  127.9 0.7 reshape_add_fusion
  128.6 11.5 %collective-permute-done.11 = bf16[96,256]{1,0:T(8,128)(2,1)S(1)} collective-permute-done((bf16[96,256]{1,0:T(8,128)(2,1)S(1)}, bf16[96,256]{1,0:T(8,128)(2,1)S(1)}, u32[]{:S(2)}, u32[]{:S(2)}) %collective-permute-start.11) | collective-permute-done | bytes 49184 | tf_op jit(solution)/shard_map/ppermute | solution.py:113
  140.1 0.6 fusion.9
  (32 shorter events, 0.4 us)
Async XLA Ops:
  0.6 3.6 %copy-start.3 = (bf16[256,384]{1,0:T(8,128)(2,1)S(1)}, bf16[256,384]{1,0:T(8,128)(2,1)}, u32[]{:S(2)}) copy-start(bf16[256,384]{1,0:T(8,128)(2,1)} %param.7) | copy-start | bytes 589828
  0.6 3.6 %copy-start.4 = (bf16[256,384]{1,0:T(8,128)(2,1)S(1)}, bf16[256,384]{1,0:T(8,128)(2,1)}, u32[]{:S(2)}) copy-start(bf16[256,384]{1,0:T(8,128)(2,1)} %param.8) | copy-start | bytes 589828
  0.6 21.9 %all-to-all-start = ((bf16[4,96,384]{2,1,0:T(8,128)(2,1)}), bf16[4,96,384]{2,1,0:T(8,128)(2,1)S(1)}, u32[]{:S(2)}, u32[]{:S(2)}) async-start(bf16[4,96,384]{2,1,0:T(8,128)(2,1)} %bitcast.34), calls=%async_computation | async-start | bytes 589824 | tf_op jit(solution)/shard_map/all_to_all | solution.py:83
  4.5 35.8 %collective-permute-start.5 = (bf16[256,384]{1,0:T(8,128)(2,1)S(1)}, bf16[256,384]{1,0:T(8,128)(2,1)}, u32[]{:S(2)}, u32[]{:S(2)}) collective-permute-start(bf16[256,384]{1,0:T(8,128)(2,1)S(1)} %fusion.7), channel_id=1, source_target_pairs={{0,512},{512,0},{1,513},{513,1},{2,514},{514,2},{3,515},{515,3},{4... | collective-permute-start | bytes 589832 | tf_op jit(solution)/shard_map/ppermute | solution.py:80
  18.7 14.6 %collective-permute-start.4 = (bf16[256,384]{1,0:T(8,128)(2,1)S(1)}, bf16[256,384]{1,0:T(8,128)(2,1)S(1)}, u32[]{:S(2)}, u32[]{:S(2)}) collective-permute-start(bf16[256,384]{1,0:T(8,128)(2,1)S(1)} %fusion.7), channel_id=1, source_target_pairs={{0,8},{8,0},{1,9},{9,1},{2,10},{10,2},{3,11},{11,3},{4,12},{12,4},... | collective-permute-start | bytes 589832 | tf_op jit(solution)/shard_map/ppermute | solution.py:81
  22.7 28.5 %collective-permute-start.3 = (bf16[96,1536]{1,0:T(8,128)(2,1)S(1)}, bf16[96,1536]{1,0:T(8,128)(2,1)S(1)}, u32[]{:S(2)}, u32[]{:S(2)}) collective-permute-start(bf16[96,1536]{1,0:T(8,128)(2,1)S(1)} %pad_maximum_fusion.2.refs_0_), channel_id=1, source_target_pairs={{384,0},{448,64},{0,128},{64,192},{128,256},{192,320},{256,384},{3... | collective-permute-start | bytes 884744 | tf_op jit(solution)/shard_map/ppermute | solution.py:21
  24.6 26.6 %collective-permute-start.2 = (bf16[96,1536]{1,0:T(8,128)(2,1)S(1)}, bf16[96,1536]{1,0:T(8,128)(2,1)S(1)}, u32[]{:S(2)}, u32[]{:S(2)}) collective-permute-start(bf16[96,1536]{1,0:T(8,128)(2,1)S(1)} %pad_maximum_fusion.2.refs_0_), channel_id=1, source_target_pairs={{128,0},{192,64},{256,128},{320,192},{384,256},{448,320},{0,384},{... | collective-permute-start | bytes 884744 | tf_op jit(solution)/shard_map/ppermute | solution.py:21
  30.6 20.6 %collective-permute-start.1 = (bf16[96,1536]{1,0:T(8,128)(2,1)S(1)}, bf16[96,1536]{1,0:T(8,128)(2,1)S(1)}, u32[]{:S(2)}, u32[]{:S(2)}) collective-permute-start(bf16[96,1536]{1,0:T(8,128)(2,1)S(1)} %pad_maximum_fusion.2.refs_0_), channel_id=1, source_target_pairs={{448,0},{0,64},{64,128},{128,192},{192,256},{256,320},{320,384},{3... | collective-permute-start | bytes 884744 | tf_op jit(solution)/shard_map/ppermute | solution.py:21
  33.3 17.9 %collective-permute-start = (bf16[96,1536]{1,0:T(8,128)(2,1)S(1)}, bf16[96,1536]{1,0:T(8,128)(2,1)S(1)}, u32[]{:S(2)}, u32[]{:S(2)}) collective-permute-start(bf16[96,1536]{1,0:T(8,128)(2,1)S(1)} %pad_maximum_fusion.2.refs_0_), channel_id=1, source_target_pairs={{64,0},{128,64},{192,128},{256,192},{320,256},{384,320},{448,384},... | collective-permute-start | bytes 884744 | tf_op jit(solution)/shard_map/ppermute | solution.py:21
  37.8 4.7 %copy-start.2 = (bf16[1,192,1024]{2,1,0:T(8,128)(2,1)S(1)}, bf16[1,192,1024]{2,1,0:T(8,128)(2,1)}, u32[]{:S(2)}) copy-start(bf16[1,192,1024]{2,1,0:T(8,128)(2,1)} %param.11) | copy-start | bytes 1179652
  40.3 2.1 %copy-start.7 = (s32[1,16]{1,0:T(1,128)S(1)}, s32[1,16]{1,0:T(1,128)}, u32[]{:S(2)}) copy-start(s32[1,16]{1,0:T(1,128)} %param.12) | copy-start | bytes 196
  40.3 9.2 %collective-permute-start.6 = (bf16[256,384]{1,0:T(8,128)(2,1)}, bf16[256,384]{1,0:T(8,128)(2,1)S(1)}, u32[]{:S(2)}, u32[]{:S(2)}) collective-permute-start(bf16[256,384]{1,0:T(8,128)(2,1)} %collective-permute-done.5), channel_id=1, source_target_pairs={{0,8},{8,0},{1,9},{9,1},{2,10},{10,2},{3,11},{11,3},{4,12},{12,4},... | collective-permute-start | bytes 589832 | tf_op jit(solution)/shard_map/ppermute | solution.py:91
  51.2 35.7 %all-to-all-start.1 = ((bf16[16,12,1024]{2,1,0:T(8,128)(2,1)}), bf16[16,12,1024]{2,1,0:T(8,128)(2,1)}, u32[]{:S(2)}, u32[]{:S(2)}) async-start(bf16[16,12,1024]{2,1,0:T(8,128)(2,1)} %gather_fusion), calls=%async_computation.1 | async-start | bytes 1048576 | tf_op jit(solution)/shard_map/all_to_all | solution.py:105
  59.8 27.5 %collective-permute-start.7 = (bf16[96,1536]{1,0:T(8,128)(2,1)S(1)}, bf16[96,1536]{1,0:T(8,128)(2,1)S(1)}, u32[]{:S(2)}, u32[]{:S(2)}) collective-permute-start(bf16[96,1536]{1,0:T(8,128)(2,1)S(1)} %collective-permute-done.2.refs_3_), channel_id=1, source_target_pairs={{64,0},{128,64},{192,128},{256,192},{320,256},{384,320},{448,384},... | collective-permute-start | bytes 884744 | tf_op jit(solution)/shard_map/ppermute | solution.py:21
  64.5 22.9 %collective-permute-start.8 = (bf16[96,1536]{1,0:T(8,128)(2,1)S(1)}, bf16[96,1536]{1,0:T(8,128)(2,1)}, u32[]{:S(2)}, u32[]{:S(2)}) collective-permute-start(bf16[96,1536]{1,0:T(8,128)(2,1)S(1)} %collective-permute-done.3.refs_4_), channel_id=1, source_target_pairs={{448,0},{0,64},{64,128},{128,192},{192,256},{256,320},{320,384},{3... | collective-permute-start | bytes 884744 | tf_op jit(solution)/shard_map/ppermute | solution.py:21
  67.1 20.3 %collective-permute-start.10 = (bf16[48,1536]{1,0:T(8,128)(2,1)}, bf16[48,1536]{1,0:T(8,128)(2,1)S(1)}, u32[]{:S(2)}, u32[]{:S(2)}) collective-permute-start(bf16[48,1536]{1,0:T(8,128)(2,1)} %slice.23), channel_id=1, source_target_pairs={{384,0},{448,64},{0,128},{64,192},{128,256},{192,320},{256,384},{3... | collective-permute-start | bytes 442376 | tf_op jit(solution)/shard_map/ppermute | solution.py:21
  70.6 15.6 %collective-permute-start.9 = (bf16[48,1536]{1,0:T(8,128)(2,1)S(1)}, bf16[48,1536]{1,0:T(8,128)(2,1)S(1)}, u32[]{:S(2)}, u32[]{:S(2)}) collective-permute-start(bf16[48,1536]{1,0:T(8,128)(2,1)S(1)} %slice.22), channel_id=1, source_target_pairs={{128,0},{192,64},{256,128},{320,192},{384,256},{448,320},{0,384},{... | collective-permute-start | bytes 442376 | tf_op jit(solution)/shard_map/ppermute | solution.py:21
  86.2 0.7 copy-start
  87.3 0.9 copy-start.1
  91.9 33.2 %all-to-all-start.2 = ((bf16[16,96,256]{2,1,0:T(8,128)(2,1)}), bf16[16,96,256]{2,1,0:T(8,128)(2,1)S(1)}, u32[]{:S(2)}, u32[]{:S(2)}) async-start(bf16[16,96,256]{2,1,0:T(8,128)(2,1)} %bitcast.15), calls=%async_computation.2 | async-start | bytes 1572864 | tf_op jit(solution)/shard_map/all_to_all | solution.py:111
  103.4 24.5 %copy-start.5 = (f32[1,1,12,1024]{3,1,2,0:T(1,128)S(1)}, f32[1,1,12,1024]{3,1,2,0:T(1,128)}, u32[]{:S(2)}) copy-start(f32[1,1,12,1024]{3,1,2,0:T(1,128)} %param.13) | copy-start | bytes 147460
  125.2 14.8 %copy-start.6 = (bf16[256,96]{0,1:T(8,128)(2,1)S(1)}, bf16[256,96]{0,1:T(8,128)(2,1)}, u32[]{:S(2)}) copy-start(bf16[256,96]{0,1:T(8,128)(2,1)} %param.10) | copy-start | bytes 147460
  125.2 14.8 %collective-permute-start.11 = (bf16[96,256]{1,0:T(8,128)(2,1)S(1)}, bf16[96,256]{1,0:T(8,128)(2,1)S(1)}, u32[]{:S(2)}, u32[]{:S(2)}) collective-permute-start(bf16[96,256]{1,0:T(8,128)(2,1)S(1)} %reduce_sum.21), channel_id=1, source_target_pairs={{0,0},{2,4},{4,28},{6,8},{8,2},{10,6},{12,30},{14,10},{16,24},{18,... | collective-permute-start | bytes 147464 | tf_op jit(solution)/shard_map/ppermute | solution.py:113

commit v8 on v7

--- a/solution.py
+++ b/solution.py
@@ -84,7 +84,7 @@
     mine = beside(quarters)
     mine, hidden_grad = lax.optimization_barrier((mine, hidden_grad))
     ring = {0: mine}
-    for step in (2, 6, 1, 7):
+    for step in (2, 6, 1, 7, 4):
         ring[step] = from_z(mine, step)
     own = lax.all_gather(jnp.stack([hidden_grad, beside_grad]), "core", axis=0)
     own, parts, far_grad = lax.optimization_barrier((own, gram_parts[0], far_grad))
@@ -98,16 +98,13 @@
     ring[1], ring[7], ring[2], ring[6] = first
     ring[3] = from_z(ring[2], 1)
     ring[5] = from_z(ring[6], 7)
-    mid = feats // 2
-    upper, lower = from_z(ring[2][:mid], 2), from_z(ring[6][mid:], 6)
     far = lax.all_gather(far_pair, "core", axis=0)
 
     kept = lax.all_to_all(ordered, ("y_hi", "z"), 0, 0, tiled=True)
-    upper, kept = lax.optimization_barrier((upper, kept))
+    ring[3], kept = lax.optimization_barrier((ring[3], kept))
     gram_stats = gram_prev + jnp.sum(kept.astype(jnp.float32), axis=0).reshape(gram_prev.shape)
 
-    pieces = [ring[step] for step in ORDER[:-1]] + [upper, lower]
-    blocks = products(own, far, pieces, lax.axis_index("x_lo")).reshape(-1, feats, tokens)
+    blocks = products(own, far, [ring[step] for step in ORDER], lax.axis_index("x_lo")).reshape(-1, feats, tokens)
     arrived = lax.all_to_all(blocks, ("x_hi", "x_mid", "y_lo"), 0, 0, tiled=True)
     shared = jnp.sum(arrived.astype(jnp.float32), axis=0).astype(jnp.bfloat16)
     home = lax.ppermute(shared, WHERE, last_hop())

time: 142 us -> 148 us (1.042)
  the two profiles are of different devices: /device:TPU:64 before, /device:TPU:112 now
where the time goes in v8:
time: 148 us; the launch traced here: 145 us
  starting transfers between devices  74.3 us (50%)
  waiting for transfers between devices  54.8 us (37%)
  blocking collectives  5.08 us (3%)
  other arithmetic  4.59 us (3%)
  Pallas kernels  3.77 us (3%)
  local copies, waits for them, and re-layouts  1.53 us (1%)
    ppermute x7, starting transfers between devices, from_z(): return lax.ppermute(value, 'z', [((i + step) % 8, i) for i in range(8)])  39.1 us
    all_to_all x1, waiting for transfers between devices, on_device(): lax.all_to_all(blocks, ('x_hi', 'x_mid', 'y_lo'), 0, 0, tiled=True)  22 us
    ppermute x7, waiting for transfers between devices, from_z(): return lax.ppermute(value, 'z', [((i + step) % 8, i) for i in range(8)])  17.8 us
    all_to_all x1, starting transfers between devices, on_device(): lax.all_to_all(blocks, ('x_hi', 'x_mid', 'y_lo'), 0, 0, tiled=True)  10 us
    ppermute x1, waiting for transfers between devices, on_device(): home = lax.ppermute(shared, WHERE, last_hop())  9.51 us
    all_to_all x1, starting transfers between devices, on_device(): kept = lax.all_to_all(ordered, ('y_hi', 'z'), 0, 0, tiled=True)  9.3 us
    ppermute x1, waiting for transfers between devices, on_device(): far_pair = jnp.stack([far_grad, lax.ppermute(far_grad, 'x_lo', SWAP)])  5.55 us
    ppermute x1, starting transfers between devices, on_device(): far_grad = lax.ppermute(hidden_grad, 'y_hi', SWAP)  4.26 us
  transfers between devices with their start and end apart: 14, of which 6 were waited for; matrix products, arithmetic and copies ran while one was open for 4% of the time, Pallas kernels for 0%

profile of v8, /device:TPU:112, one launch (start us, length us, event | category | flops | bytes accessed | tf_op | source)
XLA Modules:
  0.0 145.0 jit_solution(16045266677242425613)
XLA Ops:
  0.6 3.6 %all-to-all-start = ((bf16[4,96,384]{2,1,0:T(8,128)(2,1)}), bf16[4,96,384]{2,1,0:T(8,128)(2,1)S(1)}, u32[]{:S(2)}, u32[]{:S(2)}) async-start(bf16[4,96,384]{2,1,0:T(8,128)(2,1)} %bitcast.34), calls=%async_computation | async-start | bytes 589824 | tf_op jit(solution)/shard_map/all_to_all | solution.py:83
  4.3 0.2 fusion.7
  4.5 4.3 %collective-permute-start.5 = (bf16[256,384]{1,0:T(8,128)(2,1)S(1)}, bf16[256,384]{1,0:T(8,128)(2,1)}, u32[]{:S(2)}, u32[]{:S(2)}) collective-permute-start(bf16[256,384]{1,0:T(8,128)(2,1)S(1)} %fusion.7), channel_id=1, source_target_pairs={{0,512},{512,0},{1,513},{513,1},{2,514},{514,2},{3,515},{515,3},{4... | collective-permute-start | bytes 589832 | tf_op jit(solution)/shard_map/ppermute | solution.py:80
  8.7 3.9 %collective-permute-start.4 = (bf16[256,384]{1,0:T(8,128)(2,1)S(1)}, bf16[256,384]{1,0:T(8,128)(2,1)S(1)}, u32[]{:S(2)}, u32[]{:S(2)}) collective-permute-start(bf16[256,384]{1,0:T(8,128)(2,1)S(1)} %fusion.7), channel_id=1, source_target_pairs={{0,8},{8,0},{1,9},{9,1},{2,10},{10,2},{3,11},{11,3},{4,12},{12,4},... | collective-permute-start | bytes 589832 | tf_op jit(solution)/shard_map/ppermute | solution.py:81
  12.7 7.9 %collective-permute-start.3 = (bf16[96,1536]{1,0:T(8,128)(2,1)S(1)}, bf16[96,1536]{1,0:T(8,128)(2,1)S(1)}, u32[]{:S(2)}, u32[]{:S(2)}) collective-permute-start(bf16[96,1536]{1,0:T(8,128)(2,1)S(1)} %pad_maximum_fusion.2.refs_0_), channel_id=1, source_target_pairs={{384,0},{448,64},{0,128},{64,192},{128,256},{192,320},{256,384},{3... | collective-permute-start | bytes 884744 | tf_op jit(solution)/shard_map/ppermute | solution.py:21
  20.6 10.4 %collective-permute-start.2 = (bf16[96,1536]{1,0:T(8,128)(2,1)S(1)}, bf16[96,1536]{1,0:T(8,128)(2,1)S(1)}, u32[]{:S(2)}, u32[]{:S(2)}) collective-permute-start(bf16[96,1536]{1,0:T(8,128)(2,1)S(1)} %pad_maximum_fusion.2.refs_0_), channel_id=1, source_target_pairs={{128,0},{192,64},{256,128},{320,192},{384,256},{448,320},{0,384},{... | collective-permute-start | bytes 884744 | tf_op jit(solution)/shard_map/ppermute | solution.py:21
  31.0 4.3 %collective-permute-start.1 = (bf16[96,1536]{1,0:T(8,128)(2,1)S(1)}, bf16[96,1536]{1,0:T(8,128)(2,1)S(1)}, u32[]{:S(2)}, u32[]{:S(2)}) collective-permute-start(bf16[96,1536]{1,0:T(8,128)(2,1)S(1)} %pad_maximum_fusion.2.refs_0_), channel_id=1, source_target_pairs={{448,0},{0,64},{64,128},{128,192},{192,256},{256,320},{320,384},{3... | collective-permute-start | bytes 884744 | tf_op jit(solution)/shard_map/ppermute | solution.py:21
  35.4 3.4 %collective-permute-start = (bf16[96,1536]{1,0:T(8,128)(2,1)S(1)}, bf16[96,1536]{1,0:T(8,128)(2,1)S(1)}, u32[]{:S(2)}, u32[]{:S(2)}) collective-permute-start(bf16[96,1536]{1,0:T(8,128)(2,1)S(1)} %pad_maximum_fusion.2.refs_0_), channel_id=1, source_target_pairs={{64,0},{128,64},{192,128},{256,192},{320,256},{384,320},{448,384},... | collective-permute-start | bytes 884744 | tf_op jit(solution)/shard_map/ppermute | solution.py:21
  38.8 0.0 copy-start
  38.8 2.5 %all-gather = bf16[4,256,384]{2,1,0:T(8,128)(2,1)S(1)} all-gather(bf16[2,256,384]{2,1,0:T(8,128)(2,1)S(1)} %pad_maximum_fusion), channel_id=2, replica_groups=mesh['y_hi'=2,'z'=8,'x_hi'=2,'x_mid'=2,'x_lo'=2,'y_lo'=4,'core'=2] {'core'}, dimensions={0}, use_global_device_ids=true | all-gather | bytes 1179648 | tf_op jit(solution)/shard_map/all_gather | solution.py:89
  41.3 2.1 %collective-permute-start.6 = (bf16[256,384]{1,0:T(8,128)(2,1)}, bf16[256,384]{1,0:T(8,128)(2,1)S(1)}, u32[]{:S(2)}, u32[]{:S(2)}) collective-permute-start(bf16[256,384]{1,0:T(8,128)(2,1)} %collective-permute-done.5), channel_id=1, source_target_pairs={{0,8},{8,0},{1,9},{9,1},{2,10},{10,2},{3,11},{11,3},{4,12},{12,4},... | collective-permute-start | bytes 589832 | tf_op jit(solution)/shard_map/ppermute | solution.py:91
  43.4 0.1 reshape.49
  43.5 1.4 gather_fusion
  44.9 5.5 %collective-permute-done.6 = bf16[256,384]{1,0:T(8,128)(2,1)S(1)} collective-permute-done((bf16[256,384]{1,0:T(8,128)(2,1)}, bf16[256,384]{1,0:T(8,128)(2,1)S(1)}, u32[]{:S(2)}, u32[]{:S(2)}) %collective-permute-start.6) | collective-permute-done | bytes 196640 | tf_op jit(solution)/shard_map/ppermute | solution.py:91
  50.5 1.8 %pad_maximum_fusion.1 = bf16[2,256,384]{2,1,0:T(8,128)(2,1)} fusion(bf16[1,256,384]{2,1,0:T(8,128)(2,1)S(1)} %bitcast.36, bf16[1,256,384]{2,1,0:T(8,128)(2,1)} %bitcast.10), kind=kLoop, calls=%fused_computation.14 | loop fusion | flops 196608 | bytes 786432 | tf_op jit(solution)/shard_map/stack | solution.py:91
  52.2 9.3 %all-to-all-start.1 = ((bf16[16,12,1024]{2,1,0:T(8,128)(2,1)}), bf16[16,12,1024]{2,1,0:T(8,128)(2,1)}, u32[]{:S(2)}, u32[]{:S(2)}) async-start(bf16[16,12,1024]{2,1,0:T(8,128)(2,1)} %gather_fusion), calls=%async_computation.1 | async-start | bytes 1048576 | tf_op jit(solution)/shard_map/all_to_all | solution.py:103
  61.5 4.6 %collective-permute-start.7 = (bf16[96,1536]{1,0:T(8,128)(2,1)S(1)}, bf16[96,1536]{1,0:T(8,128)(2,1)S(1)}, u32[]{:S(2)}, u32[]{:S(2)}) collective-permute-start(bf16[96,1536]{1,0:T(8,128)(2,1)S(1)} %collective-permute-done.2.refs_3_), channel_id=1, source_target_pairs={{64,0},{128,64},{192,128},{256,192},{320,256},{384,320},{448,384},... | collective-permute-start | bytes 884744 | tf_op jit(solution)/shard_map/ppermute | solution.py:21
  66.1 5.2 %collective-permute-start.9 = (bf16[96,1536]{1,0:T(8,128)(2,1)S(1)}, bf16[96,1536]{1,0:T(8,128)(2,1)}, u32[]{:S(2)}, u32[]{:S(2)}) collective-permute-start(bf16[96,1536]{1,0:T(8,128)(2,1)S(1)} %pad_maximum_fusion.2.refs_0_), channel_id=1, source_target_pairs={{256,0},{320,64},{384,128},{448,192},{0,256},{64,320},{128,384},{1... | collective-permute-start | bytes 884744 | tf_op jit(solution)/shard_map/ppermute | solution.py:21
  71.3 3.4 %collective-permute-start.8 = (bf16[96,1536]{1,0:T(8,128)(2,1)S(1)}, bf16[96,1536]{1,0:T(8,128)(2,1)}, u32[]{:S(2)}, u32[]{:S(2)}) collective-permute-start(bf16[96,1536]{1,0:T(8,128)(2,1)S(1)} %collective-permute-done.3.refs_4_), channel_id=1, source_target_pairs={{448,0},{0,64},{64,128},{128,192},{192,256},{256,320},{320,384},{3... | collective-permute-start | bytes 884744 | tf_op jit(solution)/shard_map/ppermute | solution.py:21
  74.7 2.6 %all-gather.1 = bf16[4,256,384]{2,1,0:T(8,128)(2,1)S(1)} all-gather(bf16[2,256,384]{2,1,0:T(8,128)(2,1)} %pad_maximum_fusion.1), channel_id=3, replica_groups=mesh['y_hi'=2,'z'=8,'x_hi'=2,'x_mid'=2,'x_lo'=2,'y_lo'=4,'core'=2] {'core'}, dimensions={0}, use_global_device_ids=true | all-gather | bytes 1179648 | tf_op jit(solution)/shard_map/all_gather | solution.py:101
  77.3 5.1 %collective-permute-done.7.refs_5_ = bf16[96,1536]{1,0:T(8,128)(2,1)S(1)} collective-permute-done((bf16[96,1536]{1,0:T(8,128)(2,1)S(1)}, bf16[96,1536]{1,0:T(8,128)(2,1)S(1)}, u32[]{:S(2)}, u32[]{:S(2)}) %collective-permute-start.7) | collective-permute-done | bytes 294944 | tf_op jit(solution)/shard_map/ppermute | solution.py:21
  82.4 9.1 %collective-permute-done.9.refs_7_ = bf16[96,1536]{1,0:T(8,128)(2,1)} collective-permute-done((bf16[96,1536]{1,0:T(8,128)(2,1)S(1)}, bf16[96,1536]{1,0:T(8,128)(2,1)}, u32[]{:S(2)}, u32[]{:S(2)}) %collective-permute-start.9) | collective-permute-done | bytes 294944 | tf_op jit(solution)/shard_map/ppermute | solution.py:21
  91.4 3.6 %collective-permute-done.8.refs_6_ = bf16[96,1536]{1,0:T(8,128)(2,1)} collective-permute-done((bf16[96,1536]{1,0:T(8,128)(2,1)S(1)}, bf16[96,1536]{1,0:T(8,128)(2,1)}, u32[]{:S(2)}, u32[]{:S(2)}) %collective-permute-start.8) | collective-permute-done | bytes 294944 | tf_op jit(solution)/shard_map/ppermute | solution.py:21
  95.0 3.8 %shard_map.86 = bf16[2,768,256]{2,1,0:T(8,128)(2,1)} custom-call(s32[1]{0:T(128)} %bitcast.x_ref, bf16[2,2,256,384]{3,2,1,0:T(8,128)(2,1)S(1)} %bitcast.30, bf16[2,2,256,384]{3,2,1,0:T(8,128)(2,1)S(1)} %bitcast.31, bf16[96,1536]{1,0:T(8,128)(2,1)S(1)} %pad_maximum_fusion.2.refs_0_, bf16[96,1536]{1,0:T(8,128)(2,1)S(1)} %collective-permute-done.refs_1_, ...), custom_call_target="tpu_custom_call" | custom-call | flops 1207959552 | bytes 6000000 | tf_op jit(solution)/shard_map/pallas_call | solution.py:63
  98.8 10.0 %all-to-all-start.2 = ((bf16[16,96,256]{2,1,0:T(8,128)(2,1)}), bf16[16,96,256]{2,1,0:T(8,128)(2,1)S(1)}, u32[]{:S(2)}, u32[]{:S(2)}) async-start(bf16[16,96,256]{2,1,0:T(8,128)(2,1)} %bitcast.15), calls=%async_computation.2 | async-start | bytes 1572864 | tf_op jit(solution)/shard_map/all_to_all | solution.py:108
  108.8 1.1 convert_reduce_fusion
  110.0 22.0 %all-to-all-done.2 = bf16[16,96,256]{2,1,0:T(8,128)(2,1)S(1)} async-done(((bf16[16,96,256]{2,1,0:T(8,128)(2,1)}), bf16[16,96,256]{2,1,0:T(8,128)(2,1)S(1)}, u32[]{:S(2)}, u32[]{:S(2)}) %all-to-all-start.2) | async-done | bytes 786464 | tf_op jit(solution)/shard_map/all_to_all | solution.py:108
  132.0 0.1 reduce_sum.21
  132.1 2.1 %collective-permute-start.10 = (bf16[96,256]{1,0:T(8,128)(2,1)S(1)}, bf16[96,256]{1,0:T(8,128)(2,1)S(1)}, u32[]{:S(2)}, u32[]{:S(2)}) collective-permute-start(bf16[96,256]{1,0:T(8,128)(2,1)S(1)} %reduce_sum.21), channel_id=1, source_target_pairs={{0,0},{2,4},{4,28},{6,8},{8,2},{10,6},{12,30},{14,10},{16,24},{18,... | collective-permute-start | bytes 147464 | tf_op jit(solution)/shard_map/ppermute | solution.py:110
  134.2 0.7 reshape_add_fusion
  134.9 9.5 %collective-permute-done.10 = bf16[96,256]{1,0:T(8,128)(2,1)S(1)} collective-permute-done((bf16[96,256]{1,0:T(8,128)(2,1)S(1)}, bf16[96,256]{1,0:T(8,128)(2,1)S(1)}, u32[]{:S(2)}, u32[]{:S(2)}) %collective-permute-start.10) | collective-permute-done | bytes 49184 | tf_op jit(solution)/shard_map/ppermute | solution.py:110
  144.4 0.6 fusion.9
  (24 shorter events, 0.2 us)
Async XLA Ops:
  0.6 3.6 %copy-start.1 = (bf16[256,384]{1,0:T(8,128)(2,1)S(1)}, bf16[256,384]{1,0:T(8,128)(2,1)}, u32[]{:S(2)}) copy-start(bf16[256,384]{1,0:T(8,128)(2,1)} %param.7) | copy-start | bytes 589828
  0.6 3.6 %copy-start.2 = (bf16[256,384]{1,0:T(8,128)(2,1)S(1)}, bf16[256,384]{1,0:T(8,128)(2,1)}, u32[]{:S(2)}) copy-start(bf16[256,384]{1,0:T(8,128)(2,1)} %param.8) | copy-start | bytes 589828
  0.6 12.0 %all-to-all-start = ((bf16[4,96,384]{2,1,0:T(8,128)(2,1)}), bf16[4,96,384]{2,1,0:T(8,128)(2,1)S(1)}, u32[]{:S(2)}, u32[]{:S(2)}) async-start(bf16[4,96,384]{2,1,0:T(8,128)(2,1)} %bitcast.34), calls=%async_computation | async-start | bytes 589824 | tf_op jit(solution)/shard_map/all_to_all | solution.py:83
  4.5 36.8 %collective-permute-start.5 = (bf16[256,384]{1,0:T(8,128)(2,1)S(1)}, bf16[256,384]{1,0:T(8,128)(2,1)}, u32[]{:S(2)}, u32[]{:S(2)}) collective-permute-start(bf16[256,384]{1,0:T(8,128)(2,1)S(1)} %fusion.7), channel_id=1, source_target_pairs={{0,512},{512,0},{1,513},{513,1},{2,514},{514,2},{3,515},{515,3},{4... | collective-permute-start | bytes 589832 | tf_op jit(solution)/shard_map/ppermute | solution.py:80
  8.7 26.6 %collective-permute-start.4 = (bf16[256,384]{1,0:T(8,128)(2,1)S(1)}, bf16[256,384]{1,0:T(8,128)(2,1)S(1)}, u32[]{:S(2)}, u32[]{:S(2)}) collective-permute-start(bf16[256,384]{1,0:T(8,128)(2,1)S(1)} %fusion.7), channel_id=1, source_target_pairs={{0,8},{8,0},{1,9},{9,1},{2,10},{10,2},{3,11},{11,3},{4,12},{12,4},... | collective-permute-start | bytes 589832 | tf_op jit(solution)/shard_map/ppermute | solution.py:81
  12.7 39.5 %collective-permute-start.3 = (bf16[96,1536]{1,0:T(8,128)(2,1)S(1)}, bf16[96,1536]{1,0:T(8,128)(2,1)S(1)}, u32[]{:S(2)}, u32[]{:S(2)}) collective-permute-start(bf16[96,1536]{1,0:T(8,128)(2,1)S(1)} %pad_maximum_fusion.2.refs_0_), channel_id=1, source_target_pairs={{384,0},{448,64},{0,128},{64,192},{128,256},{192,320},{256,384},{3... | collective-permute-start | bytes 884744 | tf_op jit(solution)/shard_map/ppermute | solution.py:21
  20.6 31.6 %collective-permute-start.2 = (bf16[96,1536]{1,0:T(8,128)(2,1)S(1)}, bf16[96,1536]{1,0:T(8,128)(2,1)S(1)}, u32[]{:S(2)}, u32[]{:S(2)}) collective-permute-start(bf16[96,1536]{1,0:T(8,128)(2,1)S(1)} %pad_maximum_fusion.2.refs_0_), channel_id=1, source_target_pairs={{128,0},{192,64},{256,128},{320,192},{384,256},{448,320},{0,384},{... | collective-permute-start | bytes 884744 | tf_op jit(solution)/shard_map/ppermute | solution.py:21
  31.0 21.2 %collective-permute-start.1 = (bf16[96,1536]{1,0:T(8,128)(2,1)S(1)}, bf16[96,1536]{1,0:T(8,128)(2,1)S(1)}, u32[]{:S(2)}, u32[]{:S(2)}) collective-permute-start(bf16[96,1536]{1,0:T(8,128)(2,1)S(1)} %pad_maximum_fusion.2.refs_0_), channel_id=1, source_target_pairs={{448,0},{0,64},{64,128},{128,192},{192,256},{256,320},{320,384},{3... | collective-permute-start | bytes 884744 | tf_op jit(solution)/shard_map/ppermute | solution.py:21
  35.4 16.9 %collective-permute-start = (bf16[96,1536]{1,0:T(8,128)(2,1)S(1)}, bf16[96,1536]{1,0:T(8,128)(2,1)S(1)}, u32[]{:S(2)}, u32[]{:S(2)}) collective-permute-start(bf16[96,1536]{1,0:T(8,128)(2,1)S(1)} %pad_maximum_fusion.2.refs_0_), channel_id=1, source_target_pairs={{64,0},{128,64},{192,128},{256,192},{320,256},{384,320},{448,384},... | collective-permute-start | bytes 884744 | tf_op jit(solution)/shard_map/ppermute | solution.py:21
  38.8 4.7 %copy-start = (bf16[1,192,1024]{2,1,0:T(8,128)(2,1)S(1)}, bf16[1,192,1024]{2,1,0:T(8,128)(2,1)}, u32[]{:S(2)}) copy-start(bf16[1,192,1024]{2,1,0:T(8,128)(2,1)} %param.11) | copy-start | bytes 1179652
  41.3 2.1 %copy-start.5 = (s32[1,16]{1,0:T(1,128)S(1)}, s32[1,16]{1,0:T(1,128)}, u32[]{:S(2)}) copy-start(s32[1,16]{1,0:T(1,128)} %param.12) | copy-start | bytes 196
  41.3 9.2 %collective-permute-start.6 = (bf16[256,384]{1,0:T(8,128)(2,1)}, bf16[256,384]{1,0:T(8,128)(2,1)S(1)}, u32[]{:S(2)}, u32[]{:S(2)}) collective-permute-start(bf16[256,384]{1,0:T(8,128)(2,1)} %collective-permute-done.5), channel_id=1, source_target_pairs={{0,8},{8,0},{1,9},{9,1},{2,10},{10,2},{3,11},{11,3},{4,12},{12,4},... | collective-permute-start | bytes 589832 | tf_op jit(solution)/shard_map/ppermute | solution.py:91
  52.2 30.1 %all-to-all-start.1 = ((bf16[16,12,1024]{2,1,0:T(8,128)(2,1)}), bf16[16,12,1024]{2,1,0:T(8,128)(2,1)}, u32[]{:S(2)}, u32[]{:S(2)}) async-start(bf16[16,12,1024]{2,1,0:T(8,128)(2,1)} %gather_fusion), calls=%async_computation.1 | async-start | bytes 1048576 | tf_op jit(solution)/shard_map/all_to_all | solution.py:103
  61.5 20.8 %collective-permute-start.7 = (bf16[96,1536]{1,0:T(8,128)(2,1)S(1)}, bf16[96,1536]{1,0:T(8,128)(2,1)S(1)}, u32[]{:S(2)}, u32[]{:S(2)}) collective-permute-start(bf16[96,1536]{1,0:T(8,128)(2,1)S(1)} %collective-permute-done.2.refs_3_), channel_id=1, source_target_pairs={{64,0},{128,64},{192,128},{256,192},{320,256},{384,320},{448,384},... | collective-permute-start | bytes 884744 | tf_op jit(solution)/shard_map/ppermute | solution.py:21
  66.1 25.3 %collective-permute-start.9 = (bf16[96,1536]{1,0:T(8,128)(2,1)S(1)}, bf16[96,1536]{1,0:T(8,128)(2,1)}, u32[]{:S(2)}, u32[]{:S(2)}) collective-permute-start(bf16[96,1536]{1,0:T(8,128)(2,1)S(1)} %pad_maximum_fusion.2.refs_0_), channel_id=1, source_target_pairs={{256,0},{320,64},{384,128},{448,192},{0,256},{64,320},{128,384},{1... | collective-permute-start | bytes 884744 | tf_op jit(solution)/shard_map/ppermute | solution.py:21
  71.3 23.7 %collective-permute-start.8 = (bf16[96,1536]{1,0:T(8,128)(2,1)S(1)}, bf16[96,1536]{1,0:T(8,128)(2,1)}, u32[]{:S(2)}, u32[]{:S(2)}) collective-permute-start(bf16[96,1536]{1,0:T(8,128)(2,1)S(1)} %collective-permute-done.3.refs_4_), channel_id=1, source_target_pairs={{448,0},{0,64},{64,128},{128,192},{192,256},{256,320},{320,384},{3... | collective-permute-start | bytes 884744 | tf_op jit(solution)/shard_map/ppermute | solution.py:21
  98.8 33.2 %all-to-all-start.2 = ((bf16[16,96,256]{2,1,0:T(8,128)(2,1)}), bf16[16,96,256]{2,1,0:T(8,128)(2,1)S(1)}, u32[]{:S(2)}, u32[]{:S(2)}) async-start(bf16[16,96,256]{2,1,0:T(8,128)(2,1)} %bitcast.15), calls=%async_computation.2 | async-start | bytes 1572864 | tf_op jit(solution)/shard_map/all_to_all | solution.py:108
  110.0 24.2 %copy-start.3 = (f32[1,1,12,1024]{3,1,2,0:T(1,128)S(1)}, f32[1,1,12,1024]{3,1,2,0:T(1,128)}, u32[]{:S(2)}) copy-start(f32[1,1,12,1024]{3,1,2,0:T(1,128)} %param.13) | copy-start | bytes 147460
  132.1 12.3 %copy-start.4 = (bf16[256,96]{0,1:T(8,128)(2,1)S(1)}, bf16[256,96]{0,1:T(8,128)(2,1)}, u32[]{:S(2)}) copy-start(bf16[256,96]{0,1:T(8,128)(2,1)} %param.10) | copy-start | bytes 147460
  132.1 12.3 %collective-permute-start.10 = (bf16[96,256]{1,0:T(8,128)(2,1)S(1)}, bf16[96,256]{1,0:T(8,128)(2,1)S(1)}, u32[]{:S(2)}, u32[]{:S(2)}) collective-permute-start(bf16[96,256]{1,0:T(8,128)(2,1)S(1)} %reduce_sum.21), channel_id=1, source_target_pairs={{0,0},{2,4},{4,28},{6,8},{8,2},{10,6},{12,30},{14,10},{16,24},{18,... | collective-permute-start | bytes 147464 | tf_op jit(solution)/shard_map/ppermute | solution.py:110

commit v9 on v7

--- a/solution.py
+++ b/solution.py
@@ -65,7 +65,7 @@
         out_shape=jax.ShapeDtypeStruct((2, rows, tokens), jnp.bfloat16),
         in_specs=[pl.BlockSpec(memory_space=pltpu.SMEM)] + [in_vmem] * (2 + len(pieces)),
         out_specs=in_vmem,
-        compiler_params=pltpu.CompilerParams(vmem_limit_bytes=32 * 1024 * 1024),
+        compiler_params=pltpu.CompilerParams(vmem_limit_bytes=12 * 1024 * 1024),
         cost_estimate=pl.CostEstimate(
             flops=4 * rows * tokens * cores * places * hidden, bytes_accessed=6000000, transcendentals=0
         ),
@@ -88,18 +88,20 @@
         ring[step] = from_z(mine, step)
     own = lax.all_gather(jnp.stack([hidden_grad, beside_grad]), "core", axis=0)
     own, parts, far_grad = lax.optimization_barrier((own, gram_parts[0], far_grad))
-    far_pair = jnp.stack([far_grad, lax.ppermute(far_grad, "x_lo", SWAP)])
+    far_beside = lax.ppermute(far_grad, "x_lo", SWAP)
     stripes = parts.reshape(lax.axis_size(("y_hi", "z")), -1, parts.shape[1])
     ordered = stripes[stripe_order[0]]
 
-    *first, far_pair, own, ordered = lax.optimization_barrier(
-        (ring[1], ring[7], ring[2], ring[6], far_pair, own, ordered)
+    mid = feats // 2
+    halves = ring[2][:mid], ring[6][mid:]
+    *first, far_beside, own, ordered = lax.optimization_barrier(
+        (ring[1], ring[7], ring[2], ring[6], *halves, far_beside, own, ordered)
     )
-    ring[1], ring[7], ring[2], ring[6] = first
+    ring[1], ring[7], ring[2], ring[6], *halves = first
+    far_pair = jnp.stack([far_grad, far_beside])
+    upper, lower = from_z(halves[0], 2), from_z(halves[1], 6)
     ring[3] = from_z(ring[2], 1)
     ring[5] = from_z(ring[6], 7)
-    mid = feats // 2
-    upper, lower = from_z(ring[2][:mid], 2), from_z(ring[6][mid:], 6)
     far = lax.all_gather(far_pair, "core", axis=0)
 
     kept = lax.all_to_all(ordered, ("y_hi", "z"), 0, 0, tiled=True)

time: 142 us -> 141 us (level)
  the two profiles are of different devices: /device:TPU:64 before, /device:TPU:112 now
where the time goes in v9:
time: 141 us; the launch traced here: 138 us
  starting transfers between devices  77.4 us (55%)
  waiting for transfers between devices  44.2 us (31%)
  blocking collectives  4.87 us (3%)
  other arithmetic  3.91 us (3%)
  Pallas kernels  3.7 us (3%)
  local copies, waits for them, and re-layouts  3.36 us (2%)
    ppermute x8, starting transfers between devices, from_z(): return lax.ppermute(value, 'z', [((i + step) % 8, i) for i in range(8)])  40.4 us
    all_to_all x1, waiting for transfers between devices, on_device(): lax.all_to_all(blocks, ('x_hi', 'x_mid', 'y_lo'), 0, 0, tiled=True)  22.1 us
    all_to_all x1, starting transfers between devices, on_device(): kept = lax.all_to_all(ordered, ('y_hi', 'z'), 0, 0, tiled=True)  10.4 us
    all_to_all x1, starting transfers between devices, on_device(): lax.all_to_all(blocks, ('x_hi', 'x_mid', 'y_lo'), 0, 0, tiled=True)  10 us
    ppermute x8, waiting for transfers between devices, from_z(): return lax.ppermute(value, 'z', [((i + step) % 8, i) for i in range(8)])  9.11 us
    ppermute x1, waiting for transfers between devices, on_device(): home = lax.ppermute(shared, WHERE, last_hop())  8.72 us
    ppermute x1, starting transfers between devices, on_device(): far_grad = lax.ppermute(hidden_grad, 'y_hi', SWAP)  4.26 us
    ppermute x1, waiting for transfers between devices, on_device(): far_beside = lax.ppermute(far_grad, 'x_lo', SWAP)  4.21 us
  transfers between devices with their start and end apart: 15, of which 8 were waited for; matrix products, arithmetic and copies ran while one was open for 4% of the time, Pallas kernels for 0%

profile of v9, /device:TPU:112, one launch (start us, length us, event | category | flops | bytes accessed | tf_op | source)
XLA Modules:
  0.0 138.3 jit_solution(418500722052744580)
XLA Ops:
  0.6 3.6 %all-to-all-start = ((bf16[4,96,384]{2,1,0:T(8,128)(2,1)}), bf16[4,96,384]{2,1,0:T(8,128)(2,1)S(1)}, u32[]{:S(2)}, u32[]{:S(2)}) async-start(bf16[4,96,384]{2,1,0:T(8,128)(2,1)} %bitcast.34), calls=%async_computation | async-start | bytes 589824 | tf_op jit(solution)/shard_map/all_to_all | solution.py:83
  4.5 4.3 %collective-permute-start.5 = (bf16[256,384]{1,0:T(8,128)(2,1)S(1)}, bf16[256,384]{1,0:T(8,128)(2,1)}, u32[]{:S(2)}, u32[]{:S(2)}) collective-permute-start(bf16[256,384]{1,0:T(8,128)(2,1)S(1)} %fusion.7), channel_id=1, source_target_pairs={{0,512},{512,0},{1,513},{513,1},{2,514},{514,2},{3,515},{515,3},{4... | collective-permute-start | bytes 589832 | tf_op jit(solution)/shard_map/ppermute | solution.py:80
  8.7 3.9 %collective-permute-start.4 = (bf16[256,384]{1,0:T(8,128)(2,1)S(1)}, bf16[256,384]{1,0:T(8,128)(2,1)S(1)}, u32[]{:S(2)}, u32[]{:S(2)}) collective-permute-start(bf16[256,384]{1,0:T(8,128)(2,1)S(1)} %fusion.7), channel_id=1, source_target_pairs={{0,8},{8,0},{1,9},{9,1},{2,10},{10,2},{3,11},{11,3},{4,12},{12,4},... | collective-permute-start | bytes 589832 | tf_op jit(solution)/shard_map/ppermute | solution.py:81
  12.7 7.9 %collective-permute-start.3 = (bf16[96,1536]{1,0:T(8,128)(2,1)S(1)}, bf16[96,1536]{1,0:T(8,128)(2,1)S(1)}, u32[]{:S(2)}, u32[]{:S(2)}) collective-permute-start(bf16[96,1536]{1,0:T(8,128)(2,1)S(1)} %pad_maximum_fusion.2.refs_0_), channel_id=1, source_target_pairs={{384,0},{448,64},{0,128},{64,192},{128,256},{192,320},{256,384},{3... | collective-permute-start | bytes 884744 | tf_op jit(solution)/shard_map/ppermute | solution.py:21
  20.6 10.4 %collective-permute-start.2 = (bf16[96,1536]{1,0:T(8,128)(2,1)S(1)}, bf16[96,1536]{1,0:T(8,128)(2,1)S(1)}, u32[]{:S(2)}, u32[]{:S(2)}) collective-permute-start(bf16[96,1536]{1,0:T(8,128)(2,1)S(1)} %pad_maximum_fusion.2.refs_0_), channel_id=1, source_target_pairs={{128,0},{192,64},{256,128},{320,192},{384,256},{448,320},{0,384},{... | collective-permute-start | bytes 884744 | tf_op jit(solution)/shard_map/ppermute | solution.py:21
  31.0 4.3 %collective-permute-start.1 = (bf16[96,1536]{1,0:T(8,128)(2,1)S(1)}, bf16[96,1536]{1,0:T(8,128)(2,1)S(1)}, u32[]{:S(2)}, u32[]{:S(2)}) collective-permute-start(bf16[96,1536]{1,0:T(8,128)(2,1)S(1)} %pad_maximum_fusion.2.refs_0_), channel_id=1, source_target_pairs={{448,0},{0,64},{64,128},{128,192},{192,256},{256,320},{320,384},{3... | collective-permute-start | bytes 884744 | tf_op jit(solution)/shard_map/ppermute | solution.py:21
  35.4 3.4 %collective-permute-start = (bf16[96,1536]{1,0:T(8,128)(2,1)S(1)}, bf16[96,1536]{1,0:T(8,128)(2,1)S(1)}, u32[]{:S(2)}, u32[]{:S(2)}) collective-permute-start(bf16[96,1536]{1,0:T(8,128)(2,1)S(1)} %pad_maximum_fusion.2.refs_0_), channel_id=1, source_target_pairs={{64,0},{128,64},{192,128},{256,192},{320,256},{384,320},{448,384},... | collective-permute-start | bytes 884744 | tf_op jit(solution)/shard_map/ppermute | solution.py:21
  38.8 2.5 %all-gather = bf16[4,256,384]{2,1,0:T(8,128)(2,1)S(1)} all-gather(bf16[2,256,384]{2,1,0:T(8,128)(2,1)S(1)} %pad_maximum_fusion), channel_id=2, replica_groups=mesh['y_hi'=2,'z'=8,'x_hi'=2,'x_mid'=2,'x_lo'=2,'y_lo'=4,'core'=2] {'core'}, dimensions={0}, use_global_device_ids=true | all-gather | bytes 1179648 | tf_op jit(solution)/shard_map/all_gather | solution.py:89
  41.3 2.1 %collective-permute-start.6 = (bf16[256,384]{1,0:T(8,128)(2,1)}, bf16[256,384]{1,0:T(8,128)(2,1)S(1)}, u32[]{:S(2)}, u32[]{:S(2)}) collective-permute-start(bf16[256,384]{1,0:T(8,128)(2,1)} %collective-permute-done.5), channel_id=1, source_target_pairs={{0,8},{8,0},{1,9},{9,1},{2,10},{10,2},{3,11},{11,3},{4,12},{12,4},... | collective-permute-start | bytes 589832 | tf_op jit(solution)/shard_map/ppermute | solution.py:91
  43.5 1.4 gather_fusion
  44.9 0.7 slice.31
  45.6 0.7 slice.30
  46.3 4.2 %collective-permute-done.6 = bf16[256,384]{1,0:T(8,128)(2,1)S(1)} collective-permute-done((bf16[256,384]{1,0:T(8,128)(2,1)}, bf16[256,384]{1,0:T(8,128)(2,1)S(1)}, u32[]{:S(2)}, u32[]{:S(2)}) %collective-permute-start.6) | collective-permute-done | bytes 196640 | tf_op jit(solution)/shard_map/ppermute | solution.py:91
  51.1 10.4 %all-to-all-start.1 = ((bf16[16,12,1024]{2,1,0:T(8,128)(2,1)}), bf16[16,12,1024]{2,1,0:T(8,128)(2,1)}, u32[]{:S(2)}, u32[]{:S(2)}) async-start(bf16[16,12,1024]{2,1,0:T(8,128)(2,1)} %gather_fusion), calls=%async_computation.1 | async-start | bytes 1048576 | tf_op jit(solution)/shard_map/all_to_all | solution.py:107
  61.5 5.5 %collective-permute-start.9 = (bf16[48,1536]{1,0:T(8,128)(2,1)}, bf16[48,1536]{1,0:T(8,128)(2,1)S(1)}, u32[]{:S(2)}, u32[]{:S(2)}) collective-permute-start(bf16[48,1536]{1,0:T(8,128)(2,1)} %slice.30), channel_id=1, source_target_pairs={{128,0},{192,64},{256,128},{320,192},{384,256},{448,320},{0,384},{... | collective-permute-start | bytes 442376 | tf_op jit(solution)/shard_map/ppermute | solution.py:21
  67.0 1.9 %collective-permute-start.10 = (bf16[48,1536]{1,0:T(8,128)(2,1)}, bf16[48,1536]{1,0:T(8,128)(2,1)}, u32[]{:S(2)}, u32[]{:S(2)}) collective-permute-start(bf16[48,1536]{1,0:T(8,128)(2,1)} %slice.31), channel_id=1, source_target_pairs={{384,0},{448,64},{0,128},{64,192},{128,256},{192,320},{256,384},{3... | collective-permute-start | bytes 442376 | tf_op jit(solution)/shard_map/ppermute | solution.py:21
  69.0 5.1 %collective-permute-start.7 = (bf16[96,1536]{1,0:T(8,128)(2,1)S(1)}, bf16[96,1536]{1,0:T(8,128)(2,1)S(1)}, u32[]{:S(2)}, u32[]{:S(2)}) collective-permute-start(bf16[96,1536]{1,0:T(8,128)(2,1)S(1)} %collective-permute-done.2.refs_3_), channel_id=1, source_target_pairs={{64,0},{128,64},{192,128},{256,192},{320,256},{384,320},{448,384},... | collective-permute-start | bytes 884744 | tf_op jit(solution)/shard_map/ppermute | solution.py:21
  74.1 1.9 %collective-permute-start.8 = (bf16[96,1536]{1,0:T(8,128)(2,1)S(1)}, bf16[96,1536]{1,0:T(8,128)(2,1)}, u32[]{:S(2)}, u32[]{:S(2)}) collective-permute-start(bf16[96,1536]{1,0:T(8,128)(2,1)S(1)} %collective-permute-done.3.refs_4_), channel_id=1, source_target_pairs={{448,0},{0,64},{64,128},{128,192},{192,256},{256,320},{320,384},{3... | collective-permute-start | bytes 884744 | tf_op jit(solution)/shard_map/ppermute | solution.py:21
  76.0 1.1 pad_maximum_fusion.1
  77.1 2.4 %all-gather.1 = bf16[4,256,384]{2,1,0:T(8,128)(2,1)S(1)} all-gather(bf16[2,256,384]{2,1,0:T(8,128)(2,1)S(1)} %pad_maximum_fusion.1), channel_id=3, replica_groups=mesh['y_hi'=2,'z'=8,'x_hi'=2,'x_mid'=2,'x_lo'=2,'y_lo'=4,'core'=2] {'core'}, dimensions={0}, use_global_device_ids=true | all-gather | bytes 1179648 | tf_op jit(solution)/shard_map/all_gather | solution.py:105
  79.5 2.2 %collective-permute-done.9.refs_7_ = bf16[48,1536]{1,0:T(8,128)(2,1)S(1)} collective-permute-done((bf16[48,1536]{1,0:T(8,128)(2,1)}, bf16[48,1536]{1,0:T(8,128)(2,1)S(1)}, u32[]{:S(2)}, u32[]{:S(2)}) %collective-permute-start.9) | collective-permute-done | bytes 147488 | tf_op jit(solution)/shard_map/ppermute | solution.py:21
  81.6 3.1 %collective-permute-done.10.refs_8_ = bf16[48,1536]{1,0:T(8,128)(2,1)} collective-permute-done((bf16[48,1536]{1,0:T(8,128)(2,1)}, bf16[48,1536]{1,0:T(8,128)(2,1)}, u32[]{:S(2)}, u32[]{:S(2)}) %collective-permute-start.10) | collective-permute-done | bytes 147488 | tf_op jit(solution)/shard_map/ppermute | solution.py:21
  84.7 2.7 %collective-permute-done.7.refs_5_ = bf16[96,1536]{1,0:T(8,128)(2,1)S(1)} collective-permute-done((bf16[96,1536]{1,0:T(8,128)(2,1)S(1)}, bf16[96,1536]{1,0:T(8,128)(2,1)S(1)}, u32[]{:S(2)}, u32[]{:S(2)}) %collective-permute-start.7) | collective-permute-done | bytes 294944 | tf_op jit(solution)/shard_map/ppermute | solution.py:21
  87.5 1.0 collective-permute-done.8.refs_6_
  88.4 3.7 %shard_map.86 = bf16[2,768,256]{2,1,0:T(8,128)(2,1)} custom-call(s32[1]{0:T(128)} %bitcast.x_ref, bf16[2,2,256,384]{3,2,1,0:T(8,128)(2,1)S(1)} %bitcast.30, bf16[2,2,256,384]{3,2,1,0:T(8,128)(2,1)S(1)} %bitcast.31, bf16[96,1536]{1,0:T(8,128)(2,1)S(1)} %pad_maximum_fusion.2.refs_0_, bf16[96,1536]{1,0:T(8,128)(2,1)S(1)} %collective-permute-done.refs_1_, ...), custom_call_target="tpu_custom_call" | custom-call | flops 1207959552 | bytes 6000000 | tf_op jit(solution)/shard_map/pallas_call | solution.py:63
  92.1 10.0 %all-to-all-start.2 = ((bf16[16,96,256]{2,1,0:T(8,128)(2,1)}), bf16[16,96,256]{2,1,0:T(8,128)(2,1)S(1)}, u32[]{:S(2)}, u32[]{:S(2)}) async-start(bf16[16,96,256]{2,1,0:T(8,128)(2,1)} %bitcast.15), calls=%async_computation.2 | async-start | bytes 1572864 | tf_op jit(solution)/shard_map/all_to_all | solution.py:113
  102.1 1.1 convert_reduce_fusion
  103.3 22.1 %all-to-all-done.2 = bf16[16,96,256]{2,1,0:T(8,128)(2,1)S(1)} async-done(((bf16[16,96,256]{2,1,0:T(8,128)(2,1)}), bf16[16,96,256]{2,1,0:T(8,128)(2,1)S(1)}, u32[]{:S(2)}, u32[]{:S(2)}) %all-to-all-start.2) | async-done | bytes 786464 | tf_op jit(solution)/shard_map/all_to_all | solution.py:113
  125.5 2.7 %collective-permute-start.11 = (bf16[96,256]{1,0:T(8,128)(2,1)S(1)}, bf16[96,256]{1,0:T(8,128)(2,1)S(1)}, u32[]{:S(2)}, u32[]{:S(2)}) collective-permute-start(bf16[96,256]{1,0:T(8,128)(2,1)S(1)} %reduce_sum.21), channel_id=1, source_target_pairs={{0,0},{2,4},{4,28},{6,8},{8,2},{10,6},{12,30},{14,10},{16,24},{18,... | collective-permute-start | bytes 147464 | tf_op jit(solution)/shard_map/ppermute | solution.py:115
  128.3 0.7 reshape_add_fusion
  128.9 8.7 %collective-permute-done.11 = bf16[96,256]{1,0:T(8,128)(2,1)S(1)} collective-permute-done((bf16[96,256]{1,0:T(8,128)(2,1)S(1)}, bf16[96,256]{1,0:T(8,128)(2,1)S(1)}, u32[]{:S(2)}, u32[]{:S(2)}) %collective-permute-start.11) | collective-permute-done | bytes 49184 | tf_op jit(solution)/shard_map/ppermute | solution.py:115
  137.7 0.6 fusion.9
  (30 shorter events, 1.2 us)
Async XLA Ops:
  0.6 3.6 %copy-start.1 = (bf16[256,384]{1,0:T(8,128)(2,1)S(1)}, bf16[256,384]{1,0:T(8,128)(2,1)}, u32[]{:S(2)}) copy-start(bf16[256,384]{1,0:T(8,128)(2,1)} %param.7) | copy-start | bytes 589828
  0.6 3.6 %copy-start.2 = (bf16[256,384]{1,0:T(8,128)(2,1)S(1)}, bf16[256,384]{1,0:T(8,128)(2,1)}, u32[]{:S(2)}) copy-start(bf16[256,384]{1,0:T(8,128)(2,1)} %param.8) | copy-start | bytes 589828
  0.6 12.0 %all-to-all-start = ((bf16[4,96,384]{2,1,0:T(8,128)(2,1)}), bf16[4,96,384]{2,1,0:T(8,128)(2,1)S(1)}, u32[]{:S(2)}, u32[]{:S(2)}) async-start(bf16[4,96,384]{2,1,0:T(8,128)(2,1)} %bitcast.34), calls=%async_computation | async-start | bytes 589824 | tf_op jit(solution)/shard_map/all_to_all | solution.py:83
  4.5 36.8 %collective-permute-start.5 = (bf16[256,384]{1,0:T(8,128)(2,1)S(1)}, bf16[256,384]{1,0:T(8,128)(2,1)}, u32[]{:S(2)}, u32[]{:S(2)}) collective-permute-start(bf16[256,384]{1,0:T(8,128)(2,1)S(1)} %fusion.7), channel_id=1, source_target_pairs={{0,512},{512,0},{1,513},{513,1},{2,514},{514,2},{3,515},{515,3},{4... | collective-permute-start | bytes 589832 | tf_op jit(solution)/shard_map/ppermute | solution.py:80
  8.7 26.6 %collective-permute-start.4 = (bf16[256,384]{1,0:T(8,128)(2,1)S(1)}, bf16[256,384]{1,0:T(8,128)(2,1)S(1)}, u32[]{:S(2)}, u32[]{:S(2)}) collective-permute-start(bf16[256,384]{1,0:T(8,128)(2,1)S(1)} %fusion.7), channel_id=1, source_target_pairs={{0,8},{8,0},{1,9},{9,1},{2,10},{10,2},{3,11},{11,3},{4,12},{12,4},... | collective-permute-start | bytes 589832 | tf_op jit(solution)/shard_map/ppermute | solution.py:81
  12.7 32.2 %collective-permute-start.3 = (bf16[96,1536]{1,0:T(8,128)(2,1)S(1)}, bf16[96,1536]{1,0:T(8,128)(2,1)S(1)}, u32[]{:S(2)}, u32[]{:S(2)}) collective-permute-start(bf16[96,1536]{1,0:T(8,128)(2,1)S(1)} %pad_maximum_fusion.2.refs_0_), channel_id=1, source_target_pairs={{384,0},{448,64},{0,128},{64,192},{128,256},{192,320},{256,384},{3... | collective-permute-start | bytes 884744 | tf_op jit(solution)/shard_map/ppermute | solution.py:21
  20.6 25.0 %collective-permute-start.2 = (bf16[96,1536]{1,0:T(8,128)(2,1)S(1)}, bf16[96,1536]{1,0:T(8,128)(2,1)S(1)}, u32[]{:S(2)}, u32[]{:S(2)}) collective-permute-start(bf16[96,1536]{1,0:T(8,128)(2,1)S(1)} %pad_maximum_fusion.2.refs_0_), channel_id=1, source_target_pairs={{128,0},{192,64},{256,128},{320,192},{384,256},{448,320},{0,384},{... | collective-permute-start | bytes 884744 | tf_op jit(solution)/shard_map/ppermute | solution.py:21
  31.0 19.4 %collective-permute-start.1 = (bf16[96,1536]{1,0:T(8,128)(2,1)S(1)}, bf16[96,1536]{1,0:T(8,128)(2,1)S(1)}, u32[]{:S(2)}, u32[]{:S(2)}) collective-permute-start(bf16[96,1536]{1,0:T(8,128)(2,1)S(1)} %pad_maximum_fusion.2.refs_0_), channel_id=1, source_target_pairs={{448,0},{0,64},{64,128},{128,192},{192,256},{256,320},{320,384},{3... | collective-permute-start | bytes 884744 | tf_op jit(solution)/shard_map/ppermute | solution.py:21
  35.4 15.3 %collective-permute-start = (bf16[96,1536]{1,0:T(8,128)(2,1)S(1)}, bf16[96,1536]{1,0:T(8,128)(2,1)S(1)}, u32[]{:S(2)}, u32[]{:S(2)}) collective-permute-start(bf16[96,1536]{1,0:T(8,128)(2,1)S(1)} %pad_maximum_fusion.2.refs_0_), channel_id=1, source_target_pairs={{64,0},{128,64},{192,128},{256,192},{320,256},{384,320},{448,384},... | collective-permute-start | bytes 884744 | tf_op jit(solution)/shard_map/ppermute | solution.py:21
  38.8 4.7 %copy-start = (bf16[1,192,1024]{2,1,0:T(8,128)(2,1)S(1)}, bf16[1,192,1024]{2,1,0:T(8,128)(2,1)}, u32[]{:S(2)}) copy-start(bf16[1,192,1024]{2,1,0:T(8,128)(2,1)} %param.11) | copy-start | bytes 1179652
  41.3 2.1 %copy-start.6 = (s32[1,16]{1,0:T(1,128)S(1)}, s32[1,16]{1,0:T(1,128)}, u32[]{:S(2)}) copy-start(s32[1,16]{1,0:T(1,128)} %param.12) | copy-start | bytes 196
  41.3 9.2 %collective-permute-start.6 = (bf16[256,384]{1,0:T(8,128)(2,1)}, bf16[256,384]{1,0:T(8,128)(2,1)S(1)}, u32[]{:S(2)}, u32[]{:S(2)}) collective-permute-start(bf16[256,384]{1,0:T(8,128)(2,1)} %collective-permute-done.5), channel_id=1, source_target_pairs={{0,8},{8,0},{1,9},{9,1},{2,10},{10,2},{3,11},{11,3},{4,12},{12,4},... | collective-permute-start | bytes 589832 | tf_op jit(solution)/shard_map/ppermute | solution.py:91
  50.5 0.7 copy-start.3
  51.1 30.5 %all-to-all-start.1 = ((bf16[16,12,1024]{2,1,0:T(8,128)(2,1)}), bf16[16,12,1024]{2,1,0:T(8,128)(2,1)}, u32[]{:S(2)}, u32[]{:S(2)}) async-start(bf16[16,12,1024]{2,1,0:T(8,128)(2,1)} %gather_fusion), calls=%async_computation.1 | async-start | bytes 1048576 | tf_op jit(solution)/shard_map/all_to_all | solution.py:107
  61.5 20.1 %collective-permute-start.9 = (bf16[48,1536]{1,0:T(8,128)(2,1)}, bf16[48,1536]{1,0:T(8,128)(2,1)S(1)}, u32[]{:S(2)}, u32[]{:S(2)}) collective-permute-start(bf16[48,1536]{1,0:T(8,128)(2,1)} %slice.30), channel_id=1, source_target_pairs={{128,0},{192,64},{256,128},{320,192},{384,256},{448,320},{0,384},{... | collective-permute-start | bytes 442376 | tf_op jit(solution)/shard_map/ppermute | solution.py:21
  67.0 17.7 %collective-permute-start.10 = (bf16[48,1536]{1,0:T(8,128)(2,1)}, bf16[48,1536]{1,0:T(8,128)(2,1)}, u32[]{:S(2)}, u32[]{:S(2)}) collective-permute-start(bf16[48,1536]{1,0:T(8,128)(2,1)} %slice.31), channel_id=1, source_target_pairs={{384,0},{448,64},{0,128},{64,192},{128,256},{192,320},{256,384},{3... | collective-permute-start | bytes 442376 | tf_op jit(solution)/shard_map/ppermute | solution.py:21
  69.0 18.5 %collective-permute-start.7 = (bf16[96,1536]{1,0:T(8,128)(2,1)S(1)}, bf16[96,1536]{1,0:T(8,128)(2,1)S(1)}, u32[]{:S(2)}, u32[]{:S(2)}) collective-permute-start(bf16[96,1536]{1,0:T(8,128)(2,1)S(1)} %collective-permute-done.2.refs_3_), channel_id=1, source_target_pairs={{64,0},{128,64},{192,128},{256,192},{320,256},{384,320},{448,384},... | collective-permute-start | bytes 884744 | tf_op jit(solution)/shard_map/ppermute | solution.py:21
  74.1 14.3 %collective-permute-start.8 = (bf16[96,1536]{1,0:T(8,128)(2,1)S(1)}, bf16[96,1536]{1,0:T(8,128)(2,1)}, u32[]{:S(2)}, u32[]{:S(2)}) collective-permute-start(bf16[96,1536]{1,0:T(8,128)(2,1)S(1)} %collective-permute-done.3.refs_4_), channel_id=1, source_target_pairs={{448,0},{0,64},{64,128},{128,192},{192,256},{256,320},{320,384},{3... | collective-permute-start | bytes 884744 | tf_op jit(solution)/shard_map/ppermute | solution.py:21
  92.1 33.3 %all-to-all-start.2 = ((bf16[16,96,256]{2,1,0:T(8,128)(2,1)}), bf16[16,96,256]{2,1,0:T(8,128)(2,1)S(1)}, u32[]{:S(2)}, u32[]{:S(2)}) async-start(bf16[16,96,256]{2,1,0:T(8,128)(2,1)} %bitcast.15), calls=%async_computation.2 | async-start | bytes 1572864 | tf_op jit(solution)/shard_map/all_to_all | solution.py:113
  103.3 25.0 %copy-start.4 = (f32[1,1,12,1024]{3,1,2,0:T(1,128)S(1)}, f32[1,1,12,1024]{3,1,2,0:T(1,128)}, u32[]{:S(2)}) copy-start(f32[1,1,12,1024]{3,1,2,0:T(1,128)} %param.13) | copy-start | bytes 147460
  125.5 12.1 %copy-start.5 = (bf16[256,96]{0,1:T(8,128)(2,1)S(1)}, bf16[256,96]{0,1:T(8,128)(2,1)}, u32[]{:S(2)}) copy-start(bf16[256,96]{0,1:T(8,128)(2,1)} %param.10) | copy-start | bytes 147460
  125.5 12.1 %collective-permute-start.11 = (bf16[96,256]{1,0:T(8,128)(2,1)S(1)}, bf16[96,256]{1,0:T(8,128)(2,1)S(1)}, u32[]{:S(2)}, u32[]{:S(2)}) collective-permute-start(bf16[96,256]{1,0:T(8,128)(2,1)S(1)} %reduce_sum.21), channel_id=1, source_target_pairs={{0,0},{2,4},{4,28},{6,8},{8,2},{10,6},{12,30},{14,10},{16,24},{18,... | collective-permute-start | bytes 147464 | tf_op jit(solution)/shard_map/ppermute | solution.py:115

commit v10 on v6

--- a/solution.py
+++ b/solution.py
@@ -65,7 +65,7 @@
         out_shape=jax.ShapeDtypeStruct((2, done + rows, tokens), jnp.bfloat16),
         in_specs=[pl.BlockSpec(memory_space=pltpu.VMEM)] * len(operands),
         out_specs=pl.BlockSpec(memory_space=pltpu.VMEM),
-        compiler_params=pltpu.CompilerParams(vmem_limit_bytes=32 * 1024 * 1024),
+        compiler_params=pltpu.CompilerParams(vmem_limit_bytes=12 * 1024 * 1024),
         cost_estimate=pl.CostEstimate(
             flops=4 * rows * tokens * sources * hidden, bytes_accessed=6000000, transcendentals=0
         ),

time: 140 us -> 140 us (level)
  no operation moved by 1% of the time
where the time goes in v10:
time: 140 us; the launch traced here: 138 us
  starting transfers between devices  69.4 us (50%)
  waiting for transfers between devices  42 us (30%)
  blocking collectives  15.4 us (11%)
  Pallas kernels  4 us (3%)
  local copies, waits for them, and re-layouts  3.78 us (3%)
  other arithmetic  2.79 us (2%)
    ppermute x8, starting transfers between devices, from_z(): return lax.ppermute(value, 'z', [((i + step) % 8, i) for i in range(8)])  39.3 us
    all_to_all x1, waiting for transfers between devices, on_device(): lax.all_to_all(blocks, ('x_hi', 'x_mid', 'y_lo'), 0, 0, tiled=True)  21 us
    all_to_all x1, starting transfers between devices, on_device(): lax.all_to_all(blocks, ('x_hi', 'x_mid', 'y_lo'), 0, 0, tiled=True)  10.7 us
    ppermute x8, waiting for transfers between devices, from_z(): return lax.ppermute(value, 'z', [((i + step) % 8, i) for i in range(8)])  9.84 us
    ppermute x1, waiting for transfers between devices, on_device(): home = lax.ppermute(shared, WHERE, last_hop())  9.34 us
    all_to_all x1, starting transfers between devices, on_device(): kept = lax.all_to_all(ordered, ('y_hi', 'z'), 0, 0, tiled=True)  8.91 us
    all_gather x1, blocking collectives, on_device(): far = lax.all_gather(far_grad, QUAD, axis=0)  7.95 us
    all_gather x1, blocking collectives, on_device(): own = lax.all_gather(hidden_grad, QUAD, axis=0)  7.47 us
  transfers between devices with their start and end apart: 13, of which 5 were waited for; matrix products, arithmetic and copies ran while one was open for 3% of the time, Pallas kernels for 1%

profile of v10, /device:TPU:112, one launch (start us, length us, event | category | flops | bytes accessed | tf_op | source)
XLA Modules:
  0.0 138.3 jit_solution(10434410977566921868)
XLA Ops:
  0.7 3.6 %all-to-all-start = ((bf16[4,96,384]{2,1,0:T(8,128)(2,1)}), bf16[4,96,384]{2,1,0:T(8,128)(2,1)S(1)}, u32[]{:S(2)}, u32[]{:S(2)}) async-start(bf16[4,96,384]{2,1,0:T(8,128)(2,1)} %bitcast.30), calls=%async_computation | async-start | bytes 589824 | tf_op jit(solution)/shard_map/all_to_all | solution.py:82
  4.3 0.2 fusion.7
  4.5 4.3 %collective-permute-start.4 = (bf16[256,384]{1,0:T(8,128)(2,1)S(1)}, bf16[256,384]{1,0:T(8,128)(2,1)}, u32[]{:S(2)}, u32[]{:S(2)}) collective-permute-start(bf16[256,384]{1,0:T(8,128)(2,1)S(1)} %fusion.7), channel_id=1, source_target_pairs={{0,512},{512,0},{1,513},{513,1},{2,514},{514,2},{3,515},{515,3},{4... | collective-permute-start | bytes 589832 | tf_op jit(solution)/shard_map/ppermute | solution.py:80
  8.8 1.8 %all-to-all-done = bf16[4,96,384]{2,1,0:T(8,128)(2,1)S(1)} async-done(((bf16[4,96,384]{2,1,0:T(8,128)(2,1)}), bf16[4,96,384]{2,1,0:T(8,128)(2,1)S(1)}, u32[]{:S(2)}, u32[]{:S(2)}) %all-to-all-start) | async-done | bytes 294944 | tf_op jit(solution)/shard_map/all_to_all | solution.py:82
  10.7 17.4 %collective-permute-start = (bf16[96,1536]{1,0:T(8,128)(2,1)S(1)}, bf16[96,1536]{1,0:T(8,128)(2,1)S(1)}, u32[]{:S(2)}, u32[]{:S(2)}) collective-permute-start(bf16[96,1536]{1,0:T(8,128)(2,1)S(1)} %pad_maximum_fusion.refs_2_), channel_id=1, source_target_pairs={{64,0},{128,64},{192,128},{256,192},{320,256},{384,320},{448,384},... | collective-permute-start | bytes 884744 | tf_op jit(solution)/shard_map/ppermute | solution.py:21
  28.1 1.9 %collective-permute-start.1 = (bf16[96,1536]{1,0:T(8,128)(2,1)S(1)}, bf16[96,1536]{1,0:T(8,128)(2,1)S(1)}, u32[]{:S(2)}, u32[]{:S(2)}) collective-permute-start(bf16[96,1536]{1,0:T(8,128)(2,1)S(1)} %pad_maximum_fusion.refs_2_), channel_id=1, source_target_pairs={{448,0},{0,64},{64,128},{128,192},{192,256},{256,320},{320,384},{3... | collective-permute-start | bytes 884744 | tf_op jit(solution)/shard_map/ppermute | solution.py:21
  30.1 3.4 %collective-permute-start.2 = (bf16[96,1536]{1,0:T(8,128)(2,1)S(1)}, bf16[96,1536]{1,0:T(8,128)(2,1)S(1)}, u32[]{:S(2)}, u32[]{:S(2)}) collective-permute-start(bf16[96,1536]{1,0:T(8,128)(2,1)S(1)} %pad_maximum_fusion.refs_2_), channel_id=1, source_target_pairs={{128,0},{192,64},{256,128},{320,192},{384,256},{448,320},{0,384},{... | collective-permute-start | bytes 884744 | tf_op jit(solution)/shard_map/ppermute | solution.py:21
  33.4 3.4 %collective-permute-start.3 = (bf16[96,1536]{1,0:T(8,128)(2,1)S(1)}, bf16[96,1536]{1,0:T(8,128)(2,1)S(1)}, u32[]{:S(2)}, u32[]{:S(2)}) collective-permute-start(bf16[96,1536]{1,0:T(8,128)(2,1)S(1)} %pad_maximum_fusion.refs_2_), channel_id=1, source_target_pairs={{384,0},{448,64},{0,128},{64,192},{128,256},{192,320},{256,384},{3... | collective-permute-start | bytes 884744 | tf_op jit(solution)/shard_map/ppermute | solution.py:21
  36.8 7.5 %all-gather = bf16[1024,384]{1,0:T(8,128)(2,1)S(1)} all-gather(bf16[256,384]{1,0:T(8,128)(2,1)S(1)} %fusion.7), channel_id=2, replica_groups=mesh['y_hi'=2,'z'=8,'x_hi'=2,'x_mid'=2,'x_lo'=2,'y_lo'=4,'core'=2] {'x_l..., dimensions={0}, use_global_device_ids=true | all-gather | bytes 983040 | tf_op jit(solution)/shard_map/all_gather | solution.py:88
  44.3 0.1 reshape.45
  44.4 1.4 %gather_fusion = bf16[16,12,1024]{2,1,0:T(8,128)(2,1)} fusion(bf16[16,12,1024]{2,1,0:T(8,128)(2,1)S(1)} %reshape.45, s32[1024]{0:T(1024)S(1)} %pad_clamp_fusion), kind=kCustom, calls=%fused_computation | custom fusion | bytes 786496 | tf_op jit(solution)/shard_map/gather | solution.py:91
  45.8 6.1 %collective-permute-done.3.refs_6_ = bf16[96,1536]{1,0:T(8,128)(2,1)S(1)} collective-permute-done((bf16[96,1536]{1,0:T(8,128)(2,1)S(1)}, bf16[96,1536]{1,0:T(8,128)(2,1)S(1)}, u32[]{:S(2)}, u32[]{:S(2)}) %collective-permute-start.3) | collective-permute-done | bytes 294944 | tf_op jit(solution)/shard_map/ppermute | solution.py:21
  51.9 8.9 %all-to-all-start.1 = ((bf16[16,12,1024]{2,1,0:T(8,128)(2,1)}), bf16[16,12,1024]{2,1,0:T(8,128)(2,1)}, u32[]{:S(2)}, u32[]{:S(2)}) async-start(bf16[16,12,1024]{2,1,0:T(8,128)(2,1)} %gather_fusion), calls=%async_computation.1 | async-start | bytes 1048576 | tf_op jit(solution)/shard_map/all_to_all | solution.py:102
  60.8 4.6 %collective-permute-start.5 = (bf16[96,1536]{1,0:T(8,128)(2,1)S(1)}, bf16[96,1536]{1,0:T(8,128)(2,1)}, u32[]{:S(2)}, u32[]{:S(2)}) collective-permute-start(bf16[96,1536]{1,0:T(8,128)(2,1)S(1)} %collective-permute-done.2.refs_5_), channel_id=1, source_target_pairs={{64,0},{128,64},{192,128},{256,192},{320,256},{384,320},{448,384},... | collective-permute-start | bytes 884744 | tf_op jit(solution)/shard_map/ppermute | solution.py:21
  65.4 1.9 %collective-permute-start.6 = (bf16[96,1536]{1,0:T(8,128)(2,1)S(1)}, bf16[96,1536]{1,0:T(8,128)(2,1)}, u32[]{:S(2)}, u32[]{:S(2)}) collective-permute-start(bf16[96,1536]{1,0:T(8,128)(2,1)S(1)} %collective-permute-done.3.refs_6_), channel_id=1, source_target_pairs={{448,0},{0,64},{64,128},{128,192},{192,256},{256,320},{320,384},{3... | collective-permute-start | bytes 884744 | tf_op jit(solution)/shard_map/ppermute | solution.py:21
  67.4 0.7 slice.23
  68.0 4.8 %collective-permute-start.7 = (bf16[48,1536]{1,0:T(8,128)(2,1)S(1)}, bf16[48,1536]{1,0:T(8,128)(2,1)S(1)}, u32[]{:S(2)}, u32[]{:S(2)}) collective-permute-start(bf16[48,1536]{1,0:T(8,128)(2,1)S(1)} %slice.22), channel_id=1, source_target_pairs={{128,0},{192,64},{256,128},{320,192},{384,256},{448,320},{0,384},{... | collective-permute-start | bytes 442376 | tf_op jit(solution)/shard_map/ppermute | solution.py:21
  72.8 1.9 %collective-permute-start.8 = (bf16[48,1536]{1,0:T(8,128)(2,1)}, bf16[48,1536]{1,0:T(8,128)(2,1)}, u32[]{:S(2)}, u32[]{:S(2)}) collective-permute-start(bf16[48,1536]{1,0:T(8,128)(2,1)} %slice.23), channel_id=1, source_target_pairs={{384,0},{448,64},{0,128},{64,192},{128,256},{192,320},{256,384},{3... | collective-permute-start | bytes 442376 | tf_op jit(solution)/shard_map/ppermute | solution.py:21
  74.8 7.9 %all-gather.1 = bf16[1024,384]{1,0:T(8,128)(2,1)S(1)} all-gather(bf16[256,384]{1,0:T(8,128)(2,1)} %collective-permute-done.4), channel_id=3, replica_groups=mesh['y_hi'=2,'z'=8,'x_hi'=2,'x_mid'=2,'x_lo'=2,'y_lo'=4,'core'=2] {'x_l..., dimensions={0}, use_global_device_ids=true | all-gather | bytes 983040 | tf_op jit(solution)/shard_map/all_gather | solution.py:101
  82.7 1.2 shard_map.86.refs_6_
  83.9 3.7 %collective-permute-done.7.refs_4_ = bf16[48,1536]{1,0:T(8,128)(2,1)S(1)} collective-permute-done((bf16[48,1536]{1,0:T(8,128)(2,1)S(1)}, bf16[48,1536]{1,0:T(8,128)(2,1)S(1)}, u32[]{:S(2)}, u32[]{:S(2)}) %collective-permute-start.7) | collective-permute-done | bytes 147488 | tf_op jit(solution)/shard_map/ppermute | solution.py:21
  87.6 0.7 copy-done
  88.3 0.9 copy-done.1
  89.2 2.8 %shard_map.87 = bf16[2,768,256]{2,1,0:T(8,128)(2,1)} custom-call(bf16[4,256,384]{2,1,0:T(8,128)(2,1)S(1)} %bitcast.26, bf16[4,256,384]{2,1,0:T(8,128)(2,1)S(1)} %bitcast.28, bf16[96,1536]{1,0:T(8,128)(2,1)} %collective-permute-done.5.refs_2_, bf16[96,1536]{1,0:T(8,128)(2,1)} %collective-permute-done.6.refs_3_, bf16[48,1536]{1,0:T(8,128)(2,1)S(1)} %copy-done.1, ...), custom_call_target="tpu_custom_call" | custom-call | flops 452984832 | bytes 6000000 | tf_op jit(solution)/shard_map/pallas_call | solution.py:63
  92.0 10.7 %all-to-all-start.2 = ((bf16[16,96,256]{2,1,0:T(8,128)(2,1)}), bf16[16,96,256]{2,1,0:T(8,128)(2,1)S(1)}, u32[]{:S(2)}, u32[]{:S(2)}) async-start(bf16[16,96,256]{2,1,0:T(8,128)(2,1)} %bitcast.10), calls=%async_computation.2 | async-start | bytes 1572864 | tf_op jit(solution)/shard_map/all_to_all | solution.py:109
  102.7 1.1 convert_reduce_fusion
  103.9 21.0 %all-to-all-done.2 = bf16[16,96,256]{2,1,0:T(8,128)(2,1)S(1)} async-done(((bf16[16,96,256]{2,1,0:T(8,128)(2,1)}), bf16[16,96,256]{2,1,0:T(8,128)(2,1)S(1)}, u32[]{:S(2)}, u32[]{:S(2)}) %all-to-all-start.2) | async-done | bytes 786464 | tf_op jit(solution)/shard_map/all_to_all | solution.py:109
  124.9 0.1 reduce_sum.21
  125.0 2.6 %collective-permute-start.9 = (bf16[96,256]{1,0:T(8,128)(2,1)S(1)}, bf16[96,256]{1,0:T(8,128)(2,1)S(1)}, u32[]{:S(2)}, u32[]{:S(2)}) collective-permute-start(bf16[96,256]{1,0:T(8,128)(2,1)S(1)} %reduce_sum.21), channel_id=1, source_target_pairs={{0,0},{2,4},{4,28},{6,8},{8,2},{10,6},{12,30},{14,10},{16,24},{18,... | collective-permute-start | bytes 147464 | tf_op jit(solution)/shard_map/ppermute | solution.py:111
  127.7 0.7 reshape_add_fusion
  128.3 9.3 %collective-permute-done.9 = bf16[96,256]{1,0:T(8,128)(2,1)S(1)} collective-permute-done((bf16[96,256]{1,0:T(8,128)(2,1)S(1)}, bf16[96,256]{1,0:T(8,128)(2,1)S(1)}, u32[]{:S(2)}, u32[]{:S(2)}) %collective-permute-start.9) | collective-permute-done | bytes 49184 | tf_op jit(solution)/shard_map/ppermute | solution.py:111
  137.7 0.6 fusion.9
  (27 shorter events, 0.1 us)
Async XLA Ops:
  0.6 3.6 %copy-start.3 = (bf16[256,384]{1,0:T(8,128)(2,1)S(1)}, bf16[256,384]{1,0:T(8,128)(2,1)}, u32[]{:S(2)}) copy-start(bf16[256,384]{1,0:T(8,128)(2,1)} %param.7) | copy-start | bytes 589828
  0.6 3.6 %copy-start.4 = (bf16[256,384]{1,0:T(8,128)(2,1)S(1)}, bf16[256,384]{1,0:T(8,128)(2,1)}, u32[]{:S(2)}) copy-start(bf16[256,384]{1,0:T(8,128)(2,1)} %param.8) | copy-start | bytes 589828
  0.7 10.0 %all-to-all-start = ((bf16[4,96,384]{2,1,0:T(8,128)(2,1)}), bf16[4,96,384]{2,1,0:T(8,128)(2,1)S(1)}, u32[]{:S(2)}, u32[]{:S(2)}) async-start(bf16[4,96,384]{2,1,0:T(8,128)(2,1)} %bitcast.30), calls=%async_computation | async-start | bytes 589824 | tf_op jit(solution)/shard_map/all_to_all | solution.py:82
  4.3 4.5 %copy-start.7 = (s32[1,16]{1,0:T(1,128)S(1)}, s32[1,16]{1,0:T(1,128)}, u32[]{:S(2)}) copy-start(s32[1,16]{1,0:T(1,128)} %param.12) | copy-start | bytes 196
  4.5 41.3 %collective-permute-start.4 = (bf16[256,384]{1,0:T(8,128)(2,1)S(1)}, bf16[256,384]{1,0:T(8,128)(2,1)}, u32[]{:S(2)}, u32[]{:S(2)}) collective-permute-start(bf16[256,384]{1,0:T(8,128)(2,1)S(1)} %fusion.7), channel_id=1, source_target_pairs={{0,512},{512,0},{1,513},{513,1},{2,514},{514,2},{3,515},{515,3},{4... | collective-permute-start | bytes 589832 | tf_op jit(solution)/shard_map/ppermute | solution.py:80
  10.7 33.6 %copy-start.2 = (bf16[1,192,1024]{2,1,0:T(8,128)(2,1)S(1)}, bf16[1,192,1024]{2,1,0:T(8,128)(2,1)}, u32[]{:S(2)}) copy-start(bf16[1,192,1024]{2,1,0:T(8,128)(2,1)} %param.11) | copy-start | bytes 1179652
  10.7 35.1 %collective-permute-start = (bf16[96,1536]{1,0:T(8,128)(2,1)S(1)}, bf16[96,1536]{1,0:T(8,128)(2,1)S(1)}, u32[]{:S(2)}, u32[]{:S(2)}) collective-permute-start(bf16[96,1536]{1,0:T(8,128)(2,1)S(1)} %pad_maximum_fusion.refs_2_), channel_id=1, source_target_pairs={{64,0},{128,64},{192,128},{256,192},{320,256},{384,320},{448,384},... | collective-permute-start | bytes 884744 | tf_op jit(solution)/shard_map/ppermute | solution.py:21
  28.1 17.6 %collective-permute-start.1 = (bf16[96,1536]{1,0:T(8,128)(2,1)S(1)}, bf16[96,1536]{1,0:T(8,128)(2,1)S(1)}, u32[]{:S(2)}, u32[]{:S(2)}) collective-permute-start(bf16[96,1536]{1,0:T(8,128)(2,1)S(1)} %pad_maximum_fusion.refs_2_), channel_id=1, source_target_pairs={{448,0},{0,64},{64,128},{128,192},{192,256},{256,320},{320,384},{3... | collective-permute-start | bytes 884744 | tf_op jit(solution)/shard_map/ppermute | solution.py:21
  30.1 15.7 %collective-permute-start.2 = (bf16[96,1536]{1,0:T(8,128)(2,1)S(1)}, bf16[96,1536]{1,0:T(8,128)(2,1)S(1)}, u32[]{:S(2)}, u32[]{:S(2)}) collective-permute-start(bf16[96,1536]{1,0:T(8,128)(2,1)S(1)} %pad_maximum_fusion.refs_2_), channel_id=1, source_target_pairs={{128,0},{192,64},{256,128},{320,192},{384,256},{448,320},{0,384},{... | collective-permute-start | bytes 884744 | tf_op jit(solution)/shard_map/ppermute | solution.py:21
  33.4 18.5 %collective-permute-start.3 = (bf16[96,1536]{1,0:T(8,128)(2,1)S(1)}, bf16[96,1536]{1,0:T(8,128)(2,1)S(1)}, u32[]{:S(2)}, u32[]{:S(2)}) collective-permute-start(bf16[96,1536]{1,0:T(8,128)(2,1)S(1)} %pad_maximum_fusion.refs_2_), channel_id=1, source_target_pairs={{384,0},{448,64},{0,128},{64,192},{128,256},{192,320},{256,384},{3... | collective-permute-start | bytes 884744 | tf_op jit(solution)/shard_map/ppermute | solution.py:21
  51.9 36.4 %all-to-all-start.1 = ((bf16[16,12,1024]{2,1,0:T(8,128)(2,1)}), bf16[16,12,1024]{2,1,0:T(8,128)(2,1)}, u32[]{:S(2)}, u32[]{:S(2)}) async-start(bf16[16,12,1024]{2,1,0:T(8,128)(2,1)} %gather_fusion), calls=%async_computation.1 | async-start | bytes 1048576 | tf_op jit(solution)/shard_map/all_to_all | solution.py:102
  60.8 27.5 %collective-permute-start.5 = (bf16[96,1536]{1,0:T(8,128)(2,1)S(1)}, bf16[96,1536]{1,0:T(8,128)(2,1)}, u32[]{:S(2)}, u32[]{:S(2)}) collective-permute-start(bf16[96,1536]{1,0:T(8,128)(2,1)S(1)} %collective-permute-done.2.refs_5_), channel_id=1, source_target_pairs={{64,0},{128,64},{192,128},{256,192},{320,256},{384,320},{448,384},... | collective-permute-start | bytes 884744 | tf_op jit(solution)/shard_map/ppermute | solution.py:21
  65.4 22.9 %collective-permute-start.6 = (bf16[96,1536]{1,0:T(8,128)(2,1)S(1)}, bf16[96,1536]{1,0:T(8,128)(2,1)}, u32[]{:S(2)}, u32[]{:S(2)}) collective-permute-start(bf16[96,1536]{1,0:T(8,128)(2,1)S(1)} %collective-permute-done.3.refs_6_), channel_id=1, source_target_pairs={{448,0},{0,64},{64,128},{128,192},{192,256},{256,320},{320,384},{3... | collective-permute-start | bytes 884744 | tf_op jit(solution)/shard_map/ppermute | solution.py:21
  68.0 19.6 %collective-permute-start.7 = (bf16[48,1536]{1,0:T(8,128)(2,1)S(1)}, bf16[48,1536]{1,0:T(8,128)(2,1)S(1)}, u32[]{:S(2)}, u32[]{:S(2)}) collective-permute-start(bf16[48,1536]{1,0:T(8,128)(2,1)S(1)} %slice.22), channel_id=1, source_target_pairs={{128,0},{192,64},{256,128},{320,192},{384,256},{448,320},{0,384},{... | collective-permute-start | bytes 442376 | tf_op jit(solution)/shard_map/ppermute | solution.py:21
  72.8 15.5 %collective-permute-start.8 = (bf16[48,1536]{1,0:T(8,128)(2,1)}, bf16[48,1536]{1,0:T(8,128)(2,1)}, u32[]{:S(2)}, u32[]{:S(2)}) collective-permute-start(bf16[48,1536]{1,0:T(8,128)(2,1)} %slice.23), channel_id=1, source_target_pairs={{384,0},{448,64},{0,128},{64,192},{128,256},{192,320},{256,384},{3... | collective-permute-start | bytes 442376 | tf_op jit(solution)/shard_map/ppermute | solution.py:21
  87.6 0.7 copy-start
  88.3 0.9 copy-start.1
  92.0 32.8 %all-to-all-start.2 = ((bf16[16,96,256]{2,1,0:T(8,128)(2,1)}), bf16[16,96,256]{2,1,0:T(8,128)(2,1)S(1)}, u32[]{:S(2)}, u32[]{:S(2)}) async-start(bf16[16,96,256]{2,1,0:T(8,128)(2,1)} %bitcast.10), calls=%async_computation.2 | async-start | bytes 1572864 | tf_op jit(solution)/shard_map/all_to_all | solution.py:109
  103.8 23.8 %copy-start.5 = (f32[1,1,12,1024]{3,1,2,0:T(1,128)S(1)}, f32[1,1,12,1024]{3,1,2,0:T(1,128)}, u32[]{:S(2)}) copy-start(f32[1,1,12,1024]{3,1,2,0:T(1,128)} %param.13) | copy-start | bytes 147460
  125.0 12.7 %copy-start.6 = (bf16[256,96]{0,1:T(8,128)(2,1)S(1)}, bf16[256,96]{0,1:T(8,128)(2,1)}, u32[]{:S(2)}) copy-start(bf16[256,96]{0,1:T(8,128)(2,1)} %param.10) | copy-start | bytes 147460
  125.0 12.7 %collective-permute-start.9 = (bf16[96,256]{1,0:T(8,128)(2,1)S(1)}, bf16[96,256]{1,0:T(8,128)(2,1)S(1)}, u32[]{:S(2)}, u32[]{:S(2)}) collective-permute-start(bf16[96,256]{1,0:T(8,128)(2,1)S(1)} %reduce_sum.21), channel_id=1, source_target_pairs={{0,0},{2,4},{4,28},{6,8},{8,2},{10,6},{12,30},{14,10},{16,24},{18,... | collective-permute-start | bytes 147464 | tf_op jit(solution)/shard_map/ppermute | solution.py:111
